TPU v7x, 256 devices: a whole 4x4x8 slice. The times are simulated.
256 devices in a mesh: emb: 128 (over y, x, z), nn: 2 (over core).
Axes of the slice: x: 4, y: 4, z: 8, core: 2. Of those that a mesh axis runs over, the one named last changes fastest.
Arguments:
- dense_input: bfloat16 [2, 32768, 128], P(None, ('emb', 'nn')), may hold values from -6 to 6
- id_owner: int32 [2, 393216, 1], P(None, ('emb', 'nn')), may hold values from 0 to 127; in each aligned block of 1536 rows (0 to 1535, 1536 to 3071, ..., all dimensions but the last counted through in order) at most 24 rows name the same one
- id_row: int32 [2, 256, 1536], P(None, ('emb', 'nn')), may hold values from 0 to 1023
- id_mask: int32 [2, 256, 1536], P(None, ('emb', 'nn')), may hold values 0 or 1
- bag_index: int32 [2, 256, 1536], P(None, ('emb', 'nn')), may hold values from 0 to 511, never falling along the last dimension, each value on 1 to 8 neighbouring positions
- labels: int32 [2, 32768], P(None, ('emb', 'nn')), may hold values from 0 to 1
- stale_owner: int32 [2, 393216, 1], P(None, ('emb', 'nn')), may hold values from 0 to 127; in each aligned block of 1536 rows (0 to 1535, 1536 to 3071, ..., all dimensions but the last counted through in order) at most 24 rows name the same one
- stale_row: int32 [2, 256, 1536], P(None, ('emb', 'nn')), may hold values from 0 to 1023
- stale_grad: bfloat16 [2, 256, 1536, 128], P(None, ('emb', 'nn')), may hold values from -6 to 6
- emb_table: float32 [131072, 128], P('emb'), may hold values from -3 to 3
- grad_squares: float32 [131072, 128], P('emb'), may hold values from 0.1 to 1
- bottom_first: bfloat16 [128, 512], replicated, may hold values from -0.5 to 0.5
- bottom_bias: float32 [512], replicated, may hold values from -3 to 3
- bottom_second: bfloat16 [512, 128], replicated, may hold values from -0.25 to 0.25
- top_weight: bfloat16 [640, 4096], replicated, may hold values from -0.25 to 0.25
- top_bias: float32 [4096], replicated, may hold values from -3 to 3
- out_weight: bfloat16 [4096], replicated, may hold values from -0.09375 to 0.09375
- top_squares: float32 [640, 4096], P('nn', 'emb'), may hold values from 1000 to 30000
Outputs:
- row_grads: bfloat16 [2, 256, 1536, 128], P(None, ('emb', 'nn'))
- new_table: float32 [131072, 128], P('emb')
- new_squares: float32 [131072, 128], P('emb')
- top_step: float32 [640, 4096], P('nn', 'emb')
Inputs may be any that keep to these rules, and one draw needn't show every extreme that they name: `id_owner`: in each aligned block of 1536 rows (one list of one micro-batch) no owner is named more than 24 times, a bound that some block reaches. `bag_index`: along each list, bag numbers never fall and each of the 512 bags holds 1 to 8 slots, some bag exactly 8. `stale_owner`: in each aligned block of 1536 rows no owner is named more than 24 times, a bound that some block reaches.
All inputs are finite; a program needn't handle non-finite values. No bound on the sum of `id_mask` on one device may be relied on, other than what follows from the above.
Results may differ from a plain program's by a relative error of at most 0.0055.
Values may be sent and summed in bfloat16 or wider, within the bound.
No kernel may reach another device: no remote copies, remote signals or barrier semaphores. Data moves between devices by JAX's collectives and lax.ppermute only.
A program may use at most 128 MiB of HBM per device.

v0:
```python
import jax
import jax.numpy as jnp
from jax import lax
from jax.sharding import PartitionSpec as P

FEATS = 4


LEARN_RATE = 0.1
LOSS_SCALE = 64.0


def rank_slots(owner_list, per_peer, peer_count):
    length = owner_list.shape[0]
    owners_all = jnp.arange(peer_count, dtype=jnp.int32)
    onehot = (owner_list[:, None] == owners_all[None, :]).astype(jnp.float32)
    blocks = onehot.reshape(length // 64, 64, peer_count)
    lower_ones = (jnp.arange(64)[:, None] >= jnp.arange(64)[None, :]).astype(jnp.float32)
    within = jnp.einsum("ij,bjp->bip", lower_ones, blocks, precision=lax.Precision.HIGHEST)
    totals = jnp.sum(blocks, axis=1)
    earlier = jnp.cumsum(totals, axis=0) - totals
    counted = within + earlier[:, None, :]
    position = jnp.sum(counted * blocks, axis=2).reshape(length) - 1.0
    return owner_list * per_peer + position.astype(jnp.int32)


def pack_index(values, slot_list, buffer_size):
    return jnp.full((buffer_size,), -1, jnp.int32).at[slot_list].set(values)


def dense_pass(
    dense_rows,
    label_rows,
    pooled,
    bottom_first,
    bottom_bias,
    bottom_second,
    top_weight,
    top_bias,
    out_weight,
):
    hidden = jax.nn.relu(
        jnp.dot(dense_rows, bottom_first, preferred_element_type=jnp.float32) + bottom_bias
    ).astype(jnp.bfloat16)
    bottom = jax.nn.relu(jnp.dot(hidden, bottom_second, preferred_element_type=jnp.float32))
    joined = jnp.concatenate([bottom, pooled], axis=1).astype(jnp.bfloat16)
    before = jnp.dot(joined, top_weight, preferred_element_type=jnp.float32) + top_bias
    gate_value = jax.nn.sigmoid(before)
    active = (before * gate_value).astype(jnp.bfloat16)
    logits = jnp.dot(active, out_weight, preferred_element_type=jnp.float32)
    logit_grad = LOSS_SCALE * (jax.nn.sigmoid(logits) - label_rows.astype(jnp.float32))
    top_delta = (
        logit_grad[:, None]
        * out_weight.astype(jnp.float32)[None, :]
        * gate_value
        * (1.0 + before * (1.0 - gate_value))
    ).astype(jnp.bfloat16)
    split_at = bottom.shape[1]
    back_grad = lax.dot_general(
        top_delta,
        top_weight[split_at:],
        (((1,), (1,)), ((), ())),
        preferred_element_type=jnp.float32,
    )
    return (joined, top_delta, back_grad)


def per_device(
    dense_input,
    id_owner,
    id_row,
    id_mask,
    bag_index,
    labels,
    stale_owner,
    stale_row,
    stale_grad,
    emb_table,
    grad_squares,
    bottom_first,
    bottom_bias,
    bottom_second,
    top_weight,
    top_bias,
    out_weight,
    top_squares,
):
    peer_count = lax.axis_size("emb")
    micro_count = id_row.shape[0]
    length = id_row.shape[2]
    row_width = emb_table.shape[1]
    table_rows = emb_table.shape[0]
    per_peer = 2 * length // peer_count
    buffer_size = peer_count * per_peer
    samples = dense_input.shape[1]
    bag_count = samples * FEATS
    owners = id_owner.reshape(micro_count, length)
    old_owners = stale_owner.reshape(micro_count, length)
    wanted_rows = id_row.reshape(micro_count, length)
    old_rows = stale_row.reshape(micro_count, length)
    live_mask = id_mask.reshape(micro_count, length).astype(jnp.float32)
    bag_ids = bag_index.reshape(micro_count, length)
    slot_lists = [
        rank_slots(owners[micro_index], per_peer, peer_count) for micro_index in range(micro_count)
    ]
    old_slots = [
        rank_slots(old_owners[micro_index], per_peer, peer_count)
        for micro_index in range(micro_count)
    ]
    requests = jnp.stack(
        [
            pack_index(wanted_rows[micro_index], slot_lists[micro_index], buffer_size)
            for micro_index in range(micro_count)
        ]
    ).reshape(micro_count, peer_count, per_peer)
    old_requests = jnp.stack(
        [
            pack_index(old_rows[micro_index], old_slots[micro_index], buffer_size)
            for micro_index in range(micro_count)
        ]
    ).reshape(micro_count, peer_count, per_peer)
    asked_rows = [
        lax.all_to_all(requests[micro_index], "emb", split_axis=0, concat_axis=0, tiled=True)
        for micro_index in range(micro_count)
    ]
    old_asked = lax.all_to_all(old_requests, "emb", split_axis=1, concat_axis=1, tiled=True)
    pooled_parts = []
    for micro_index in range(micro_count):
        lookup = jnp.maximum(asked_rows[micro_index].reshape(buffer_size), 0)
        fetched = (
            jnp.take(emb_table, lookup, axis=0)
            .astype(jnp.bfloat16)
            .reshape(peer_count, per_peer, row_width)
        )
        replies = lax.all_to_all(fetched, "emb", split_axis=0, concat_axis=0, tiled=True).reshape(
            buffer_size, row_width
        )
        picked = (
            jnp.take(replies, slot_lists[micro_index], axis=0).astype(jnp.float32)
            * live_mask[micro_index][:, None]
        )
        bag_sums = jax.ops.segment_sum(
            picked, bag_ids[micro_index], num_segments=bag_count, indices_are_sorted=True
        )
        pooled_parts.append(bag_sums.reshape(samples, FEATS * row_width))
    pooled = jnp.concatenate(pooled_parts, axis=0)
    outgoing = jnp.stack(
        [
            jnp.zeros((buffer_size, row_width), jnp.bfloat16)
            .at[old_slots[micro_index]]
            .set(stale_grad[micro_index, 0])
            for micro_index in range(micro_count)
        ]
    ).reshape(micro_count, peer_count, per_peer, row_width)
    incoming = lax.all_to_all(outgoing, "emb", split_axis=1, concat_axis=1, tiled=True)
    targets = jnp.maximum(old_asked.reshape(micro_count * buffer_size), 0)
    grad_terms = incoming.reshape(micro_count * buffer_size, row_width)
    shard_sum = (
        jnp.zeros((table_rows, row_width), jnp.float32)
        .at[targets]
        .add(grad_terms.astype(jnp.float32))
    )
    row_sum = lax.psum(shard_sum, "nn")
    dense_rows = dense_input.reshape(micro_count * samples, dense_input.shape[2])
    label_rows = labels.reshape(micro_count * samples)
    joined, top_delta, back_grad = dense_pass(
        dense_rows,
        label_rows,
        pooled,
        bottom_first,
        bottom_bias,
        bottom_second,
        top_weight,
        top_bias,
        out_weight,
    )
    bag_grad = back_grad.reshape(micro_count, bag_count, row_width)
    row_grads = jnp.stack(
        [
            (
                jnp.take(bag_grad[micro_index], bag_ids[micro_index], axis=0)
                * live_mask[micro_index][:, None]
            ).astype(jnp.bfloat16)
            for micro_index in range(micro_count)
        ]
    ).reshape(micro_count, 1, length, row_width)
    unit_part = lax.psum_scatter(
        lax.dot_general(
            top_delta, joined, (((0,), (0,)), ((), ())), preferred_element_type=jnp.float32
        ),
        "emb",
        scatter_dimension=0,
        tiled=True,
    )
    top_grad = lax.psum_scatter(unit_part, "nn", scatter_dimension=1, tiled=True).T
    top_step = top_grad * lax.rsqrt(top_squares + top_grad * top_grad)
    new_squares = grad_squares + row_sum * row_sum
    new_table = emb_table - LEARN_RATE * row_sum * lax.rsqrt(new_squares)
    return (row_grads, new_table, new_squares, top_step)


def solution(mesh):
    return jax.shard_map(
        per_device,
        mesh=mesh,
        in_specs=(
            P(None, ("emb", "nn"), None),
            P(None, ("emb", "nn"), None),
            P(None, ("emb", "nn"), None),
            P(None, ("emb", "nn"), None),
            P(None, ("emb", "nn"), None),
            P(None, ("emb", "nn")),
            P(None, ("emb", "nn"), None),
            P(None, ("emb", "nn"), None),
            P(None, ("emb", "nn"), None, None),
            P("emb", None),
            P("emb", None),
            P(),
            P(),
            P(),
            P(),
            P(),
            P(),
            P("nn", "emb"),
        ),
        out_specs=(
            P(None, ("emb", "nn"), None, None),
            P("emb", None),
            P("emb", None),
            P("nn", "emb"),
        ),
        check_vma=False,
    )
```

profile of v0, /device:TPU:8, one launch (start us, length us, event | category | flops | bytes accessed | tf_op | source)
XLA Modules:
  0.0 900.2 jit_solution(12111976959611152874)
XLA Ops:
  13.3 6.2 scatter_custom_fusion
  20.2 15.4 %all-to-all-start = ((s32[128,1,24]{2,1,0:T(1,128)}), s32[128,1,24]{2,1,0:T(1,128)S(1)}, u32[]{:S(2)}, u32[]{:S(2)}) async-start(s32[128,1,24]{2,1,0:T(1,128)} %bitcast.4), calls=%async_computation | async-start | bytes 131072 | tf_op jit(solution)/shard_map/all_to_all | solution.py:123
  35.7 6.2 scatter_custom_fusion.2
  41.9 4.5 all-to-all-done
  46.4 20.0 %all_to_all.38 = s32[128,1,24]{2,1,0:T(1,128)S(1)} all-to-all(s32[128,1,24]{2,1,0:T(1,128)S(1)} %bitcast.98), channel_id=1, replica_groups=mesh['emb'=128,'nn'=2] {'emb'}, dimensions={0} | all-to-all | bytes 24576 | tf_op jit(solution)/shard_map/all_to_all | solution.py:123
  67.0 8.3 gather_fusion
  75.3 2.3 select_convert_fusion.1
  77.6 7.3 all-to-all-start.1
  85.1 8.3 gather_fusion.1
  93.4 2.3 select_convert_fusion
  95.8 11.1 %all-to-all-done.1 = bf16[128,24,128]{2,1,0:T(8,128)(2,1)S(1)} async-done(((bf16[128,24,128]{2,1,0:T(8,128)(2,1)}), bf16[128,24,128]{2,1,0:T(8,128)(2,1)S(1)}, u32[]{:S(2)}, u32[]{:S(2)}) %all-to-all-start.1) | async-done | bytes 786464 | tf_op jit(solution)/shard_map/all_to_all | solution.py:135
  106.9 8.7 all-to-all-start.3
  116.6 14.7 %scatter_custom_fusion.1 = f32[512,128]{1,0:T(8,128)S(1)} fusion(s32[1536]{0:T(1024)S(1)} %get-tuple-element.47, f32[1536]{0:T(1024)S(1)} %get-tuple-element.45, pred[1536]{0:T(1024)(128)(4,1)S(1)} %get-tuple-element.51, bf16[]{:T(256)} %constant.30.clone.2, f32[]{:T(128)} %constant.42.clone.1, bf16[3072,128]{1,0:T(8,128)(2,1)S(1)} %bitcast.93, ...), kind=kCustom, calls=%fused_computation.63 | custom fusion | flops 786432 | bytes 1067014 | tf_op jit(solution)/shard_map/scatter-add | solution.py:142
  131.4 4.8 all-to-all-done.3
  136.1 14.9 %scatter_custom_fusion.3 = f32[512,128]{1,0:T(8,128)S(1)} fusion(s32[1536]{0:T(1024)S(1)} %get-tuple-element.48, f32[1536]{0:T(1024)S(1)} %get-tuple-element.46, pred[1536]{0:T(1024)(128)(4,1)S(1)} %get-tuple-element.53, bf16[]{:T(256)} %constant.30.clone.2, f32[]{:T(128)} %constant.42.clone.1, bf16[3072,128]{1,0:T(8,128)(2,1)S(1)} %bitcast.94, ...), kind=kCustom, calls=%fused_computation.58 | custom fusion | flops 786432 | bytes 1067014 | tf_op jit(solution)/shard_map/scatter-add | solution.py:142
  151.2 4.3 convolution_add_fusion
  157.5 6.9 fusion.55
  168.2 6.2 scatter_custom_fusion.4
  174.5 6.2 scatter_custom_fusion.5
  181.6 9.5 %all-to-all-start.4 = ((s32[2,128,24]{2,0,1:T(2,128)}), s32[2,128,24]{2,0,1:T(2,128)S(1)}, u32[]{:S(2)}, u32[]{:S(2)}) async-start(s32[2,128,24]{2,0,1:T(2,128)} %copy.53), calls=%async_computation.4 | async-start | bytes 262144 | tf_op jit(solution)/shard_map/all_to_all | solution.py:126
  191.1 4.7 scatter_custom_fusion.6
  195.8 4.7 scatter_custom_fusion.7
  202.4 13.2 %all-to-all-start.5 = ((bf16[2,128,24,128]{3,2,0,1:T(8,128)(2,1)}), bf16[2,128,24,128]{3,2,0,1:T(8,128)(2,1)S(1)}, u32[]{:S(2)}, u32[]{:S(2)}) async-start(bf16[2,128,24,128]{3,2,0,1:T(8,128)(2,1)} %pad_maximum_fusion), calls=%async_computation.5 | async-start | bytes 3145728 | tf_op jit(solution)/shard_map/all_to_all | solution.py:155
  216.0 5.9 fusion
  222.1 3.7 gather_fusion.2
  225.8 2.6 gather_fusion.3
  228.4 2.1 fusion.30
  230.5 27.8 %all-to-all-done.5 = bf16[2,128,24,128]{3,2,0,1:T(8,128)(2,1)S(1)} async-done(((bf16[2,128,24,128]{3,2,0,1:T(8,128)(2,1)}), bf16[2,128,24,128]{3,2,0,1:T(8,128)(2,1)S(1)}, u32[]{:S(2)}, u32[]{:S(2)}) %all-to-all-start.5) | async-done | bytes 1572896 | tf_op jit(solution)/shard_map/all_to_all | solution.py:155
  259.7 36.7 %scatter_custom_fusion.8 = f32[1024,128]{1,0:T(8,128)} fusion(s32[6144]{0:T(1024)S(1)} %reshape.551, bf16[6144,128]{1,0:T(8,128)(2,1)} %bitcast.92, f32[]{:T(128)} %constant.42.clone.1), kind=kCustom, calls=%fused_computation.21 | custom fusion | flops 1572864 | bytes 2097156 | tf_op jit(solution)/shard_map/scatter-add | solution.py:161
  298.5 506.9 %reduce-scatter.5.cloned.1.call-done = f32[32,640]{1,0:T(8,128)} async-done(((f32[4096,640]{1,0:T(8,128)}), f32[32,640]{1,0:T(8,128)}) %reduce-scatter.5.cloned.1.call-update) | async-done | bytes 81936 | tf_op jit(solution)/shard_map/reduce_scatter | solution.py:187
  807.3 2.1 multiply_subtract_fusion
  809.4 81.2 %reduce-scatter.7.cloned.1.call-done = f32[320,32]{1,0:T(8,128)} async-done(((f32[640,32]{1,0:T(8,128)}), f32[320,32]{1,0:T(8,128)}) %reduce-scatter.7.cloned.1.call-update) | async-done | bytes 40976
  (124 shorter events, 23.7 us)
Async XLA Ops:
  8.0 107.9 %copy-start = (bf16[512,128]{1,0:T(8,128)(2,1)S(1)}, bf16[512,128]{1,0:T(8,128)(2,1)}, u32[]{:S(2)}) copy-start(bf16[512,128]{1,0:T(8,128)(2,1)} %param.37) | copy-start | bytes 393220
  8.0 58.9 %copy-start.1 = (f32[1024,128]{1,0:T(8,128)S(1)}, f32[1024,128]{1,0:T(8,128)}, u32[]{:S(2)}) copy-start(f32[1024,128]{1,0:T(8,128)} %param.33) | copy-start | bytes 1572868
  20.2 26.2 %all-to-all-start = ((s32[128,1,24]{2,1,0:T(1,128)}), s32[128,1,24]{2,1,0:T(1,128)S(1)}, u32[]{:S(2)}, u32[]{:S(2)}) async-start(s32[128,1,24]{2,1,0:T(1,128)} %bitcast.4), calls=%async_computation | async-start | bytes 131072 | tf_op jit(solution)/shard_map/all_to_all | solution.py:123
  77.6 29.3 %all-to-all-start.1 = ((bf16[128,24,128]{2,1,0:T(8,128)(2,1)}), bf16[128,24,128]{2,1,0:T(8,128)(2,1)S(1)}, u32[]{:S(2)}, u32[]{:S(2)}) async-start(bf16[128,24,128]{2,1,0:T(8,128)(2,1)} %bitcast.5), calls=%async_computation.1 | async-start | bytes 1572864 | tf_op jit(solution)/shard_map/all_to_all | solution.py:135
  85.0 30.8 %copy-start.6 = (bf16[4096]{0:T(1024)(128)(2,1)S(1)}, bf16[4096]{0:T(1024)(128)(2,1)}, u32[]{:S(2)}) copy-start(bf16[4096]{0:T(1024)(128)(2,1)} %param.40) | copy-start | bytes 24580
  85.1 30.8 %copy-start.9 = (s32[2,1,1536]{2,1,0:T(1,128)S(1)}, s32[2,1,1536]{2,1,0:T(1,128)}, u32[]{:S(2)}) copy-start(s32[2,1,1536]{2,1,0:T(1,128)} %param.27) | copy-start | bytes 36868
  85.1 30.8 %copy-start.11 = (bf16[128,512]{1,0:T(8,128)(2,1)S(1)}, bf16[128,512]{1,0:T(8,128)(2,1)}, u32[]{:S(2)}) copy-start(bf16[128,512]{1,0:T(8,128)(2,1)} %param.35) | copy-start | bytes 393220
  85.1 30.8 %copy-start.12 = (bf16[2,128,128]{2,1,0:T(8,128)(2,1)S(1)}, bf16[2,128,128]{2,1,0:T(8,128)(2,1)}, u32[]{:S(2)}) copy-start(bf16[2,128,128]{2,1,0:T(8,128)(2,1)} %param.24) | copy-start | bytes 196612
  85.1 30.8 %copy-start.14 = (f32[512]{0:T(512)S(1)}, f32[512]{0:T(512)}, u32[]{:S(2)}) copy-start(f32[512]{0:T(512)} %param.36) | copy-start | bytes 6148
  85.1 31.4 %copy-start.7 = (s32[2,1,1536]{2,1,0:T(1,128)S(1)}, s32[2,1,1536]{2,1,0:T(1,128)}, u32[]{:S(2)}) copy-start(s32[2,1,1536]{2,1,0:T(1,128)} %param.28) | copy-start | bytes 36868
  93.4 57.7 %copy-start.13 = (f32[4096]{0:T(1024)S(1)}, f32[4096]{0:T(1024)}, u32[]{:S(2)}) copy-start(f32[4096]{0:T(1024)} %param.39) | copy-start | bytes 49156
  106.9 29.3 %all-to-all-start.3 = ((bf16[128,24,128]{2,1,0:T(8,128)(2,1)}), bf16[128,24,128]{2,1,0:T(8,128)(2,1)S(1)}, u32[]{:S(2)}, u32[]{:S(2)}) async-start(bf16[128,24,128]{2,1,0:T(8,128)(2,1)} %bitcast.10), calls=%async_computation.3 | async-start | bytes 1572864 | tf_op jit(solution)/shard_map/all_to_all | solution.py:135
  115.6 689.8 %reduce-scatter.5.cloned.1.call-start = ((), (), s32[]{:S(2)}) async-start(), calls=%async_computation.9 | async-start | bytes 10567680 | tf_op jit(solution)/shard_map/reduce_scatter | solution.py:187
  155.5 2.1 copy-start.15
  155.5 1.2 copy-start.10
  164.4 0.7 copy-start.4
  164.4 3.7 copy-start.8
  164.4 26.6 %copy-start.2 = (bf16[2,1,1536,128]{3,2,1,0:T(8,128)(2,1)S(1)}, bf16[2,1,1536,128]{3,2,1,0:T(8,128)(2,1)}, u32[]{:S(2)}) copy-start(bf16[2,1,1536,128]{3,2,1,0:T(8,128)(2,1)} %param.32) | copy-start | bytes 2359300
  181.6 20.8 %all-to-all-start.4 = ((s32[2,128,24]{2,0,1:T(2,128)}), s32[2,128,24]{2,0,1:T(2,128)S(1)}, u32[]{:S(2)}, u32[]{:S(2)}) async-start(s32[2,128,24]{2,0,1:T(2,128)} %copy.53), calls=%async_computation.4 | async-start | bytes 262144 | tf_op jit(solution)/shard_map/all_to_all | solution.py:126
  202.4 55.9 %all-to-all-start.5 = ((bf16[2,128,24,128]{3,2,0,1:T(8,128)(2,1)}), bf16[2,128,24,128]{3,2,0,1:T(8,128)(2,1)S(1)}, u32[]{:S(2)}, u32[]{:S(2)}) async-start(bf16[2,128,24,128]{3,2,0,1:T(8,128)(2,1)} %pad_maximum_fusion), calls=%async_computation.5 | async-start | bytes 3145728 | tf_op jit(solution)/shard_map/all_to_all | solution.py:155
  215.6 591.6 %all-reduce.2.cloned.1.call-start = ((), (), s32[]{:S(2)}) async-start(), calls=%async_computation.8 | async-start | bytes 1048576 | tf_op jit(solution)/shard_map/psum | solution.py:163
  259.7 547.6 %copy-start.3 = (f32[1024,128]{1,0:T(8,128)S(1)}, f32[1024,128]{1,0:T(8,128)}, u32[]{:S(2)}) copy-start(f32[1024,128]{1,0:T(8,128)} %param.34) | copy-start | bytes 1572868
  259.7 631.9 %copy-start.5 = (f32[320,32]{0,1:T(8,128)S(1)}, f32[320,32]{0,1:T(8,128)}, u32[]{:S(2)}) copy-start(f32[320,32]{0,1:T(8,128)} %param.41) | copy-start | bytes 122884
  296.4 594.2 %reduce-scatter.7.cloned.1.call-start = ((), (), s32[]{:S(2)}) async-start(), calls=%async_computation.10 | async-start | bytes 491520
Sparse Core Ops, SparseCore 0:
  164.6 640.7 reduce-scatter.4
Sparse Core Ops, SparseCore 1:
  296.5 25.1 all-reduce.1
  807.3 83.3 reduce-scatter.6
where the time goes:
time: 911 us; the launch traced here: 900 us
  waiting for transfers between devices  637 us (70%)
  other arithmetic  82.8 us (9%)
  local copies, waits for them, and re-layouts  67 us (7%)
  starting transfers between devices  54.3 us (6%)
  matrix products  22.5 us (2%)
  blocking collectives  20 us (2%)
  between operations  16.6 us (2%)
    reduce_scatter x1, waiting for transfers between devices, per_device(): lax.psum_scatter(lax.dot_general(top_delta, joined, (((0,), (0,)), ((), (...  507 us
    unnamed x4, waiting for transfers between devices  81.3 us
    scatter-add x1, other arithmetic, per_device(): shard_sum = jnp.zeros((table_rows, row_width), jnp.float32).at[targets].a...  36.7 us
    scatter-add x2, other arithmetic, per_device(): jax.ops.segment_sum(picked, bag_ids[micro_index], num_segments=bag_count,...  29.6 us
    all_to_all x1, waiting for transfers between devices, per_device(): lax.all_to_all(outgoing, 'emb', split_axis=1, concat_axis=1, tiled=True)  27.8 us
    scatter x4, local copies, waits for them, and re-layouts, pack_index(): return jnp.full((buffer_size,), -1, jnp.int32).at[slot_list].set(values)  24.8 us
    all_to_all x1, blocking collectives, per_device(): lax.all_to_all(requests[micro_index], 'emb', split_axis=0, concat_axis=0,...  20 us
  transfers between devices with their start and end apart: 8, of which 7 were waited for; matrix products, arithmetic and copies ran while one was open for 13% of the time, Pallas kernels for 0%

commit v1 on v0

v1 whole, which is shorter than its diff:
```python
import functools

import jax
import jax.numpy as jnp
from jax import lax
from jax.experimental import pallas as pl
from jax.experimental.pallas import tpu as pltpu
from jax.sharding import Mesh, PartitionSpec as P

FEATS = 4
CAP = 24
RING = 8
LEARN_RATE = 0.1
LOSS_SCALE = 64.0
LANES = 128
VMEM = 48 * 1024 * 1024
BF = jnp.bfloat16
F32 = jnp.float32
I32 = jnp.int32


def iota(shape, axis):
    return lax.broadcasted_iota(I32, shape, axis)


def ones_where(cond):
    return jnp.where(cond, 1.0, 0.0).astype(BF)


def mm(a, b):
    return jnp.dot(a, b, preferred_element_type=F32)


def call(body, out_shape, scratch=(), **more):
    return pl.pallas_call(
        body,
        out_shape=out_shape,
        scratch_shapes=scratch,
        compiler_params=pltpu.CompilerParams(vmem_limit_bytes=VMEM),
        **more,
    )


def nt(a, b):
    return lax.dot_general(a, b, (((1,), (1,)), ((), ())), preferred_element_type=F32)


def route_body(owner_ref, old_owner_ref, row_ref, old_row_ref, bag_ref, req_ref, bagpos_ref, pos_ref):
    peers = req_ref.shape[0]
    length = owner_ref.shape[2]
    chunk = 256 if length % 256 == 0 else length
    upper = ones_where(iota((chunk, chunk), 0) <= iota((chunk, chunk), 1))
    zero = jnp.zeros((LANES, length), F32)
    total = jnp.zeros((peers, LANES), F32)
    bag_total = jnp.zeros((peers, LANES), F32)
    for turn in range(4):
        mb = turn % 2
        own = (owner_ref if turn < 2 else old_owner_ref)[mb]
        row = (row_ref if turn < 2 else old_row_ref)[mb] + 1
        hit = own == iota((peers, length), 0)
        onehot = ones_where(hit)
        carry = jnp.zeros((peers, 1), F32)
        parts = []
        for at in range(0, length, chunk):
            counted = mm(onehot[:, at : at + chunk], upper) + carry
            carry = counted[:, chunk - 1 :]
            parts.append(counted)
        counted = jnp.concatenate(parts, axis=1)
        rank = jnp.sum(jnp.where(hit, counted, 0.0), axis=0, keepdims=True).astype(I32) - 1
        place = iota((LANES, length), 0) == rank + turn * CAP

        def spread(value):
            high = jnp.where(place, (value >> 5).astype(F32), zero).astype(BF)
            low = jnp.where(place, (value & 31).astype(F32), zero).astype(BF)
            return nt(onehot, high) * 32.0 + nt(onehot, low)

        total += spread(row)
        if turn < 2:
            bag_total += spread(bag_ref[mb])
        else:
            pos_ref[mb] = own * CAP + rank
    req_ref[...] = total.astype(I32) - 1
    bagpos_ref[...] = bag_total.astype(I32) - 1


def gather_body(z_ref, req_ref, mine_ref, other_ref, first_ref, second_ref, cols_ref, hot_ref, out_ref):
    groups = first_ref.shape[0]
    ring = mine_ref.shape[0]
    half = mine_ref.shape[1]
    both = 2 * CAP
    for z in range(ring):
        part = req_ref[pl.ds(z, groups, stride=ring), :]
        part = jnp.concatenate([part, jnp.zeros((LANES - groups, LANES), I32)], axis=0)
        cols_ref[z] = part.T
    me = z_ref[0]

    def step(pair, carry):
        for zi in range(2):
            z = pair * 2 + zi
            offset = lax.rem(me - z + ring, ring)
            cols = cols_ref[z]
            for w in range(groups):
                hot_ref[w * both : (w + 1) * both, :] = ones_where(
                    cols[:both, w : w + 1] == iota((both, 2 * half), 1)
                )
            found = mm(hot_ref[:, :half], mine_ref[offset]) + mm(hot_ref[:, half:], other_ref[offset])
            out_ref[zi] = found.reshape(groups, both, LANES)
        for mb, ref in enumerate((first_ref, second_ref)):
            ref[:, pl.ds(pl.multiple_of(pair * both, both), both), :] = jnp.concatenate(
                [out_ref[zi, :, mb * CAP : (mb + 1) * CAP, :] for zi in range(2)], axis=1
            ).astype(BF)
        return carry

    lax.fori_loop(0, ring // 2, step, 0)


def pool_body(bagpos_ref, reply_ref, out_ref):
    groups, per, width = reply_ref.shape
    samples = out_ref.shape[0]
    bags = samples * FEATS
    flat = reply_ref[...].reshape(groups * per, width)
    size = 2 * per
    total = jnp.zeros((bags, width), F32)
    for at in range(0, groups * per, size):
        hot = ones_where(bagpos_ref[:, at : at + size] == iota((bags, size), 0))
        total += mm(hot, flat[at : at + size])
    for feat in range(FEATS):
        out_ref[:, feat * width : (feat + 1) * width] = total[
            feat * samples : (feat + 1) * samples
        ].astype(BF)


def outgoing_body(pos_ref, grad_ref, out_ref):
    here, _, per, width = out_ref.shape
    length = pos_ref.shape[2]
    first = pl.program_id(0) * here * per
    for mb in range(2):
        pos = pos_ref[mb] - first
        for w in range(here):
            hot = ones_where(pos == iota((per, length), 0) + w * per)
            out_ref[w, mb] = mm(hot, grad_ref[mb]).astype(BF)


def scatter_body(rows_ref, grad_ref, out_ref):
    groups = grad_ref.shape[0]
    width = grad_ref.shape[3]
    table_rows = out_ref.shape[1]
    wide = grad_ref[...].astype(F32)
    count = groups * 2 * CAP
    for zi in range(2):
        part = wide[:, :, zi * CAP : (zi + 1) * CAP, :].reshape(count, width).astype(BF)
        hot = ones_where(rows_ref[zi] == iota((table_rows, count), 0))
        out_ref[zi] = mm(hot, part)


def pick_body(bag_ref, back_ref, out_ref):
    samples = back_ref.shape[0] // 2
    bags = samples * FEATS
    length = bag_ref.shape[2]
    width = back_ref.shape[1] // FEATS
    for mb in range(2):
        rows = back_ref[mb * samples : (mb + 1) * samples, :]
        grads = jnp.concatenate(
            [rows[:, feat * width : (feat + 1) * width] for feat in range(FEATS)], axis=0
        ).astype(BF)
        for at in range(0, length, LANES):
            ids = jnp.broadcast_to(bag_ref[mb, :, at : at + LANES], (LANES, LANES)).T
            hot = jnp.concatenate(
                [ones_where(ids == iota((LANES, LANES), 1) + block) for block in range(0, bags, LANES)],
                axis=1,
            )
            out_ref[mb, 0, at : at + LANES, :] = mm(hot, grads).astype(BF)


def shape_of(shape, dtype):
    return jax.ShapeDtypeStruct(shape, dtype)


def ring_of(size, shift):
    return [(i, (i + shift) % size) for i in range(size)]


def per_device(
    dense_input,
    id_owner,
    id_row,
    id_mask,
    bag_index,
    labels,
    stale_owner,
    stale_row,
    stale_grad,
    emb_table,
    grad_squares,
    bottom_first,
    bottom_bias,
    bottom_second,
    top_weight,
    top_bias,
    out_weight,
    top_squares,
):
    groups = lax.axis_size("w")
    ring = lax.axis_size("z")
    peers = groups * ring
    core = lax.axis_index("nn")
    my_z = lax.axis_index("z")
    swap = [(0, 1), (1, 0)]
    length = id_row.shape[2]
    width = emb_table.shape[1]
    table_rows = emb_table.shape[0]
    half_rows = table_rows // 2
    samples = dense_input.shape[1]
    bags = samples * FEATS
    per = ring * CAP

    my_half = lax.dynamic_slice_in_dim(emb_table, core * half_rows, half_rows, 0).astype(BF)
    blocks = [my_half]
    ahead, back = my_half, my_half
    behind = []
    for step in range(1, ring // 2 + 1):
        ahead = lax.ppermute(ahead, "z", ring_of(ring, 1))
        blocks.append(ahead)
        if step < ring - ring // 2:
            back = lax.ppermute(back, "z", ring_of(ring, -1))
            behind.append(back)
    mine_table = jnp.stack(blocks + behind[::-1])
    other_table = lax.ppermute(mine_table, "nn", swap)

    bag_order = (bag_index & (FEATS - 1)) * samples + (bag_index >> 2)
    bag_or_none = jnp.where(id_mask > 0, bag_order + 1, 0)
    requests, bagpos, old_pos = call(
        route_body,
        (
            shape_of((peers, LANES), I32),
            shape_of((peers, LANES), I32),
            shape_of((2, 1, length), I32),
        ),
    )(
        id_owner.reshape(2, 1, length),
        stale_owner.reshape(2, 1, length),
        id_row,
        stale_row,
        bag_or_none,
    )
    asked = lax.all_to_all(requests, "w", split_axis=0, concat_axis=0, tiled=True)
    bag_rows = (
        bagpos[:, : 2 * CAP].reshape(peers, 2, CAP).transpose(1, 0, 2).reshape(2, 1, peers * CAP)
    )
    old_rows = (
        asked[:, 2 * CAP : 4 * CAP]
        .reshape(groups, ring, 2 * CAP)
        .transpose(1, 0, 2)
        .reshape(ring, 1, groups * 2 * CAP)
    )
    wanted = jnp.where(asked >= 0, asked ^ (core * half_rows), -1)

    replies = call(
        gather_body,
        tuple(shape_of((groups, per, width), BF) for _ in range(2)),
        (
            pltpu.VMEM((ring, LANES, LANES), I32),
            pltpu.VMEM((groups * 2 * CAP, table_rows), BF),
            pltpu.VMEM((2, groups, 2 * CAP, width), F32),
        ),
        in_specs=[pl.BlockSpec(memory_space=pltpu.SMEM)] + [pl.BlockSpec()] * 3,
    )(my_z.reshape(1), wanted, mine_table, other_table)
    pooled = []
    for mb in range(2):
        here = lax.all_to_all(replies[mb], "w", split_axis=0, concat_axis=0, tiled=True)
        pooled.append(call(pool_body, shape_of((samples, FEATS * width), BF))(bag_rows[mb], here))
    pooled = jnp.concatenate(pooled, axis=0)

    cut = 4
    outgoing = call(
        outgoing_body,
        shape_of((groups, 2, per, width), BF),
        grid=(cut,),
        in_specs=[
            pl.BlockSpec((2, 1, length), lambda i: (0, 0, 0)),
            pl.BlockSpec((2, length, width), lambda i: (0, 0, 0)),
        ],
        out_specs=pl.BlockSpec((groups // cut, 2, per, width), lambda i: (i, 0, 0, 0)),
    )(old_pos, stale_grad.reshape(2, length, width))
    incoming = lax.all_to_all(outgoing, "w", split_axis=0, concat_axis=0, tiled=True)
    sums = call(
        scatter_body,
        shape_of((ring, table_rows, width), F32),
        grid=(ring // 2,),
        in_specs=[
            pl.BlockSpec((2, 1, groups * 2 * CAP), lambda i: (i, 0, 0)),
            pl.BlockSpec((groups, 2, 2 * CAP, width), lambda i: (0, 0, i, 0)),
        ],
        out_specs=pl.BlockSpec((2, table_rows, width), lambda i: (i, 0, 0)),
    )(old_rows, incoming)
    sums = sums.reshape(ring, 2, half_rows, width)
    theirs = lax.dynamic_index_in_dim(sums, 1 - core, 1, keepdims=False)
    ours = lax.dynamic_index_in_dim(sums, core, 1, keepdims=False)
    ours = (ours + lax.ppermute(theirs, "nn", swap)).astype(BF)
    ours = lax.all_to_all(ours, "z", split_axis=0, concat_axis=0, tiled=True)
    ours = jnp.sum(ours.astype(F32), axis=0)
    theirs = lax.ppermute(ours, "nn", swap)
    row_sum = jnp.where(
        core == 0,
        jnp.concatenate([ours, theirs], axis=0),
        jnp.concatenate([theirs, ours], axis=0),
    )
    new_squares = grad_squares + row_sum * row_sum
    new_table = emb_table - LEARN_RATE * row_sum * lax.rsqrt(new_squares)

    dense_rows = dense_input.reshape(2 * samples, dense_input.shape[2])
    label_rows = labels.reshape(2 * samples)
    hidden = jax.nn.relu(mm(dense_rows, bottom_first) + bottom_bias).astype(BF)
    bottom = jax.nn.relu(mm(hidden, bottom_second)).astype(BF)
    joined = jnp.concatenate([bottom, pooled], axis=1)
    before = mm(joined, top_weight) + top_bias
    gate = jax.nn.sigmoid(before)
    active = (before * gate).astype(BF)
    logits = mm(active, out_weight)
    logit_grad = LOSS_SCALE * (jax.nn.sigmoid(logits) - label_rows.astype(F32))
    top_delta = (
        logit_grad[:, None]
        * out_weight.astype(F32)[None, :]
        * gate
        * (1.0 + before * (1.0 - gate))
    ).astype(BF)
    split_at = bottom.shape[1]
    back_grad = nt(top_delta, top_weight[split_at:])
    row_grads = call(pick_body, shape_of((2, 1, length, width), BF))(bag_or_none - 1, back_grad)

    inputs = joined.shape[1] // 2

    def outer(at):
        part = lax.dynamic_slice_in_dim(joined, at * inputs, inputs, 1)
        return lax.dot_general(top_delta, part, (((0,), (0,)), ((), ())), preferred_element_type=F32)

    sent = lax.ppermute(outer(1 - core).astype(BF), "nn", swap)
    unit_part = (outer(core) + sent.astype(F32)).astype(BF)
    units = unit_part.shape[0] // peers
    unit_part = lax.all_to_all(
        unit_part.reshape(groups, ring * units, inputs), "w", split_axis=0, concat_axis=0, tiled=True
    )
    unit_part = jnp.sum(unit_part.astype(F32), axis=0).astype(BF).reshape(ring, units, inputs)
    unit_part = lax.all_to_all(unit_part, "z", split_axis=0, concat_axis=0, tiled=True)
    top_grad = jnp.sum(unit_part.astype(F32), axis=0).T
    top_step = top_grad * lax.rsqrt(top_squares + top_grad * top_grad)
    return (row_grads, new_table, new_squares, top_step)


def solution(mesh, ring=RING):
    devices = mesh.devices
    fine = Mesh(devices.reshape(devices.shape[0] // ring, ring, devices.shape[1]), ("w", "z", "nn"))
    rows = ("w", "z", "nn")
    emb = ("w", "z")
    return jax.shard_map(
        per_device,
        mesh=fine,
        in_specs=(
            P(None, rows, None),
            P(None, rows, None),
            P(None, rows, None),
            P(None, rows, None),
            P(None, rows, None),
            P(None, rows),
            P(None, rows, None),
            P(None, rows, None),
            P(None, rows, None, None),
            P(emb, None),
            P(emb, None),
            P(),
            P(),
            P(),
            P(),
            P(),
            P(),
            P("nn", emb),
        ),
        out_specs=(
            P(None, rows, None, None),
            P(emb, None),
            P(emb, None),
            P("nn", emb),
        ),
        check_vma=False,
    )
```

time: 911 us -> 224 us (0.25); the launches traced: 900 us -> 223 us
  waiting for transfers between devices: 637 us -> 96 us
  other arithmetic: 82.8 us -> 14.5 us
  local copies, waits for them, and re-layouts: 67 us -> 14.3 us
  Pallas kernels: 0 us -> 24.6 us
  blocking collectives: 20 us -> 0 us
  between operations: 16.6 us -> 1.02 us
    reduce_scatter x1 -> x0, waiting for transfers between devices: 507 us -> none  [per_device(): lax.psum_scatter(lax.dot_general(top_delta, joined, (((0,), (0,)), ((), (...]
    unnamed x4 -> x0, waiting for transfers between devices: 81.3 us -> none
    scatter-add x3 -> x0, other arithmetic: 66.3 us -> none  [the longest x1 36.7 us: per_device(): shard_sum = jnp.zeros((table_rows, row_width), jnp.float32).at[targets].a...]
    scatter x6 -> x0, local copies, waits for them, and re-layouts: 34.2 us -> none  [the longest x4 24.8 us: pack_index(): return jnp.full((buffer_size,), -1, jnp.int32).at[slot_list].set(values)]
    all_to_all x5 -> x7, waiting for transfers between devices: 48.7 us -> 81.2 us  [the longest x1 36.9 us: per_device(): lax.all_to_all(unit_part.reshape(groups, ring * units, inputs), 'w', spli...]
    pallas_call x0 -> x7, Pallas kernels: none -> 24.6 us  [the longest x1 6.47 us: per_device(): call(gather_body, tuple((shape_of((groups, per, width), BF) for _ in rang...]
    gather x4 -> x0, local copies, waits for them, and re-layouts: 22.9 us -> none  [the longest x2 16.6 us: per_device(): jnp.take(emb_table, lookup, axis=0).astype(jnp.bfloat16)]
    all_to_all x1 -> x0, blocking collectives: 20 us -> none  [per_device(): lax.all_to_all(requests[micro_index], 'emb', split_axis=0, concat_axis=0,...]
  transfers between devices with their start and end apart: 8 -> 18, of which waited for: 7 -> 9; matrix products, arithmetic and copies ran while one was open for 13% -> 16% of each run, Pallas kernels for 0% -> 11%
where the time goes in v1:
time: 224 us; the launch traced here: 223 us
  waiting for transfers between devices  96 us (43%)
  starting transfers between devices  56 us (25%)
  Pallas kernels  24.6 us (11%)
  matrix products  16.2 us (7%)
  other arithmetic  14.5 us (6%)
  local copies, waits for them, and re-layouts  14.3 us (6%)
    all_to_all x1, waiting for transfers between devices, per_device(): lax.all_to_all(unit_part.reshape(groups, ring * units, inputs), 'w', spli...  36.9 us
    all_to_all x1, waiting for transfers between devices, per_device(): ours = lax.all_to_all(ours, 'z', split_axis=0, concat_axis=0, tiled=True)  24.6 us
    ppermute x4, waiting for transfers between devices, per_device(): ahead = lax.ppermute(ahead, 'z', ring_of(ring, 1))  12 us
    all_to_all x2, starting transfers between devices, per_device(): lax.all_to_all(replies[mb], 'w', split_axis=0, concat_axis=0, tiled=True)  11.2 us
    ppermute x3, starting transfers between devices, per_device(): back = lax.ppermute(back, 'z', ring_of(ring, -1))  10.5 us
    all_to_all x2, waiting for transfers between devices, per_device(): lax.all_to_all(replies[mb], 'w', split_axis=0, concat_axis=0, tiled=True)  9.38 us
    unnamed x42, local copies, waits for them, and re-layouts  8.71 us
    all_to_all x1, waiting for transfers between devices, per_device(): lax.all_to_all(outgoing, 'w', split_axis=0, concat_axis=0, tiled=True)  8.18 us
  transfers between devices with their start and end apart: 18, of which 9 were waited for; matrix products, arithmetic and copies ran while one was open for 16% of the time, Pallas kernels for 11%

profile of v1, /device:TPU:8, one launch (start us, length us, event | category | flops | bytes accessed | tf_op | source)
XLA Modules:
  0.0 222.6 jit_solution(11538469803962388594)
XLA Ops:
  1.7 2.0 collective-permute-start
  3.7 4.0 %collective-permute-start.4 = (bf16[512,128]{1,0:T(8,128)(2,1)S(1)}, bf16[512,128]{1,0:T(8,128)(2,1)S(1)}, u32[]{:S(2)}, u32[]{:S(2)}) collective-permute-start(bf16[512,128]{1,0:T(8,128)(2,1)S(1)} %get-tuple-element.17), channel_id=1, source_target_pairs={{0,14},{2,0},{4,2},{6,4},{8,6},{10,8},{12,10},{14,12},{1,15},{3,1}... | collective-permute-start | bytes 393224 | tf_op jit(solution)/shard_map/ppermute | solution.py:225
  11.3 4.0 %shard_map.201 = (s32[128,128]{1,0:T(8,128)}, s32[128,128]{1,0:T(8,128)S(1)}, s32[2,1,1536]{2,1,0:T(1,128)S(1)}) custom-call(s32[2,1,1536]{2,1,0:T(1,128)S(1)} %bitcast.71, s32[2,1,1536]{2,1,0:T(1,128)S(1)} %bitcast.72, s32[2,1,1536]{2,1,0:T(1,128)S(1)} %copy-done.6, s32[2,1,1536]{2,1,0:T(1,128)S(1)} %copy-done.7, s32[2,1,1536]{2,1,0:T(1,128)S(1)} %get-tuple-element.19.bag_ref), custom_call_target="tpu_custom_call" | custom-call | tf_op jit(solution)/shard_map/pallas_call | solution.py:232
  15.3 7.4 %all-to-all-start = ((s32[16,8,128]{2,1,0:T(8,128)}), s32[16,8,128]{2,1,0:T(8,128)S(1)}, u32[]{:S(2)}, u32[]{:S(2)}) async-start(s32[16,8,128]{2,1,0:T(8,128)} %bitcast.6), calls=%async_computation | async-start | bytes 131072 | tf_op jit(solution)/shard_map/all_to_all | solution.py:246
  23.8 6.3 %shard_map.206 = bf16[16,2,192,128]{3,2,1,0:T(8,128)(2,1)} custom-call(s32[2,1,1536]{2,1,0:T(1,128)S(1)} %get-tuple-element.13.pos_ref, bf16[2,1536,128]{2,1,0:T(8,128)(2,1)S(1)} %bitcast.69), custom_call_target="tpu_custom_call" | custom-call | tf_op jit(solution)/shard_map/pallas_call | solution.py:275
  30.1 3.2 %collective-permute-start.5 = (bf16[512,128]{1,0:T(8,128)(2,1)S(1)}, bf16[512,128]{1,0:T(8,128)(2,1)S(1)}, u32[]{:S(2)}, u32[]{:S(2)}) collective-permute-start(bf16[512,128]{1,0:T(8,128)(2,1)S(1)} %collective-permute-done.4), channel_id=1, source_target_pairs={{0,14},{2,0},{4,2},{6,4},{8,6},{10,8},{12,10},{14,12},{1,15},{3,1}... | collective-permute-start | bytes 393224 | tf_op jit(solution)/shard_map/ppermute | solution.py:225
  33.3 2.9 %collective-permute-done.1 = bf16[512,128]{1,0:T(8,128)(2,1)S(1)} collective-permute-done((bf16[512,128]{1,0:T(8,128)(2,1)S(1)}, bf16[512,128]{1,0:T(8,128)(2,1)S(1)}, u32[]{:S(2)}, u32[]{:S(2)}) %collective-permute-start.1) | collective-permute-done | bytes 131104 | tf_op jit(solution)/shard_map/ppermute | solution.py:222
  36.3 3.2 %collective-permute-start.6 = (bf16[512,128]{1,0:T(8,128)(2,1)S(1)}, bf16[512,128]{1,0:T(8,128)(2,1)S(1)}, u32[]{:S(2)}, u32[]{:S(2)}) collective-permute-start(bf16[512,128]{1,0:T(8,128)(2,1)S(1)} %collective-permute-done.5), channel_id=1, source_target_pairs={{0,14},{2,0},{4,2},{6,4},{8,6},{10,8},{12,10},{14,12},{1,15},{3,1}... | collective-permute-start | bytes 393224 | tf_op jit(solution)/shard_map/ppermute | solution.py:225
  39.5 2.9 %collective-permute-done.2 = bf16[512,128]{1,0:T(8,128)(2,1)S(1)} collective-permute-done((bf16[512,128]{1,0:T(8,128)(2,1)S(1)}, bf16[512,128]{1,0:T(8,128)(2,1)S(1)}, u32[]{:S(2)}, u32[]{:S(2)}) %collective-permute-start.2) | collective-permute-done | bytes 131104 | tf_op jit(solution)/shard_map/ppermute | solution.py:222
  42.5 6.2 %collective-permute-done.3 = bf16[512,128]{1,0:T(8,128)(2,1)S(1)} collective-permute-done((bf16[512,128]{1,0:T(8,128)(2,1)S(1)}, bf16[512,128]{1,0:T(8,128)(2,1)S(1)}, u32[]{:S(2)}, u32[]{:S(2)}) %collective-permute-start.3) | collective-permute-done | bytes 131104 | tf_op jit(solution)/shard_map/ppermute | solution.py:222
  48.7 7.2 %all-to-all-start.3 = ((bf16[16,2,192,128]{3,2,1,0:T(8,128)(2,1)}), bf16[16,2,192,128]{3,2,1,0:T(8,128)(2,1)S(1)}, u32[]{:S(2)}, u32[]{:S(2)}) async-start(bf16[16,2,192,128]{3,2,1,0:T(8,128)(2,1)} %shard_map.206), calls=%async_computation.3 | async-start | bytes 3145728 | tf_op jit(solution)/shard_map/all_to_all | solution.py:285
  56.1 2.8 %collective-permute-done.7.other_ref = bf16[8,512,128]{2,1,0:T(8,128)(2,1)} collective-permute-done((bf16[8,512,128]{2,1,0:T(8,128)(2,1)S(1)}, bf16[8,512,128]{2,1,0:T(8,128)(2,1)}, u32[]{:S(2)}, u32[]{:S(2)}) %collective-permute-start.7) | collective-permute-done | bytes 1048608 | tf_op jit(solution)/shard_map/ppermute | solution.py:228
  58.9 6.5 %shard_map.202 = (bf16[16,192,128]{2,1,0:T(8,128)(2,1)}, bf16[16,192,128]{2,1,0:T(8,128)(2,1)S(1)}) custom-call(s32[1]{0:T(128)} %bitcast.5.z_ref, s32[128,128]{1,0:T(8,128)S(1)} %xor_select_fusion.req_ref, bf16[8,512,128]{2,1,0:T(8,128)(2,1)S(1)} %bitcast_dynamic-update-slice_fusion.mine_ref, bf16[8,512,128]{2,1,0:T(8,128)(2,1)} %collective-permute-done.7.other_ref), custom_call_target="tpu_custom_call" | custom-call | tf_op jit(solution)/shard_map/pallas_call | solution.py:258
  66.3 8.2 %all-to-all-done.3.grad_ref = bf16[16,2,192,128]{3,2,1,0:T(8,128)(2,1)S(1)} async-done(((bf16[16,2,192,128]{3,2,1,0:T(8,128)(2,1)}), bf16[16,2,192,128]{3,2,1,0:T(8,128)(2,1)S(1)}, u32[]{:S(2)}, u32[]{:S(2)}) %all-to-all-start.3) | async-done | bytes 1572896 | tf_op jit(solution)/shard_map/all_to_all | solution.py:285
  74.4 5.3 %all-to-all-start.1 = ((bf16[16,192,128]{2,1,0:T(8,128)(2,1)}), bf16[16,192,128]{2,1,0:T(8,128)(2,1)S(1)}, u32[]{:S(2)}, u32[]{:S(2)}) async-start(bf16[16,192,128]{2,1,0:T(8,128)(2,1)} %get-tuple-element.11), calls=%async_computation.1 | async-start | bytes 1572864 | tf_op jit(solution)/shard_map/all_to_all | solution.py:270
  79.8 9.4 %all-to-all-done.1.reply_ref = bf16[16,192,128]{2,1,0:T(8,128)(2,1)S(1)} async-done(((bf16[16,192,128]{2,1,0:T(8,128)(2,1)}), bf16[16,192,128]{2,1,0:T(8,128)(2,1)S(1)}, u32[]{:S(2)}, u32[]{:S(2)}) %all-to-all-start.1) | async-done | bytes 786464 | tf_op jit(solution)/shard_map/all_to_all | solution.py:270
  89.2 5.9 %all-to-all-start.2 = ((bf16[16,192,128]{2,1,0:T(8,128)(2,1)}), bf16[16,192,128]{2,1,0:T(8,128)(2,1)S(1)}, u32[]{:S(2)}, u32[]{:S(2)}) async-start(bf16[16,192,128]{2,1,0:T(8,128)(2,1)} %copy-done.2), calls=%async_computation.2 | async-start | bytes 1572864 | tf_op jit(solution)/shard_map/all_to_all | solution.py:270
  100.5 4.0 %shard_map.207 = f32[8,1024,128]{2,1,0:T(8,128)S(1)} custom-call(s32[8,1,768]{2,1,0:T(1,128)S(1)} %reshape.60.rows_ref, bf16[16,2,192,128]{3,2,1,0:T(8,128)(2,1)S(1)} %all-to-all-done.3.grad_ref), custom_call_target="tpu_custom_call" | custom-call | tf_op jit(solution)/shard_map/pallas_call | solution.py:286
  104.6 1.9 copy-done.1
  110.1 4.3 %convolution_add_fusion = f32[256,4096]{1,0:T(8,128)S(1)} fusion(bf16[640,4096]{1,0:T(8,128)(2,1)} %param.32, f32[4096]{0:T(1024)S(1)} %copy-done.15, bf16[128,512]{1,0:T(8,128)(2,1)S(1)} %shard_map.204, bf16[128,512]{1,0:T(8,128)(2,1)S(1)} %shard_map.203, bf16[256,128]{1,0:T(8,128)(2,1)S(1)} %copy-done.12), kind=kOutput, calls=%fused_computation.1 | convolution fusion | flops 1344208896 | bytes 9781248 | tf_op jit(solution)/shard_map/dot_general | solution.py:31
  117.3 2.5 %convolution_convert_fusion = bf16[4096,320]{0,1:T(8,128)(2,1)} fusion(bf16[256,4096]{1,0:T(8,128)(2,1)S(1)} %multiply_convert_fusion, bf16[256,640]{1,0:T(8,128)(2,1)S(1)} %maximum_maximum_fusion, s32[]{:T(128)S(6)} %select_n.40), kind=kOutput, calls=%fused_computation | convolution fusion | flops 672399360 | bytes 4915204 | tf_op jit(solution)/shard_map/dot_general | solution.py:335
  120.3 3.5 %fusion.2 = bf16[8,512,128]{2,1,0:T(8,128)(2,1)} fusion(f32[8,512,128]{2,1,0:T(8,128)} %collective-permute-done.8, f32[8,2,512,128]{3,2,1,0:T(8,128)} %bitcast.68, s32[]{:T(128)S(6)} %select_n.36), kind=kLoop, calls=%fused_computation.10 | loop fusion | flops 1048576 | bytes 5242884 | tf_op jit(solution)/shard_map/convert_element_type | solution.py:299
  123.8 5.5 %all-to-all-start.4 = ((bf16[8,512,128]{2,1,0:T(8,128)(2,1)}), bf16[8,512,128]{2,1,0:T(8,128)(2,1)}, u32[]{:S(2)}, u32[]{:S(2)}) async-start(bf16[8,512,128]{2,1,0:T(8,128)(2,1)} %fusion.2), calls=%async_computation.4 | async-start | bytes 2097152 | tf_op jit(solution)/shard_map/all_to_all | solution.py:300
  129.3 2.7 %add_convert_fusion = bf16[4096,320]{0,1:T(8,128)(2,1)S(1)} fusion(bf16[4096,320]{0,1:T(8,128)(2,1)} %collective-permute-done.10, bf16[256,4096]{1,0:T(8,128)(2,1)S(1)} %multiply_convert_fusion, bf16[256,640]{1,0:T(8,128)(2,1)S(1)} %maximum_maximum_fusion, s32[]{:T(128)S(6)} %select_n.39), kind=kOutput, calls=%fused_computation.2 | convolution fusion | flops 675020800 | bytes 7536644 | tf_op jit(solution)/shard_map/dot_general | solution.py:335
  133.7 24.6 %all-to-all-done.4 = bf16[8,512,128]{2,1,0:T(8,128)(2,1)} async-done(((bf16[8,512,128]{2,1,0:T(8,128)(2,1)}), bf16[8,512,128]{2,1,0:T(8,128)(2,1)}, u32[]{:S(2)}, u32[]{:S(2)}) %all-to-all-start.4) | async-done | bytes 1048608 | tf_op jit(solution)/shard_map/all_to_all | solution.py:300
  158.3 7.3 %all-to-all-start.5 = ((bf16[16,256,320]{1,2,0:T(8,128)(2,1)}), bf16[16,256,320]{1,2,0:T(8,128)(2,1)}, u32[]{:S(2)}, u32[]{:S(2)}) async-start(bf16[16,256,320]{1,2,0:T(8,128)(2,1)} %bitcast.74), calls=%async_computation.5 | async-start | bytes 5242880 | tf_op jit(solution)/shard_map/all_to_all | solution.py:340
  167.3 36.9 %all-to-all-done.5 = bf16[16,256,320]{1,2,0:T(8,128)(2,1)} async-done(((bf16[16,256,320]{1,2,0:T(8,128)(2,1)}), bf16[16,256,320]{1,2,0:T(8,128)(2,1)}, u32[]{:S(2)}, u32[]{:S(2)}) %all-to-all-start.5) | async-done | bytes 2621472 | tf_op jit(solution)/shard_map/all_to_all | solution.py:340
  204.2 2.1 reduce_sum.31
  207.1 4.0 %all-to-all-start.6 = ((bf16[8,32,320]{2,1,0:T(8,128)(2,1)}), bf16[8,32,320]{2,1,0:T(8,128)(2,1)}, u32[]{:S(2)}, u32[]{:S(2)}) async-start(bf16[8,32,320]{2,1,0:T(8,128)(2,1)} %bitcast.25), calls=%async_computation.6 | async-start | bytes 393216 | tf_op jit(solution)/shard_map/all_to_all | solution.py:344
  211.2 3.6 %fusion.back_ref = f32[256,512]{1,0:T(8,128)S(1)} fusion(bf16[256,4096]{1,0:T(8,128)(2,1)S(1)} %multiply_convert_fusion, bf16[640,4096]{1,0:T(8,128)(2,1)} %param.32), kind=kOutput, calls=%fused_computation.3 | convolution fusion | flops 1073741824 | bytes 6815744 | tf_op jit(solution)/shard_map/dot_general | solution.py:45
  216.7 2.2 multiply_subtract_fusion
  218.8 2.1 all-to-all-done.6
  (84 shorter events, 27.1 us)
Async XLA Ops:
  0.6 96.9 %copy-start = (bf16[512,128]{1,0:T(8,128)(2,1)S(1)}, bf16[512,128]{1,0:T(8,128)(2,1)}, u32[]{:S(2)}) copy-start(bf16[512,128]{1,0:T(8,128)(2,1)} %param.31) | copy-start | bytes 393220
  1.7 28.4 %collective-permute-start = (bf16[512,128]{1,0:T(8,128)(2,1)S(1)}, bf16[512,128]{1,0:T(8,128)(2,1)S(1)}, u32[]{:S(2)}, u32[]{:S(2)}) collective-permute-start(bf16[512,128]{1,0:T(8,128)(2,1)S(1)} %get-tuple-element.17), channel_id=1, source_target_pairs={{0,2},{2,4},{4,6},{6,8},{8,10},{10,12},{12,14},{14,0},{1,3},{3,5},... | collective-permute-start | bytes 393224 | tf_op jit(solution)/shard_map/ppermute | solution.py:222
  3.7 26.4 %collective-permute-start.4 = (bf16[512,128]{1,0:T(8,128)(2,1)S(1)}, bf16[512,128]{1,0:T(8,128)(2,1)S(1)}, u32[]{:S(2)}, u32[]{:S(2)}) collective-permute-start(bf16[512,128]{1,0:T(8,128)(2,1)S(1)} %get-tuple-element.17), channel_id=1, source_target_pairs={{0,14},{2,0},{4,2},{6,4},{8,6},{10,8},{12,10},{14,12},{1,15},{3,1}... | collective-permute-start | bytes 393224 | tf_op jit(solution)/shard_map/ppermute | solution.py:225
  8.5 0.7 copy-start.4
  15.3 33.4 %all-to-all-start = ((s32[16,8,128]{2,1,0:T(8,128)}), s32[16,8,128]{2,1,0:T(8,128)S(1)}, u32[]{:S(2)}, u32[]{:S(2)}) async-start(s32[16,8,128]{2,1,0:T(8,128)} %bitcast.6), calls=%async_computation | async-start | bytes 131072 | tf_op jit(solution)/shard_map/all_to_all | solution.py:246
  22.7 1.1 copy-start.3
  30.1 6.2 %collective-permute-start.1 = (bf16[512,128]{1,0:T(8,128)(2,1)S(1)}, bf16[512,128]{1,0:T(8,128)(2,1)S(1)}, u32[]{:S(2)}, u32[]{:S(2)}) collective-permute-start(bf16[512,128]{1,0:T(8,128)(2,1)S(1)} %collective-permute-done), channel_id=1, source_target_pairs={{0,2},{2,4},{4,6},{6,8},{8,10},{10,12},{12,14},{14,0},{1,3},{3,5},... | collective-permute-start | bytes 393224 | tf_op jit(solution)/shard_map/ppermute | solution.py:222
  30.1 6.2 %collective-permute-start.5 = (bf16[512,128]{1,0:T(8,128)(2,1)S(1)}, bf16[512,128]{1,0:T(8,128)(2,1)S(1)}, u32[]{:S(2)}, u32[]{:S(2)}) collective-permute-start(bf16[512,128]{1,0:T(8,128)(2,1)S(1)} %collective-permute-done.4), channel_id=1, source_target_pairs={{0,14},{2,0},{4,2},{6,4},{8,6},{10,8},{12,10},{14,12},{1,15},{3,1}... | collective-permute-start | bytes 393224 | tf_op jit(solution)/shard_map/ppermute | solution.py:225
  36.3 6.2 %collective-permute-start.2 = (bf16[512,128]{1,0:T(8,128)(2,1)S(1)}, bf16[512,128]{1,0:T(8,128)(2,1)S(1)}, u32[]{:S(2)}, u32[]{:S(2)}) collective-permute-start(bf16[512,128]{1,0:T(8,128)(2,1)S(1)} %collective-permute-done.1), channel_id=1, source_target_pairs={{0,2},{2,4},{4,6},{6,8},{8,10},{10,12},{12,14},{14,0},{1,3},{3,5},... | collective-permute-start | bytes 393224 | tf_op jit(solution)/shard_map/ppermute | solution.py:222
  36.3 12.4 %collective-permute-start.6 = (bf16[512,128]{1,0:T(8,128)(2,1)S(1)}, bf16[512,128]{1,0:T(8,128)(2,1)S(1)}, u32[]{:S(2)}, u32[]{:S(2)}) collective-permute-start(bf16[512,128]{1,0:T(8,128)(2,1)S(1)} %collective-permute-done.5), channel_id=1, source_target_pairs={{0,14},{2,0},{4,2},{6,4},{8,6},{10,8},{12,10},{14,12},{1,15},{3,1}... | collective-permute-start | bytes 393224 | tf_op jit(solution)/shard_map/ppermute | solution.py:225
  42.4 6.2 %collective-permute-start.3 = (bf16[512,128]{1,0:T(8,128)(2,1)S(1)}, bf16[512,128]{1,0:T(8,128)(2,1)S(1)}, u32[]{:S(2)}, u32[]{:S(2)}) collective-permute-start(bf16[512,128]{1,0:T(8,128)(2,1)S(1)} %collective-permute-done.2), channel_id=1, source_target_pairs={{0,2},{2,4},{4,6},{6,8},{8,10},{10,12},{12,14},{14,0},{1,3},{3,5},... | collective-permute-start | bytes 393224 | tf_op jit(solution)/shard_map/ppermute | solution.py:222
  48.7 48.9 %copy-start.16 = (f32[512]{0:T(512)S(1)}, f32[512]{0:T(512)}, u32[]{:S(2)}) copy-start(f32[512]{0:T(512)} %param.30) | copy-start | bytes 6148
  48.7 40.5 %copy-start.9 = (s32[16,8,128]{2,1,0:T(8,128)}, s32[16,8,128]{2,1,0:T(8,128)S(1)}, u32[]{:S(2)}) copy-start(s32[16,8,128]{2,1,0:T(8,128)S(1)} %all-to-all-done) | copy-start | bytes 196612
  48.7 25.7 %all-to-all-start.3 = ((bf16[16,2,192,128]{3,2,1,0:T(8,128)(2,1)}), bf16[16,2,192,128]{3,2,1,0:T(8,128)(2,1)S(1)}, u32[]{:S(2)}, u32[]{:S(2)}) async-start(bf16[16,2,192,128]{3,2,1,0:T(8,128)(2,1)} %shard_map.206), calls=%async_computation.3 | async-start | bytes 3145728 | tf_op jit(solution)/shard_map/all_to_all | solution.py:285
  56.0 2.9 %collective-permute-start.7 = (bf16[8,512,128]{2,1,0:T(8,128)(2,1)S(1)}, bf16[8,512,128]{2,1,0:T(8,128)(2,1)}, u32[]{:S(2)}, u32[]{:S(2)}) collective-permute-start(bf16[8,512,128]{2,1,0:T(8,128)(2,1)S(1)} %bitcast_dynamic-update-slice_fusion.mine_ref), channel_id=1, source_target_pairs={{0,1},{1,0},{2,3},{3,2},{4,5},{5,4},{6,7},{7,6},{8,9},{9,8},{10,11... | collective-permute-start | bytes 3145736 | tf_op jit(solution)/shard_map/ppermute | solution.py:228
  65.3 0.9 copy-start.2
  74.4 14.7 %all-to-all-start.1 = ((bf16[16,192,128]{2,1,0:T(8,128)(2,1)}), bf16[16,192,128]{2,1,0:T(8,128)(2,1)S(1)}, u32[]{:S(2)}, u32[]{:S(2)}) async-start(bf16[16,192,128]{2,1,0:T(8,128)(2,1)} %get-tuple-element.11), calls=%async_computation.1 | async-start | bytes 1572864 | tf_op jit(solution)/shard_map/all_to_all | solution.py:270
  89.2 19.9 %all-to-all-start.2 = ((bf16[16,192,128]{2,1,0:T(8,128)(2,1)}), bf16[16,192,128]{2,1,0:T(8,128)(2,1)S(1)}, u32[]{:S(2)}, u32[]{:S(2)}) async-start(bf16[16,192,128]{2,1,0:T(8,128)(2,1)} %copy-done.2), calls=%async_computation.2 | async-start | bytes 1572864 | tf_op jit(solution)/shard_map/all_to_all | solution.py:270
  104.6 2.0 copy-start.1
  104.6 5.5 %copy-start.12 = (bf16[256,128]{1,0:T(8,128)(2,1)S(1)}, bf16[256,128]{1,0:T(8,128)(2,1)}, u32[]{:S(2)}) copy-start(bf16[256,128]{1,0:T(8,128)(2,1)} %fusion.8) | copy-start | bytes 196612
  104.6 5.5 %copy-start.15 = (f32[4096]{0:T(1024)S(1)}, f32[4096]{0:T(1024)}, u32[]{:S(2)}) copy-start(f32[4096]{0:T(1024)} %param.33) | copy-start | bytes 49156
  108.1 12.2 %collective-permute-start.8 = (f32[8,512,128]{2,1,0:T(8,128)}, f32[8,512,128]{2,1,0:T(8,128)}, u32[]{:S(2)}, u32[]{:S(2)}) collective-permute-start(f32[8,512,128]{2,1,0:T(8,128)} %dynamic-slice_bitcast_fusion), channel_id=1, source_target_pairs={{0,1},{1,0},{2,3},{3,2},{4,5},{5,4},{6,7},{7,6},{8,9},{9,8},{10,11... | collective-permute-start | bytes 6291464 | tf_op jit(solution)/shard_map/ppermute | solution.py:299
  114.4 1.2 copy-start.14
  114.4 1.2 copy-start.11
  119.8 9.4 %collective-permute-start.10 = (bf16[4096,320]{0,1:T(8,128)(2,1)}, bf16[4096,320]{0,1:T(8,128)(2,1)}, u32[]{:S(2)}, u32[]{:S(2)}) collective-permute-start(bf16[4096,320]{0,1:T(8,128)(2,1)} %convolution_convert_fusion), channel_id=1, source_target_pairs={{0,1},{1,0},{2,3},{3,2},{4,5},{5,4},{6,7},{7,6},{8,9},{9,8},{10,11... | collective-permute-start | bytes 7864328 | tf_op jit(solution)/shard_map/ppermute | solution.py:337
  123.8 34.5 %all-to-all-start.4 = ((bf16[8,512,128]{2,1,0:T(8,128)(2,1)}), bf16[8,512,128]{2,1,0:T(8,128)(2,1)}, u32[]{:S(2)}, u32[]{:S(2)}) async-start(bf16[8,512,128]{2,1,0:T(8,128)(2,1)} %fusion.2), calls=%async_computation.4 | async-start | bytes 2097152 | tf_op jit(solution)/shard_map/all_to_all | solution.py:300
  158.3 45.9 %all-to-all-start.5 = ((bf16[16,256,320]{1,2,0:T(8,128)(2,1)}), bf16[16,256,320]{1,2,0:T(8,128)(2,1)}, u32[]{:S(2)}, u32[]{:S(2)}) async-start(bf16[16,256,320]{1,2,0:T(8,128)(2,1)} %bitcast.74), calls=%async_computation.5 | async-start | bytes 5242880 | tf_op jit(solution)/shard_map/all_to_all | solution.py:340
  167.0 49.7 %collective-permute-start.9 = (f32[512,128]{1,0:T(8,128)S(1)}, f32[512,128]{1,0:T(8,128)}, u32[]{:S(2)}, u32[]{:S(2)}) collective-permute-start(f32[512,128]{1,0:T(8,128)S(1)} %convert_reduce_fusion), channel_id=1, source_target_pairs={{0,1},{1,0},{2,3},{3,2},{4,5},{5,4},{6,7},{7,6},{8,9},{9,8},{10,11... | collective-permute-start | bytes 786440 | tf_op jit(solution)/shard_map/ppermute | solution.py:302
  207.1 13.9 %all-to-all-start.6 = ((bf16[8,32,320]{2,1,0:T(8,128)(2,1)}), bf16[8,32,320]{2,1,0:T(8,128)(2,1)}, u32[]{:S(2)}, u32[]{:S(2)}) async-start(bf16[8,32,320]{2,1,0:T(8,128)(2,1)} %bitcast.25), calls=%async_computation.6 | async-start | bytes 393216 | tf_op jit(solution)/shard_map/all_to_all | solution.py:344
  211.2 5.5 %copy-start.8 = (f32[1024,128]{1,0:T(8,128)S(1)}, f32[1024,128]{1,0:T(8,128)}, u32[]{:S(2)}) copy-start(f32[1024,128]{1,0:T(8,128)} %param.27) | copy-start | bytes 1572868
  211.2 5.5 %copy-start.10 = (f32[1024,128]{1,0:T(8,128)S(1)}, f32[1024,128]{1,0:T(8,128)}, u32[]{:S(2)}) copy-start(f32[1024,128]{1,0:T(8,128)} %param.28) | copy-start | bytes 1572868
  214.7 7.2 %copy-start.13 = (f32[320,32]{0,1:T(8,128)S(1)}, f32[320,32]{0,1:T(8,128)}, u32[]{:S(2)}) copy-start(f32[320,32]{0,1:T(8,128)} %param.35) | copy-start | bytes 122884
  (3 other events, 2.1 us)

commit v2 on v1

v2 whole, which is shorter than its diff:
```python
import functools

import jax
import jax.numpy as jnp
from jax import lax
from jax.experimental import pallas as pl
from jax.experimental.pallas import tpu as pltpu
from jax.sharding import Mesh, PartitionSpec as P

FEATS = 4
CAP = 24
RING = 8
LEARN_RATE = 0.1
LOSS_SCALE = 64.0
LANES = 128
VMEM = 24 * 1024 * 1024
BF = jnp.bfloat16
F32 = jnp.float32
I32 = jnp.int32


def iota(shape, axis):
    return lax.broadcasted_iota(I32, shape, axis)


def ones_where(cond):
    return jnp.where(cond, 1.0, 0.0).astype(BF)


def mm(a, b):
    return jnp.dot(a, b, preferred_element_type=F32)


def call(body, out_shape, scratch=(), vmem=VMEM, **more):
    return pl.pallas_call(
        body,
        out_shape=out_shape,
        scratch_shapes=scratch,
        compiler_params=pltpu.CompilerParams(vmem_limit_bytes=vmem),
        **more,
    )


def nt(a, b):
    return lax.dot_general(a, b, (((1,), (1,)), ((), ())), preferred_element_type=F32)


def route_body(bag_count, *refs):
    lists, (high_ref, low_ref, bagpos_ref, pos_ref, bag_ref), (held, sems) = (
        refs[:6],
        refs[6:11],
        refs[11:],
    )
    copies = [pltpu.make_async_copy(ref, held.at[i], sems.at[i]) for i, ref in enumerate(lists)]
    for copy in copies:
        copy.start()
    for copy in copies:
        copy.wait()
    owner_ref, old_owner_ref, row_ref, old_row_ref, mask_ref, index_ref = [held.at[i] for i in range(6)]
    peers = high_ref.shape[0]
    length = pos_ref.shape[2]
    samples = bag_count // FEATS
    bags = index_ref[...]
    bag_ref[...] = jnp.where(mask_ref[...] > 0, (bags & (FEATS - 1)) * samples + (bags >> 2) + 1, 0)
    chunk = 256 if length % 256 == 0 else length
    upper = ones_where(iota((chunk, chunk), 0) <= iota((chunk, chunk), 1))
    zero = jnp.zeros((LANES, length), F32)
    high_total = jnp.zeros((peers, LANES), F32)
    low_total = jnp.zeros((peers, LANES), F32)
    bag_total = jnp.zeros((peers, LANES), F32)
    for turn in range(4):
        mb = turn % 2
        own = (owner_ref if turn < 2 else old_owner_ref)[mb]
        row = (row_ref if turn < 2 else old_row_ref)[mb] + 1
        hit = own == iota((peers, length), 0)
        onehot = ones_where(hit)
        carry = jnp.zeros((peers, 1), F32)
        parts = []
        for at in range(0, length, chunk):
            counted = mm(onehot[:, at : at + chunk], upper) + carry
            carry = counted[:, chunk - 1 :]
            parts.append(counted)
        counted = jnp.concatenate(parts, axis=1)
        rank = jnp.sum(jnp.where(hit, counted, 0.0), axis=0, keepdims=True).astype(I32) - 1
        place = iota((LANES, length), 0) == rank + turn * CAP

        def spread(value):
            high = jnp.where(place, (value >> 5).astype(F32), zero).astype(BF)
            low = jnp.where(place, (value & 31).astype(F32), zero).astype(BF)
            return nt(onehot, high), nt(onehot, low)

        high, low = spread(row)
        high_total += high
        low_total += low
        if turn < 2:
            high, low = spread(bag_ref[mb])
            bag_total += high * 32.0 + low
        else:
            pos_ref[mb] = own * CAP + rank
    high_ref[...] = high_total
    low_ref[...] = low_total
    bagpos_ref[...] = bag_total.astype(I32) - 1


def gather_body(z_ref, asked_ref, *refs):
    pairs = (len(refs) - 8) // 3
    ring = 2 * pairs + 2
    halves, passed = refs[:2], refs[2 : 2 + 2 * pairs]
    swapped, far_ref = refs[2 + 2 * pairs : 2 + 3 * pairs], refs[2 + 3 * pairs]
    out_ref, wanted_ref, cols_ref, hot_ref, req_ref = refs[-5:]
    groups = out_ref.shape[0]
    half = halves[0].shape[0]
    both = 2 * CAP
    for w in range(groups):
        rows = asked_ref[w].astype(F32)
        row = (rows[:ring] * 32.0 + rows[8 : 8 + ring]).astype(I32) - 1
        req_ref[w * ring : (w + 1) * ring, :] = jnp.where(row >= 0, row ^ z_ref[1], -1)
    wanted_ref[...] = req_ref[...]
    for z in range(ring):
        part = req_ref[pl.ds(z, groups, stride=ring), :]
        part = jnp.concatenate([part, jnp.zeros((LANES - groups, LANES), I32)], axis=0)
        cols_ref[z] = part.T
    me = z_ref[0]
    for offset in range(ring):
        z = lax.rem(me - offset + ring, ring)
        cols = cols_ref[z]
        for w in range(groups):
            hot_ref[w * both : (w + 1) * both, :] = ones_where(
                cols[:both, w : w + 1] == iota((both, 2 * half), 1)
            )
        if offset == 0:
            mine, other = halves[0][...], halves[1][...]
        elif offset == ring // 2:
            mine, other = far_ref[0], far_ref[1]
        else:
            at, way = (offset - 1, 0) if offset < ring // 2 else (ring - offset - 1, 1)
            mine, other = passed[2 * at + way][...], swapped[at][way]
        found = mm(hot_ref[:, :half], mine) + mm(hot_ref[:, half:], other)
        out_ref[:, z] = found.reshape(groups, both, LANES).astype(BF)


def pool_body(bagpos_ref, reply_ref, out_ref):
    groups, ring, both, width = reply_ref.shape
    samples = out_ref.shape[0] // 2
    bags = samples * FEATS
    slots = groups * ring * CAP
    size = slots // 8
    wide = reply_ref[...].astype(F32)
    for mb in range(2):
        flat = wide[:, :, mb * CAP : (mb + 1) * CAP, :].reshape(slots, width).astype(BF)
        total = jnp.zeros((bags, width), F32)
        for at in range(0, slots, size):
            hot = ones_where(bagpos_ref[mb, :, at : at + size] == iota((bags, size), 0))
            total += mm(hot, flat[at : at + size])
        for feat in range(FEATS):
            out_ref[mb * samples : (mb + 1) * samples, feat * width : (feat + 1) * width] = total[
                feat * samples : (feat + 1) * samples
            ].astype(BF)


def tie_body(*refs):
    del refs


def tie(value, *after):
    anywhere = pl.BlockSpec(memory_space=pl.ANY)
    return call(
        tie_body,
        vmem=1024 * 1024,
        out_shape=jax.ShapeDtypeStruct(value.shape, value.dtype),
        in_specs=[anywhere] * (1 + len(after)),
        out_specs=anywhere,
        input_output_aliases={0: 0},
    )(value, *after)


def outgoing_body(pos_ref, grad_ref, high_ref, low_ref, *refs):
    out_ref = refs[-1]
    here, rows, width = out_ref.shape
    ring = high_ref.shape[0] // here
    per = ring * CAP
    length = pos_ref.shape[2]
    first = pl.program_id(0) * here * per
    pad = [jnp.zeros((8 - ring, width), F32)] if ring < 8 else []
    for w in range(here):
        placed = []
        for mb in range(2):
            hot = ones_where(pos_ref[mb] - first == iota((per, length), 0) + w * per)
            placed.append(mm(hot, grad_ref[mb]).reshape(ring, CAP, width))
        out_ref[w, : rows - 16] = jnp.concatenate(placed, axis=1).reshape(rows - 16, width).astype(BF)
        mine = slice(w * ring, (w + 1) * ring)
        out_ref[w, rows - 16 :] = jnp.concatenate(
            [high_ref[mine]] + pad + [low_ref[mine]] + pad, axis=0
        ).astype(BF)


def scatter_body(at_ref, rows_ref, grad_ref, *refs):
    ring = rows_ref.shape[0]
    groups, _, width = grad_ref.shape
    both = 2 * CAP
    out_ref = refs[-1]
    half = out_ref.shape[1]
    count = groups * both
    for offset in range(ring):
        z = lax.rem(at_ref[0] + offset, ring)
        part = grad_ref[:, pl.ds(pl.multiple_of(z * both, both), both), :].reshape(count, width)
        sums = mm(ones_where(rows_ref[z] == iota((half, count), 0) + at_ref[1]), part)
        if len(refs) > 2:
            sums += refs[0][offset]
        out_ref[offset] = sums.astype(out_ref.dtype)


def outer_body(part_ref, delta_ref, *refs):
    out_ref = refs[-1]
    units = out_ref.shape[2]
    product = lax.dot_general(
        part_ref[...], delta_ref[...], (((0,), (0,)), ((), ())), preferred_element_type=F32
    )
    for w in range(out_ref.shape[0]):
        block = product[:, w * units : (w + 1) * units]
        if len(refs) > 1:
            block += refs[0][w].astype(F32)
        out_ref[w] = block.astype(BF)


def pick_body(bag_ref, back_ref, out_ref):
    samples = back_ref.shape[0] // 2
    bags = samples * FEATS
    length = bag_ref.shape[2]
    width = back_ref.shape[1] // FEATS
    for mb in range(2):
        rows = back_ref[mb * samples : (mb + 1) * samples, :]
        grads = jnp.concatenate(
            [rows[:, feat * width : (feat + 1) * width] for feat in range(FEATS)], axis=0
        ).astype(BF)
        for at in range(0, length, LANES):
            ids = jnp.broadcast_to(bag_ref[mb, :, at : at + LANES] - 1, (LANES, LANES)).T
            hot = jnp.concatenate(
                [ones_where(ids == iota((LANES, LANES), 1) + block) for block in range(0, bags, LANES)],
                axis=1,
            )
            out_ref[mb, 0, at : at + LANES, :] = mm(hot, grads).astype(BF)


def shape_of(shape, dtype):
    return jax.ShapeDtypeStruct(shape, dtype)


def ring_of(size, shift):
    return [(i, (i + shift) % size) for i in range(size)]


def per_device(
    dense_input,
    id_owner,
    id_row,
    id_mask,
    bag_index,
    labels,
    stale_owner,
    stale_row,
    stale_grad,
    emb_table,
    grad_squares,
    bottom_first,
    bottom_bias,
    bottom_second,
    top_weight,
    top_bias,
    out_weight,
    top_squares,
):
    groups = lax.axis_size("w")
    ring = lax.axis_size("z")
    peers = groups * ring
    core = lax.axis_index("nn")
    my_z = lax.axis_index("z")
    swap = [(0, 1), (1, 0)]
    length = id_row.shape[2]
    width = emb_table.shape[1]
    table_rows = emb_table.shape[0]
    half_rows = table_rows // 2
    samples = dense_input.shape[1]

    my_half = lax.dynamic_slice_in_dim(emb_table, core * half_rows, half_rows, 0).astype(BF)
    other_half = lax.dynamic_slice_in_dim(emb_table, (1 - core) * half_rows, half_rows, 0).astype(BF)
    rounds = []
    ahead, back = my_half, my_half
    for _ in range(1, ring // 2):
        ahead = lax.ppermute(ahead, "z", ring_of(ring, 1))
        back = lax.ppermute(back, "z", ring_of(ring, -1))
        rounds.append((ahead, back))
    swapped = [lax.ppermute(jnp.stack(blocks), "nn", swap) for blocks in rounds]
    far = jnp.stack([ahead, swapped[-1][0] if swapped else other_half])
    far = lax.ppermute(far, "z", ring_of(ring, 1))

    anywhere = pl.BlockSpec(memory_space=pl.ANY)
    high, low, bagpos, old_pos, bag_or_none = call(
        functools.partial(route_body, samples * FEATS),
        (
            shape_of((peers, LANES), F32),
            shape_of((peers, LANES), F32),
            shape_of((peers, LANES), I32),
            shape_of((2, 1, length), I32),
            shape_of((2, 1, length), I32),
        ),
        (pltpu.VMEM((6, 2, 1, length), I32), pltpu.SemaphoreType.DMA((6,))),
        in_specs=[anywhere] * 6,
    )(
        id_owner.reshape(2, 1, length),
        stale_owner.reshape(2, 1, length),
        id_row,
        stale_row,
        id_mask,
        bag_index,
    )
    bag_rows = (
        bagpos[:, : 2 * CAP].reshape(peers, 2, CAP).transpose(1, 0, 2).reshape(2, 1, peers * CAP)
    )

    cut = 4
    rows = ring * 2 * CAP + 16
    square = pl.BlockSpec((peers // cut, LANES), lambda i: (i, 0))
    outgoing = call(
        outgoing_body,
        shape_of((groups, rows, width), BF),
        grid=(cut,),
        in_specs=[
            pl.BlockSpec((2, 1, length), lambda i: (0, 0, 0)),
            pl.BlockSpec((2, length, width), lambda i: (0, 0, 0)),
            square,
            square,
        ]
        + [anywhere] * 2,
        out_specs=pl.BlockSpec((groups // cut, rows, width), lambda i: (i, 0, 0)),
    )(old_pos, stale_grad.reshape(2, length, width), high, low, *(rounds[0] if rounds else (my_half, my_half)))
    if len(rounds) > 1:
        outgoing = tie(outgoing, *rounds[1])
    incoming = lax.all_to_all(outgoing, "w", split_axis=0, concat_axis=0, tiled=True)

    others = [my_half, other_half, *(block for blocks in rounds for block in blocks), *swapped, far]
    replies, wanted = call(
        gather_body,
        (
            shape_of((groups, ring, 2 * CAP, width), BF),
            shape_of((peers, LANES), I32),
        ),
        (
            pltpu.VMEM((ring, LANES, LANES), I32),
            pltpu.VMEM((groups * 2 * CAP, table_rows), BF),
            pltpu.VMEM((peers, LANES), I32),
        ),
        grid=(1,),
        in_specs=[
            pl.BlockSpec(memory_space=pltpu.SMEM),
            pl.BlockSpec((groups, 16, width), lambda i: (0, rows // 16 - 1, 0)),
        ]
        + [pl.BlockSpec(x.shape, lambda i, n=x.ndim: (0,) * n) for x in others],
        out_specs=(
            pl.BlockSpec((groups, ring, 2 * CAP, width), lambda i: (0, 0, 0, 0)),
            pl.BlockSpec((peers, LANES), lambda i: (0, 0)),
        ),
    )(jnp.stack([my_z, core * half_rows]), incoming, *others)
    here_replies = lax.all_to_all(replies, "w", split_axis=0, concat_axis=0, tiled=True)
    old_rows = (
        wanted[:, 2 * CAP : 4 * CAP]
        .reshape(groups, ring, 2 * CAP)
        .transpose(1, 0, 2)
        .reshape(ring, 1, groups * 2 * CAP)
    )

    def scatter(first, dtype, *more):
        return call(
            scatter_body,
            shape_of((ring, half_rows, width), dtype),
            in_specs=[pl.BlockSpec(memory_space=pltpu.SMEM)]
            + [pl.BlockSpec()] * (2 + len(more))
            + [anywhere],
        )(jnp.stack([my_z, jnp.full((), first, I32)]), old_rows, incoming, *more, replies)

    theirs = lax.ppermute(scatter(half_rows, F32), "nn", swap)
    ours = scatter(0, BF, theirs)
    pooled = call(
        pool_body,
        shape_of((2 * samples, FEATS * width), BF),
    )(bag_rows, here_replies)

    dense_rows = dense_input.reshape(2 * samples, dense_input.shape[2])
    label_rows = labels.reshape(2 * samples)
    hidden = jax.nn.relu(mm(dense_rows, bottom_first) + bottom_bias).astype(BF)
    bottom = jax.nn.relu(mm(hidden, bottom_second)).astype(BF)
    joined = jnp.concatenate([bottom, pooled], axis=1)
    before = mm(joined, top_weight) + top_bias
    gate = jax.nn.sigmoid(before)
    active = (before * gate).astype(BF)
    logits = mm(active, out_weight)
    logit_grad = LOSS_SCALE * (jax.nn.sigmoid(logits) - label_rows.astype(F32))
    top_delta = (
        logit_grad[:, None]
        * out_weight.astype(F32)[None, :]
        * gate
        * (1.0 + before * (1.0 - gate))
    ).astype(BF)
    split_at = bottom.shape[1]
    back_grad = nt(top_delta, top_weight[split_at:])
    row_grads = call(pick_body, shape_of((2, 1, length, width), BF))(bag_or_none, back_grad)

    inputs = joined.shape[1] // 2
    units = top_delta.shape[1] // peers

    def outer(at, *more):
        here = groups // 4
        wide = ring * units
        block = pl.BlockSpec((here, inputs, wide), lambda i: (i, 0, 0))
        return call(
            outer_body,
            shape_of((groups, inputs, wide), BF),
            grid=(4,),
            in_specs=[
                pl.BlockSpec((2 * samples, inputs), lambda i: (0, 0)),
                pl.BlockSpec((2 * samples, here * wide), lambda i: (0, i)),
            ]
            + [block] * len(more),
            out_specs=block,
        )(lax.dynamic_slice_in_dim(joined, at * inputs, inputs, 1), top_delta, *more)

    unit_part = outer(core, lax.ppermute(outer(1 - core), "nn", swap))
    ours = tie(ours, unit_part)
    unit_part = lax.all_to_all(unit_part, "w", split_axis=0, concat_axis=0, tiled=True)

    arrived = [lax.ppermute(ours[shift], "z", ring_of(ring, shift)) for shift in range(1, ring)]
    arrived[0] = tie(arrived[0], row_grads)
    half_sum = ours[0].astype(F32)
    for part in arrived:
        half_sum += part.astype(F32)
    theirs = lax.ppermute(half_sum, "nn", swap)
    row_sum = jnp.where(
        core == 0,
        jnp.concatenate([half_sum, theirs], axis=0),
        jnp.concatenate([theirs, half_sum], axis=0),
    )
    new_squares = grad_squares + row_sum * row_sum
    new_table = emb_table - LEARN_RATE * row_sum * lax.rsqrt(new_squares)

    unit_part = jnp.sum(unit_part.astype(F32), axis=0).T.astype(BF).reshape(ring, units, inputs)
    unit_part = tie(unit_part, row_grads, new_table)
    unit_part = lax.all_to_all(unit_part, "z", split_axis=0, concat_axis=0, tiled=True)
    top_grad = jnp.sum(unit_part.astype(F32), axis=0).T
    top_step = top_grad * lax.rsqrt(top_squares + top_grad * top_grad)
    return (row_grads, new_table, new_squares, top_step)


def solution(mesh, ring=RING):
    devices = mesh.devices
    fine = Mesh(devices.reshape(devices.shape[0] // ring, ring, devices.shape[1]), ("w", "z", "nn"))
    rows = ("w", "z", "nn")
    emb = ("w", "z")
    return jax.shard_map(
        per_device,
        mesh=fine,
        in_specs=(
            P(None, rows, None),
            P(None, rows, None),
            P(None, rows, None),
            P(None, rows, None),
            P(None, rows, None),
            P(None, rows),
            P(None, rows, None),
            P(None, rows, None),
            P(None, rows, None, None),
            P(emb, None),
            P(emb, None),
            P(),
            P(),
            P(),
            P(),
            P(),
            P(),
            P("nn", emb),
        ),
        out_specs=(
            P(None, rows, None, None),
            P(emb, None),
            P(emb, None),
            P("nn", emb),
        ),
        check_vma=False,
    )
```

time: 224 us -> 181 us (0.81)
  waiting for transfers between devices: 96 us -> 53.3 us
  blocking collectives: 0 us -> 12.6 us
  Pallas kernels: 24.6 us -> 33.2 us
  starting transfers between devices: 56 us -> 47.8 us
  other arithmetic: 14.5 us -> 8.71 us
  matrix products: 16.2 us -> 10.6 us
    all_to_all x6 -> x2, waiting for transfers between devices: 73 us -> 24.4 us  [the longest x1 17.6 us: per_device(): lax.all_to_all(replies, 'w', split_axis=0, concat_axis=0, tiled=True)]
    all_to_all x6 -> x2, starting transfers between devices: 35.3 us -> 13.8 us  [the longest x1 7.23 us: per_device(): lax.all_to_all(replies, 'w', split_axis=0, concat_axis=0, tiled=True)]
    ppermute x4 -> x14, waiting for transfers between devices: 2.76 us -> 20 us  [the longest x1 9.12 us: per_device(): far = lax.ppermute(far, 'z', ring_of(ring, 1))]
    ppermute x4 -> x14, starting transfers between devices: 0.91 us -> 13.7 us  [the longest x7 12.5 us: per_device(): lax.ppermute(ours[shift], 'z', ring_of(ring, shift))]
    all_to_all x0 -> x1, blocking collectives: none -> 12.6 us  [per_device(): lax.all_to_all(unit_part, 'z', split_axis=0, concat_axis=0, tiled=True)]
    pallas_call x7 -> x13, Pallas kernels: 24.6 us -> 33.2 us  [the longest x2 7.23 us: scatter(): call(scatter_body, shape_of((ring, half_rows, width), dtype), in_specs=[p...]
    ppermute x4 -> x3, waiting for transfers between devices: 12 us -> 3.66 us  [per_device(): ahead = lax.ppermute(ahead, 'z', ring_of(ring, 1))]
    all_to_all x1, waiting for transfers between devices: 8.18 us -> 0.01 us  [per_device(): lax.all_to_all(outgoing, 'w', split_axis=0, concat_axis=0, tiled=True)]
  transfers between devices with their start and end apart: 18 -> 23, of which waited for: 9 -> 13; matrix products, arithmetic and copies ran while one was open for 16% -> 7% of each run, Pallas kernels for 11% -> 12%
where the time goes in v2:
time: 181 us
  waiting for transfers between devices  53.3 us (29%)
  starting transfers between devices  47.8 us (26%)
  Pallas kernels  33.2 us (18%)
  local copies, waits for them, and re-layouts  13.4 us (7%)
  blocking collectives  12.6 us (7%)
  matrix products  10.6 us (6%)
  other arithmetic  8.71 us (5%)
    all_to_all x1, waiting for transfers between devices, per_device(): lax.all_to_all(replies, 'w', split_axis=0, concat_axis=0, tiled=True)  17.6 us
    ppermute x3, starting transfers between devices, per_device(): back = lax.ppermute(back, 'z', ring_of(ring, -1))  12.9 us
    all_to_all x1, blocking collectives, per_device(): lax.all_to_all(unit_part, 'z', split_axis=0, concat_axis=0, tiled=True)  12.6 us
    ppermute x7, starting transfers between devices, per_device(): lax.ppermute(ours[shift], 'z', ring_of(ring, shift))  12.5 us
    unnamed x47, local copies, waits for them, and re-layouts  10 us
    ppermute x1, waiting for transfers between devices, per_device(): far = lax.ppermute(far, 'z', ring_of(ring, 1))  9.12 us
    ppermute x7, waiting for transfers between devices, per_device(): lax.ppermute(ours[shift], 'z', ring_of(ring, shift))  7.47 us
    all_to_all x1, starting transfers between devices, per_device(): lax.all_to_all(outgoing, 'w', split_axis=0, concat_axis=0, tiled=True)  7.41 us
  transfers between devices with their start and end apart: 23, of which 13 were waited for; matrix products, arithmetic and copies ran while one was open for 7% of the time, Pallas kernels for 12%

profile of v2, /device:TPU:8, one launch (start us, length us, event | category | flops | bytes accessed | tf_op | source)
XLA Modules:
  0.0 180.5 jit_solution(1625657082344977928)
XLA Ops:
  1.8 5.9 %collective-permute-start.1 = (bf16[512,128]{1,0:T(8,128)(2,1)S(1)}, bf16[512,128]{1,0:T(8,128)(2,1)S(1)}, u32[]{:S(2)}, u32[]{:S(2)}) collective-permute-start(bf16[512,128]{1,0:T(8,128)(2,1)S(1)} %get-tuple-element.28.refs_0_), channel_id=1, source_target_pairs={{0,14},{2,0},{4,2},{6,4},{8,6},{10,8},{12,10},{14,12},{1,15},{3,1}... | collective-permute-start | bytes 393224 | tf_op jit(solution)/shard_map/ppermute | solution.py:291
  7.7 2.8 %collective-permute-done.1.refs_1_.refs_3_ = bf16[512,128]{1,0:T(8,128)(2,1)S(1)} collective-permute-done((bf16[512,128]{1,0:T(8,128)(2,1)S(1)}, bf16[512,128]{1,0:T(8,128)(2,1)S(1)}, u32[]{:S(2)}, u32[]{:S(2)}) %collective-permute-start.1) | collective-permute-done | bytes 131104 | tf_op jit(solution)/shard_map/ppermute | solution.py:291
  10.4 3.7 %collective-permute-start.3 = (bf16[512,128]{1,0:T(8,128)(2,1)S(1)}, bf16[512,128]{1,0:T(8,128)(2,1)S(1)}, u32[]{:S(2)}, u32[]{:S(2)}) collective-permute-start(bf16[512,128]{1,0:T(8,128)(2,1)S(1)} %collective-permute-done.1.refs_1_.refs_3_), channel_id=1, source_target_pairs={{0,14},{2,0},{4,2},{6,4},{8,6},{10,8},{12,10},{14,12},{1,15},{3,1}... | collective-permute-start | bytes 393224 | tf_op jit(solution)/shard_map/ppermute | solution.py:291
  18.4 3.5 %shard_map.201 = (f32[128,128]{1,0:T(8,128)S(1)}, f32[128,128]{1,0:T(8,128)S(1)}, s32[128,128]{1,0:T(8,128)S(1)}, s32[2,1,1536]{2,1,0:T(1,128)S(1)}, s32[2,1,1536]{2,1,0:T(1,128)S(1)}) custom-call(s32[2,1,1536]{2,1,0:T(1,128)S(1)} %bitcast.72, s32[2,1,1536]{2,1,0:T(1,128)S(1)} %bitcast.73, s32[2,1,1536]{2,1,0:T(1,128)S(1)} %copy-done.12, ...), custom_call_target="tpu_custom_call" | custom-call | tf_op jit(solution)/shard_map/pallas_call | solution.py:298
  23.0 6.3 %shard_map.202.refs_0_ = bf16[16,400,128]{2,1,0:T(8,128)(2,1)} custom-call(s32[2,1,1536]{2,1,0:T(1,128)S(1)} %get-tuple-element.13.pos_ref, bf16[2,1536,128]{2,1,0:T(8,128)(2,1)S(1)} %bitcast.69, f32[128,128]{1,0:T(8,128)S(1)} %get-tuple-element.14.high_ref, f32[128,128]{1,0:T(8,128)S(1)} %get-tuple-element.15.low_ref, ...), custom_call_target="tpu_custom_call" | custom-call | tf_op jit(solution)/shard_map/pallas_call | solution.py:324
  29.3 7.4 %all-to-all-start = ((bf16[16,400,128]{2,1,0:T(8,128)(2,1)}), bf16[16,400,128]{2,1,0:T(8,128)(2,1)S(1)}, u32[]{:S(2)}, u32[]{:S(2)}) async-start(bf16[16,400,128]{2,1,0:T(8,128)(2,1)} %shard_map.203), calls=%async_computation | async-start | bytes 3276800 | tf_op jit(solution)/shard_map/all_to_all | solution.py:339
  36.7 3.2 %collective-permute-start.5 = (bf16[512,128]{1,0:T(8,128)(2,1)S(1)}, bf16[512,128]{1,0:T(8,128)(2,1)S(1)}, u32[]{:S(2)}, u32[]{:S(2)}) collective-permute-start(bf16[512,128]{1,0:T(8,128)(2,1)S(1)} %collective-permute-done.3.refs_2_.refs_5_), channel_id=1, source_target_pairs={{0,14},{2,0},{4,2},{6,4},{8,6},{10,8},{12,10},{14,12},{1,15},{3,1}... | collective-permute-start | bytes 393224 | tf_op jit(solution)/shard_map/ppermute | solution.py:291
  40.0 2.5 %collective-permute-done.5.refs_7_ = bf16[512,128]{1,0:T(8,128)(2,1)S(1)} collective-permute-done((bf16[512,128]{1,0:T(8,128)(2,1)S(1)}, bf16[512,128]{1,0:T(8,128)(2,1)S(1)}, u32[]{:S(2)}, u32[]{:S(2)}) %collective-permute-start.5) | collective-permute-done | bytes 131104 | tf_op jit(solution)/shard_map/ppermute | solution.py:291
  42.5 3.7 %collective-permute-done.4.refs_6_ = bf16[512,128]{1,0:T(8,128)(2,1)S(1)} collective-permute-done((bf16[512,128]{1,0:T(8,128)(2,1)S(1)}, bf16[512,128]{1,0:T(8,128)(2,1)S(1)}, u32[]{:S(2)}, u32[]{:S(2)}) %collective-permute-start.4) | collective-permute-done | bytes 131104 | tf_op jit(solution)/shard_map/ppermute | solution.py:290
  50.1 9.1 %collective-permute-done.9.refs_11_ = bf16[2,512,128]{2,1,0:T(8,128)(2,1)} collective-permute-done((bf16[2,512,128]{2,1,0:T(8,128)(2,1)}, bf16[2,512,128]{2,1,0:T(8,128)(2,1)}, u32[]{:S(2)}, u32[]{:S(2)}) %collective-permute-start.9) | collective-permute-done | bytes 262176 | tf_op jit(solution)/shard_map/ppermute | solution.py:295
  59.2 6.1 %shard_map.204 = (bf16[16,8,48,128]{3,2,1,0:T(8,128)(2,1)}, s32[128,128]{1,0:T(8,128)S(1)}) custom-call(s32[2]{0:T(128)S(1)} %get-tuple-element.31.z_ref, bf16[16,400,128]{2,1,0:T(8,128)(2,1)S(1)} %all-to-all-done.asked_ref.grad_ref, bf16[512,128]{1,0:T(8,128)(2,1)S(1)} %get-tuple-element.28.refs_0_, bf16[512,128]{1,0:T(8,128)(2,1)S(1)} %get-tuple-element.27.refs_1_, ...), custom_call_target="tpu_custom_call" | custom-call | tf_op jit(solution)/shard_map/pallas_call | solution.py:342
  65.3 7.2 %all-to-all-start.1 = ((bf16[16,8,48,128]{3,2,1,0:T(8,128)(2,1)}), bf16[16,8,48,128]{3,2,1,0:T(8,128)(2,1)S(1)}, u32[]{:S(2)}, u32[]{:S(2)}) async-start(bf16[16,8,48,128]{3,2,1,0:T(8,128)(2,1)} %get-tuple-element.16.refs_0_.refs_1_), calls=%async_computation.1 | async-start | bytes 3145728 | tf_op jit(solution)/shard_map/all_to_all | solution.py:364
  76.9 17.6 %all-to-all-done.1.reply_ref = bf16[16,8,48,128]{3,2,1,0:T(8,128)(2,1)S(1)} async-done(((bf16[16,8,48,128]{3,2,1,0:T(8,128)(2,1)}), bf16[16,8,48,128]{3,2,1,0:T(8,128)(2,1)S(1)}, u32[]{:S(2)}, u32[]{:S(2)}) %all-to-all-start.1) | async-done | bytes 1572896 | tf_op jit(solution)/shard_map/all_to_all | solution.py:364
  94.6 1.8 shard_map.205
  96.6 4.3 %convolution_add_fusion = f32[256,4096]{1,0:T(8,128)S(1)} fusion(bf16[640,4096]{1,0:T(8,128)(2,1)} %param.32, f32[4096]{0:T(1024)} %param.33, bf16[256,128]{1,0:T(8,128)(2,1)S(1)} %fusion.7, bf16[256,512]{1,0:T(8,128)(2,1)S(1)} %shard_map.205), kind=kOutput, calls=%fused_computation | convolution fusion | flops 1343881216 | bytes 9781248 | tf_op jit(solution)/shard_map/dot_general | solution.py:31
  102.2 1.7 multiply_convert_fusion.delta_ref
  103.9 2.9 %shard_map.209 = bf16[16,320,256]{2,1,0:T(8,128)(2,1)} custom-call(bf16[256,320]{1,0:T(8,128)(2,1)S(1)} %get-tuple-element.29.part_ref, bf16[256,4096]{1,0:T(8,128)(2,1)S(1)} %multiply_convert_fusion.delta_ref), custom_call_target="tpu_custom_call" | custom-call | tf_op jit(solution)/shard_map/pallas_call | solution.py:415
  108.3 3.7 %shard_map.207 = f32[8,512,128]{2,1,0:T(8,128)} custom-call(s32[2]{0:T(128)S(1)} %get-tuple-element.32.at_ref, s32[8,1,768]{2,1,0:T(1,128)S(1)} %reshape.50.rows_ref, bf16[16,400,128]{2,1,0:T(8,128)(2,1)S(1)} %all-to-all-done.asked_ref.grad_ref, bf16[16,8,48,128]{3,2,1,0:T(8,128)(2,1)} %get-tuple-element.16.refs_0_.refs_1_), custom_call_target="tpu_custom_call" | custom-call | tf_op jit(solution)/shard_map/pallas_call | solution.py:373
  113.3 3.4 %shard_map.210.refs_1_ = bf16[16,320,256]{2,1,0:T(8,128)(2,1)S(1)} custom-call(bf16[256,320]{1,0:T(8,128)(2,1)S(1)} %get-tuple-element.30.part_ref, bf16[256,4096]{1,0:T(8,128)(2,1)S(1)} %copy-done.4, bf16[16,320,256]{2,1,0:T(8,128)(2,1)} %collective-permute-done.11.refs_0_), custom_call_target="tpu_custom_call" | custom-call | tf_op jit(solution)/shard_map/pallas_call | solution.py:415
  116.8 1.5 copy-done.1
  118.3 6.6 %all-to-all-start.2 = ((bf16[16,320,256]{2,1,0:T(8,128)(2,1)}), bf16[16,320,256]{2,1,0:T(8,128)(2,1)}, u32[]{:S(2)}, u32[]{:S(2)}) async-start(bf16[16,320,256]{2,1,0:T(8,128)(2,1)} %copy-done.1), calls=%async_computation.2 | async-start | bytes 5242880 | tf_op jit(solution)/shard_map/all_to_all | solution.py:429
  125.0 3.6 %shard_map.208.refs_0_ = bf16[8,512,128]{2,1,0:T(8,128)(2,1)S(1)} custom-call(s32[2]{0:T(128)S(1)} %pad_add_fusion.1.at_ref, s32[8,1,768]{2,1,0:T(1,128)S(1)} %reshape.50.rows_ref, bf16[16,400,128]{2,1,0:T(8,128)(2,1)S(1)} %all-to-all-done.asked_ref.grad_ref, f32[8,512,128]{2,1,0:T(8,128)} %collective-permute-done.10.refs_0_, ...), custom_call_target="tpu_custom_call" | custom-call | tf_op jit(solution)/shard_map/pallas_call | solution.py:373
  128.7 3.2 %collective-permute-start.18 = (bf16[512,128]{1,0:T(8,128)(2,1)S(1)}, bf16[512,128]{1,0:T(8,128)(2,1)S(1)}, u32[]{:S(2)}, u32[]{:S(2)}) collective-permute-start(bf16[512,128]{1,0:T(8,128)(2,1)S(1)} %get-tuple-element.21), channel_id=1, source_target_pairs={{0,14},{2,0},{4,2},{6,4},{8,6},{10,8},{12,10},{14,12},{1,15},{3,1}... | collective-permute-start | bytes 393224 | tf_op jit(solution)/shard_map/ppermute | solution.py:431
  132.0 1.6 collective-permute-start.16
  133.6 4.3 %collective-permute-start.15 = (bf16[512,128]{1,0:T(8,128)(2,1)S(1)}, bf16[512,128]{1,0:T(8,128)(2,1)S(1)}, u32[]{:S(2)}, u32[]{:S(2)}) collective-permute-start(bf16[512,128]{1,0:T(8,128)(2,1)S(1)} %get-tuple-element.24), channel_id=1, source_target_pairs={{0,8},{2,10},{4,12},{6,14},{8,0},{10,2},{12,4},{14,6},{1,9},{3,11}... | collective-permute-start | bytes 393224 | tf_op jit(solution)/shard_map/ppermute | solution.py:431
  138.3 3.2 %collective-permute-start.13 = (bf16[512,128]{1,0:T(8,128)(2,1)S(1)}, bf16[512,128]{1,0:T(8,128)(2,1)S(1)}, u32[]{:S(2)}, u32[]{:S(2)}) collective-permute-start(bf16[512,128]{1,0:T(8,128)(2,1)S(1)} %get-tuple-element.26), channel_id=1, source_target_pairs={{0,4},{2,6},{4,8},{6,10},{8,12},{10,14},{12,0},{14,2},{1,5},{3,7},... | collective-permute-start | bytes 393224 | tf_op jit(solution)/shard_map/ppermute | solution.py:431
  141.5 3.8 %fusion.back_ref = f32[256,512]{1,0:T(8,128)S(1)} fusion(bf16[256,4096]{1,0:T(8,128)(2,1)S(1)} %copy-done.5, bf16[640,4096]{1,0:T(8,128)(2,1)} %param.32), kind=kOutput, calls=%fused_computation.1 | convolution fusion | flops 1073741824 | bytes 6815744 | tf_op jit(solution)/shard_map/dot_general | solution.py:45
  145.4 1.9 %shard_map.206.refs_1_ = bf16[2,1,1536,128]{3,2,1,0:T(8,128)(2,1)} custom-call(s32[2,1,1536]{2,1,0:T(1,128)S(1)} %get-tuple-element.11.bag_ref, f32[256,512]{1,0:T(8,128)S(1)} %fusion.back_ref), custom_call_target="tpu_custom_call" | custom-call | tf_op jit(solution)/shard_map/pallas_call | solution.py:406
  148.4 5.7 %collective-permute-done.16 = bf16[512,128]{1,0:T(8,128)(2,1)S(1)} collective-permute-done((bf16[512,128]{1,0:T(8,128)(2,1)S(1)}, bf16[512,128]{1,0:T(8,128)(2,1)S(1)}, u32[]{:S(2)}, u32[]{:S(2)}) %collective-permute-start.16) | collective-permute-done | bytes 131104 | tf_op jit(solution)/shard_map/ppermute | solution.py:431
  158.2 6.7 %all-to-all-done.2 = bf16[16,320,256]{2,1,0:T(8,128)(2,1)} async-done(((bf16[16,320,256]{2,1,0:T(8,128)(2,1)}), bf16[16,320,256]{2,1,0:T(8,128)(2,1)}, u32[]{:S(2)}, u32[]{:S(2)}) %all-to-all-start.2) | async-done | bytes 2621472 | tf_op jit(solution)/shard_map/all_to_all | solution.py:429
  164.9 2.1 %reduce_sum.21 = bf16[320,256]{1,0:T(8,128)(2,1)S(1)} reduce(bf16[16,320,256]{2,1,0:T(8,128)(2,1)} %all-to-all-done.2, bf16[]{:T(256)} %constant.38.clone.1), dimensions={0}, to_apply=%region_0.1 | reduce | flops 1228800 | bytes 2785282 | tf_op jit(solution)/shard_map/reduce_sum | solution.py:445
  167.2 12.6 %all_to_all.20 = bf16[8,32,320]{2,1,0:T(8,128)(2,1)S(1)} all-to-all(bf16[8,32,320]{2,1,0:T(8,128)(2,1)S(1)} %shard_map.213), channel_id=1, replica_groups=mesh['w'=16,'z'=8,'nn'=2] {'z'}, dimensions={0} | all-to-all | bytes 327680 | tf_op jit(solution)/shard_map/all_to_all | solution.py:447
  (104 shorter events, 25.8 us)
Async XLA Ops:
  0.6 75.0 %copy-start = (bf16[512,128]{1,0:T(8,128)(2,1)S(1)}, bf16[512,128]{1,0:T(8,128)(2,1)}, u32[]{:S(2)}) copy-start(bf16[512,128]{1,0:T(8,128)(2,1)} %param.31) | copy-start | bytes 393220
  1.8 8.7 %collective-permute-start.1 = (bf16[512,128]{1,0:T(8,128)(2,1)S(1)}, bf16[512,128]{1,0:T(8,128)(2,1)S(1)}, u32[]{:S(2)}, u32[]{:S(2)}) collective-permute-start(bf16[512,128]{1,0:T(8,128)(2,1)S(1)} %get-tuple-element.28.refs_0_), channel_id=1, source_target_pairs={{0,14},{2,0},{4,2},{6,4},{8,6},{10,8},{12,10},{14,12},{1,15},{3,1}... | collective-permute-start | bytes 393224 | tf_op jit(solution)/shard_map/ppermute | solution.py:291
  7.7 6.5 %collective-permute-start = (bf16[512,128]{1,0:T(8,128)(2,1)S(1)}, bf16[512,128]{1,0:T(8,128)(2,1)S(1)}, u32[]{:S(2)}, u32[]{:S(2)}) collective-permute-start(bf16[512,128]{1,0:T(8,128)(2,1)S(1)} %get-tuple-element.28.refs_0_), channel_id=1, source_target_pairs={{0,2},{2,4},{4,6},{6,8},{8,10},{10,12},{12,14},{14,0},{1,3},{3,5},... | collective-permute-start | bytes 393224 | tf_op jit(solution)/shard_map/ppermute | solution.py:290
  10.4 18.9 %collective-permute-start.3 = (bf16[512,128]{1,0:T(8,128)(2,1)S(1)}, bf16[512,128]{1,0:T(8,128)(2,1)S(1)}, u32[]{:S(2)}, u32[]{:S(2)}) collective-permute-start(bf16[512,128]{1,0:T(8,128)(2,1)S(1)} %collective-permute-done.1.refs_1_.refs_3_), channel_id=1, source_target_pairs={{0,14},{2,0},{4,2},{6,4},{8,6},{10,8},{12,10},{14,12},{1,15},{3,1}... | collective-permute-start | bytes 393224 | tf_op jit(solution)/shard_map/ppermute | solution.py:291
  14.1 15.2 %collective-permute-start.2 = (bf16[512,128]{1,0:T(8,128)(2,1)S(1)}, bf16[512,128]{1,0:T(8,128)(2,1)S(1)}, u32[]{:S(2)}, u32[]{:S(2)}) collective-permute-start(bf16[512,128]{1,0:T(8,128)(2,1)S(1)} %collective-permute-done.refs_0_.refs_2_), channel_id=1, source_target_pairs={{0,2},{2,4},{4,6},{6,8},{8,10},{10,12},{12,14},{14,0},{1,3},{3,5},... | collective-permute-start | bytes 393224 | tf_op jit(solution)/shard_map/ppermute | solution.py:290
  29.3 29.9 %all-to-all-start = ((bf16[16,400,128]{2,1,0:T(8,128)(2,1)}), bf16[16,400,128]{2,1,0:T(8,128)(2,1)S(1)}, u32[]{:S(2)}, u32[]{:S(2)}) async-start(bf16[16,400,128]{2,1,0:T(8,128)(2,1)} %shard_map.203), calls=%async_computation | async-start | bytes 3276800 | tf_op jit(solution)/shard_map/all_to_all | solution.py:339
  36.7 5.7 %collective-permute-start.5 = (bf16[512,128]{1,0:T(8,128)(2,1)S(1)}, bf16[512,128]{1,0:T(8,128)(2,1)S(1)}, u32[]{:S(2)}, u32[]{:S(2)}) collective-permute-start(bf16[512,128]{1,0:T(8,128)(2,1)S(1)} %collective-permute-done.3.refs_2_.refs_5_), channel_id=1, source_target_pairs={{0,14},{2,0},{4,2},{6,4},{8,6},{10,8},{12,10},{14,12},{1,15},{3,1}... | collective-permute-start | bytes 393224 | tf_op jit(solution)/shard_map/ppermute | solution.py:291
  40.0 6.2 %collective-permute-start.4 = (bf16[512,128]{1,0:T(8,128)(2,1)S(1)}, bf16[512,128]{1,0:T(8,128)(2,1)S(1)}, u32[]{:S(2)}, u32[]{:S(2)}) collective-permute-start(bf16[512,128]{1,0:T(8,128)(2,1)S(1)} %collective-permute-done.2.refs_1_.refs_4_), channel_id=1, source_target_pairs={{0,2},{2,4},{4,6},{6,8},{8,10},{10,12},{12,14},{14,0},{1,3},{3,5},... | collective-permute-start | bytes 393224 | tf_op jit(solution)/shard_map/ppermute | solution.py:290
  46.2 2.1 %collective-permute-start.8 = (bf16[2,512,128]{2,1,0:T(8,128)(2,1)S(1)}, bf16[2,512,128]{2,1,0:T(8,128)(2,1)S(1)}, u32[]{:S(2)}, u32[]{:S(2)}) collective-permute-start(bf16[2,512,128]{2,1,0:T(8,128)(2,1)S(1)} %pad_maximum_fusion.3), channel_id=1, source_target_pairs={{0,1},{1,0},{2,3},{3,2},{4,5},{5,4},{6,7},{7,6},{8,9},{9,8},{10,11... | collective-permute-start | bytes 786440 | tf_op jit(solution)/shard_map/ppermute | solution.py:293
  47.0 25.6 %copy-start.20 = (bf16[4096]{0:T(1024)(128)(2,1)S(1)}, bf16[4096]{0:T(1024)(128)(2,1)}, u32[]{:S(2)}) copy-start(bf16[4096]{0:T(1024)(128)(2,1)} %param.34) | copy-start | bytes 24580
  47.0 2.1 %collective-permute-start.6 = (bf16[2,512,128]{2,1,0:T(8,128)(2,1)}, bf16[2,512,128]{2,1,0:T(8,128)(2,1)S(1)}, u32[]{:S(2)}, u32[]{:S(2)}) collective-permute-start(bf16[2,512,128]{2,1,0:T(8,128)(2,1)} %pad_maximum_fusion.4), channel_id=1, source_target_pairs={{0,1},{1,0},{2,3},{3,2},{4,5},{5,4},{6,7},{7,6},{8,9},{9,8},{10,11... | collective-permute-start | bytes 786440 | tf_op jit(solution)/shard_map/ppermute | solution.py:293
  48.2 1.9 %collective-permute-start.7 = (bf16[2,512,128]{2,1,0:T(8,128)(2,1)}, bf16[2,512,128]{2,1,0:T(8,128)(2,1)}, u32[]{:S(2)}, u32[]{:S(2)}) collective-permute-start(bf16[2,512,128]{2,1,0:T(8,128)(2,1)} %pad_maximum_fusion.5), channel_id=1, source_target_pairs={{0,1},{1,0},{2,3},{3,2},{4,5},{5,4},{6,7},{7,6},{8,9},{9,8},{10,11... | collective-permute-start | bytes 786440 | tf_op jit(solution)/shard_map/ppermute | solution.py:293
  49.0 10.2 %collective-permute-start.9 = (bf16[2,512,128]{2,1,0:T(8,128)(2,1)}, bf16[2,512,128]{2,1,0:T(8,128)(2,1)}, u32[]{:S(2)}, u32[]{:S(2)}) collective-permute-start(bf16[2,512,128]{2,1,0:T(8,128)(2,1)} %pad_maximum_fusion.2), channel_id=1, source_target_pairs={{0,2},{2,4},{4,6},{6,8},{8,10},{10,12},{12,14},{14,0},{1,3},{3,5},... | collective-permute-start | bytes 786440 | tf_op jit(solution)/shard_map/ppermute | solution.py:295
  65.3 29.2 %all-to-all-start.1 = ((bf16[16,8,48,128]{3,2,1,0:T(8,128)(2,1)}), bf16[16,8,48,128]{3,2,1,0:T(8,128)(2,1)S(1)}, u32[]{:S(2)}, u32[]{:S(2)}) async-start(bf16[16,8,48,128]{3,2,1,0:T(8,128)(2,1)} %get-tuple-element.16.refs_0_.refs_1_), calls=%async_computation.1 | async-start | bytes 3145728 | tf_op jit(solution)/shard_map/all_to_all | solution.py:364
  108.1 5.3 %collective-permute-start.11 = (bf16[16,320,256]{2,1,0:T(8,128)(2,1)}, bf16[16,320,256]{2,1,0:T(8,128)(2,1)}, u32[]{:S(2)}, u32[]{:S(2)}) collective-permute-start(bf16[16,320,256]{2,1,0:T(8,128)(2,1)} %shard_map.209), channel_id=1, source_target_pairs={{0,1},{1,0},{2,3},{3,2},{4,5},{5,4},{6,7},{7,6},{8,9},{9,8},{10,11... | collective-permute-start | bytes 7864328 | tf_op jit(solution)/shard_map/ppermute | solution.py:427
  108.3 5.0 %copy-start.4 = (bf16[256,4096]{1,0:T(8,128)(2,1)S(1)}, bf16[256,4096]{1,0:T(8,128)(2,1)}, u32[]{:S(2)}) copy-start(bf16[256,4096]{1,0:T(8,128)(2,1)} %copy-done.3) | copy-start | bytes 6291460
  112.0 13.0 %collective-permute-start.10 = (f32[8,512,128]{2,1,0:T(8,128)}, f32[8,512,128]{2,1,0:T(8,128)}, u32[]{:S(2)}, u32[]{:S(2)}) collective-permute-start(f32[8,512,128]{2,1,0:T(8,128)} %shard_map.207), channel_id=1, source_target_pairs={{0,1},{1,0},{2,3},{3,2},{4,5},{5,4},{6,7},{7,6},{8,9},{9,8},{10,11... | collective-permute-start | bytes 6291464 | tf_op jit(solution)/shard_map/ppermute | solution.py:381
  118.3 46.6 %all-to-all-start.2 = ((bf16[16,320,256]{2,1,0:T(8,128)(2,1)}), bf16[16,320,256]{2,1,0:T(8,128)(2,1)}, u32[]{:S(2)}, u32[]{:S(2)}) async-start(bf16[16,320,256]{2,1,0:T(8,128)(2,1)} %copy-done.1), calls=%async_computation.2 | async-start | bytes 5242880 | tf_op jit(solution)/shard_map/all_to_all | solution.py:429
  128.5 13.0 %copy-start.5 = (bf16[256,4096]{1,0:T(8,128)(2,1)S(1)}, bf16[256,4096]{1,0:T(8,128)(2,1)}, u32[]{:S(2)}) copy-start(bf16[256,4096]{1,0:T(8,128)(2,1)} %copy-done.3) | copy-start | bytes 6291460
  128.6 9.3 %collective-permute-start.12 = (bf16[512,128]{1,0:T(8,128)(2,1)S(1)}, bf16[512,128]{1,0:T(8,128)(2,1)S(1)}, u32[]{:S(2)}, u32[]{:S(2)}) collective-permute-start(bf16[512,128]{1,0:T(8,128)(2,1)S(1)} %get-tuple-element.20), channel_id=1, source_target_pairs={{0,2},{2,4},{4,6},{6,8},{8,10},{10,12},{12,14},{14,0},{1,3},{3,5},... | collective-permute-start | bytes 393224 | tf_op jit(solution)/shard_map/ppermute | solution.py:431
  128.7 9.6 %collective-permute-start.18 = (bf16[512,128]{1,0:T(8,128)(2,1)S(1)}, bf16[512,128]{1,0:T(8,128)(2,1)S(1)}, u32[]{:S(2)}, u32[]{:S(2)}) collective-permute-start(bf16[512,128]{1,0:T(8,128)(2,1)S(1)} %get-tuple-element.21), channel_id=1, source_target_pairs={{0,14},{2,0},{4,2},{6,4},{8,6},{10,8},{12,10},{14,12},{1,15},{3,1}... | collective-permute-start | bytes 393224 | tf_op jit(solution)/shard_map/ppermute | solution.py:431
  132.0 16.5 %collective-permute-start.17 = (bf16[512,128]{1,0:T(8,128)(2,1)S(1)}, bf16[512,128]{1,0:T(8,128)(2,1)S(1)}, u32[]{:S(2)}, u32[]{:S(2)}) collective-permute-start(bf16[512,128]{1,0:T(8,128)(2,1)S(1)} %get-tuple-element.22), channel_id=1, source_target_pairs={{0,12},{2,14},{4,0},{6,2},{8,4},{10,6},{12,8},{14,10},{1,13},{3,15... | collective-permute-start | bytes 393224 | tf_op jit(solution)/shard_map/ppermute | solution.py:431
  132.0 22.2 %collective-permute-start.16 = (bf16[512,128]{1,0:T(8,128)(2,1)S(1)}, bf16[512,128]{1,0:T(8,128)(2,1)S(1)}, u32[]{:S(2)}, u32[]{:S(2)}) collective-permute-start(bf16[512,128]{1,0:T(8,128)(2,1)S(1)} %get-tuple-element.23), channel_id=1, source_target_pairs={{0,10},{2,12},{4,14},{6,0},{8,2},{10,4},{12,6},{14,8},{1,11},{3,13... | collective-permute-start | bytes 393224 | tf_op jit(solution)/shard_map/ppermute | solution.py:431
  133.6 20.5 %collective-permute-start.15 = (bf16[512,128]{1,0:T(8,128)(2,1)S(1)}, bf16[512,128]{1,0:T(8,128)(2,1)S(1)}, u32[]{:S(2)}, u32[]{:S(2)}) collective-permute-start(bf16[512,128]{1,0:T(8,128)(2,1)S(1)} %get-tuple-element.24), channel_id=1, source_target_pairs={{0,8},{2,10},{4,12},{6,14},{8,0},{10,2},{12,4},{14,6},{1,9},{3,11}... | collective-permute-start | bytes 393224 | tf_op jit(solution)/shard_map/ppermute | solution.py:431
  137.9 16.5 %collective-permute-start.14 = (bf16[512,128]{1,0:T(8,128)(2,1)S(1)}, bf16[512,128]{1,0:T(8,128)(2,1)S(1)}, u32[]{:S(2)}, u32[]{:S(2)}) collective-permute-start(bf16[512,128]{1,0:T(8,128)(2,1)S(1)} %get-tuple-element.25), channel_id=1, source_target_pairs={{0,6},{2,8},{4,10},{6,12},{8,14},{10,0},{12,2},{14,4},{1,7},{3,9},... | collective-permute-start | bytes 393224 | tf_op jit(solution)/shard_map/ppermute | solution.py:431
  138.3 19.0 %copy-start.16 = (f32[1024,128]{1,0:T(8,128)S(1)}, f32[1024,128]{1,0:T(8,128)}, u32[]{:S(2)}) copy-start(f32[1024,128]{1,0:T(8,128)} %param.27) | copy-start | bytes 1572868
  138.3 19.0 %copy-start.17 = (f32[1024,128]{1,0:T(8,128)S(1)}, f32[1024,128]{1,0:T(8,128)}, u32[]{:S(2)}) copy-start(f32[1024,128]{1,0:T(8,128)} %param.28) | copy-start | bytes 1572868
  138.3 17.2 %collective-permute-start.13 = (bf16[512,128]{1,0:T(8,128)(2,1)S(1)}, bf16[512,128]{1,0:T(8,128)(2,1)S(1)}, u32[]{:S(2)}, u32[]{:S(2)}) collective-permute-start(bf16[512,128]{1,0:T(8,128)(2,1)S(1)} %get-tuple-element.26), channel_id=1, source_target_pairs={{0,4},{2,6},{4,8},{6,10},{8,12},{10,14},{12,0},{14,2},{1,5},{3,7},... | collective-permute-start | bytes 393224 | tf_op jit(solution)/shard_map/ppermute | solution.py:431
  148.4 18.8 %copy-start.7 = (bf16[2,1,1536,128]{3,2,1,0:T(8,128)(2,1)S(1)}, bf16[2,1,1536,128]{3,2,1,0:T(8,128)(2,1)}, u32[]{:S(2)}) copy-start(bf16[2,1,1536,128]{3,2,1,0:T(8,128)(2,1)} %shard_map.206.refs_1_) | copy-start | bytes 2359300
  155.6 24.3 %copy-start.19 = (f32[320,32]{0,1:T(8,128)S(1)}, f32[320,32]{0,1:T(8,128)}, u32[]{:S(2)}) copy-start(f32[320,32]{0,1:T(8,128)} %param.35) | copy-start | bytes 122884
  155.6 1.6 collective-permute-start.19
  158.2 22.4 %copy-start.8 = (f32[1024,128]{1,0:T(8,128)}, f32[1024,128]{1,0:T(8,128)S(1)}, u32[]{:S(2)}) copy-start(f32[1024,128]{1,0:T(8,128)S(1)} %get-tuple-element.18.refs_2_) | copy-start | bytes 1572868
  (14 other events, 19.8 us)

commit v3 on v2

--- a/solution.py
+++ b/solution.py
@@ -13,7 +13,8 @@
 LEARN_RATE = 0.1
 LOSS_SCALE = 64.0
 LANES = 128
-VMEM = 24 * 1024 * 1024
+PLACES = 256
+VMEM = 14 * 1024 * 1024
 BF = jnp.bfloat16
 F32 = jnp.float32
 I32 = jnp.int32
@@ -25,6 +26,20 @@
 
 def ones_where(cond):
     return jnp.where(cond, 1.0, 0.0).astype(BF)
+
+
+def near(values, first, count):
+    values = values - first
+    return jnp.where((values >= 0) & (values < count), values, -1).astype(F32).astype(BF)
+
+
+def meet(places, shape, axis):
+    index = iota(shape, axis).astype(F32).astype(BF)
+    return jnp.where(places == index, jnp.ones(shape, BF), jnp.zeros(shape, BF))
+
+
+def hits(values, shape, axis, first=0):
+    return meet(near(values, first, shape[axis]), shape, axis)
 
 
 def mm(a, b):
@@ -103,10 +118,10 @@
 
 
 def gather_body(z_ref, asked_ref, *refs):
-    pairs = (len(refs) - 8) // 3
+    pairs = max((len(refs) - 8) // 3, 0)
     ring = 2 * pairs + 2
     halves, passed = refs[:2], refs[2 : 2 + 2 * pairs]
-    swapped, far_ref = refs[2 + 2 * pairs : 2 + 3 * pairs], refs[2 + 3 * pairs]
+    *swapped, far_ref = refs[2 + 2 * pairs : -5]
     out_ref, wanted_ref, cols_ref, hot_ref, req_ref = refs[-5:]
     groups = out_ref.shape[0]
     half = halves[0].shape[0]
@@ -124,38 +139,80 @@
     for offset in range(ring):
         z = lax.rem(me - offset + ring, ring)
         cols = cols_ref[z]
-        for w in range(groups):
-            hot_ref[w * both : (w + 1) * both, :] = ones_where(
-                cols[:both, w : w + 1] == iota((both, 2 * half), 1)
-            )
+        for at in range(0, 2 * half, PLACES):
+            ids = near(cols[:both], at, PLACES)
+            for w in range(groups):
+                hot_ref[offset % 2, w * both : (w + 1) * both, at : at + PLACES] = meet(
+                    ids[:, w : w + 1], (both, PLACES), 1
+                )
         if offset == 0:
             mine, other = halves[0][...], halves[1][...]
         elif offset == ring // 2:
-            mine, other = far_ref[0], far_ref[1]
+            mine, other = far_ref[...], swapped[0][0]
         else:
             at, way = (offset - 1, 0) if offset < ring // 2 else (ring - offset - 1, 1)
-            mine, other = passed[2 * at + way][...], swapped[at][way]
-        found = mm(hot_ref[:, :half], mine) + mm(hot_ref[:, half:], other)
+            mine, other = passed[2 * at + way][...], swapped[at][way + (at == 0)]
+        hot = hot_ref[offset % 2]
+        found = mm(hot[:, :half], mine) + mm(hot[:, half:], other)
         out_ref[:, z] = found.reshape(groups, both, LANES).astype(BF)
 
 
-def pool_body(bagpos_ref, reply_ref, out_ref):
+def gate_of(before):
+    return 0.5 + 0.5 * jnp.tanh(0.5 * before)
+
+
+def dense_body(*refs):
+    bagpos_ref, reply_ref, bottom_ref, bias_ref, out_weight_ref, label_ref, weight_ref = refs[:7]
+    joined_ref, delta_ref, held, slope_ref, sems = refs[-5:]
+    steps, _, wide = held.shape
+    copies = [
+        pltpu.make_async_copy(weight_ref.at[:, pl.ds(i * wide, wide)], held.at[i], sems.at[i])
+        for i in range(steps)
+    ]
+    for copy in copies:
+        copy.start()
+
     groups, ring, both, width = reply_ref.shape
-    samples = out_ref.shape[0] // 2
+    samples = joined_ref.shape[0] // 2
     bags = samples * FEATS
     slots = groups * ring * CAP
     size = slots // 8
-    wide = reply_ref[...].astype(F32)
+    split_at = bottom_ref.shape[1]
+    reply = reply_ref[...].astype(F32)
     for mb in range(2):
-        flat = wide[:, :, mb * CAP : (mb + 1) * CAP, :].reshape(slots, width).astype(BF)
+        flat = reply[:, :, mb * CAP : (mb + 1) * CAP, :].reshape(slots, width).astype(BF)
         total = jnp.zeros((bags, width), F32)
         for at in range(0, slots, size):
-            hot = ones_where(bagpos_ref[mb, :, at : at + size] == iota((bags, size), 0))
+            ids = bagpos_ref[mb, :, at : at + size]
+            hot = jnp.concatenate(
+                [hits(ids, (min(PLACES, bags), size), 0, low) for low in range(0, bags, PLACES)], axis=0
+            )
             total += mm(hot, flat[at : at + size])
+        rows = slice(mb * samples, (mb + 1) * samples)
+        joined_ref[rows, :split_at] = bottom_ref[rows]
         for feat in range(FEATS):
-            out_ref[mb * samples : (mb + 1) * samples, feat * width : (feat + 1) * width] = total[
-                feat * samples : (feat + 1) * samples
-            ].astype(BF)
+            at = split_at + feat * width
+            joined_ref[rows, at : at + width] = total[feat * samples : (feat + 1) * samples].astype(BF)
+
+    joined = joined_ref[...]
+    sums = jnp.zeros((2 * samples, LANES), F32)
+    for step in range(steps):
+        copies[step].wait()
+        before = mm(joined, held[step]) + bias_ref[step]
+        gate = gate_of(before)
+        slope_ref[step] = gate * (1.0 + before * (1.0 - gate))
+        terms = (before * gate).astype(BF).astype(F32) * out_weight_ref[step]
+        for at in range(0, wide, LANES):
+            sums += terms[:, at : at + LANES]
+    logits = jnp.sum(sums, axis=1, keepdims=True)
+    labels = jnp.concatenate(
+        [jnp.broadcast_to(label_ref[mb : mb + 1], (LANES, samples)).T[:, :1] for mb in range(2)], axis=0
+    )
+    logit_grad = LOSS_SCALE * (gate_of(logits) - labels.astype(F32))
+    for step in range(steps):
+        delta_ref[:, step * wide : (step + 1) * wide] = (
+            logit_grad * out_weight_ref[step] * slope_ref[step]
+        ).astype(BF)
 
 
 def tie_body(*refs):
@@ -182,12 +239,13 @@
     length = pos_ref.shape[2]
     first = pl.program_id(0) * here * per
     pad = [jnp.zeros((8 - ring, width), F32)] if ring < 8 else []
+    placed = []
+    for mb in range(2):
+        hot = [hits(pos_ref[mb] - first, (per, length), 0, w * per) for w in range(here)]
+        placed.append(mm(jnp.concatenate(hot, axis=0), grad_ref[mb]).reshape(here * ring, CAP, width))
+    placed = jnp.concatenate(placed, axis=1).reshape(here, rows - 16, width).astype(BF)
     for w in range(here):
-        placed = []
-        for mb in range(2):
-            hot = ones_where(pos_ref[mb] - first == iota((per, length), 0) + w * per)
-            placed.append(mm(hot, grad_ref[mb]).reshape(ring, CAP, width))
-        out_ref[w, : rows - 16] = jnp.concatenate(placed, axis=1).reshape(rows - 16, width).astype(BF)
+        out_ref[w, : rows - 16] = placed[w]
         mine = slice(w * ring, (w + 1) * ring)
         out_ref[w, rows - 16 :] = jnp.concatenate(
             [high_ref[mine]] + pad + [low_ref[mine]] + pad, axis=0
@@ -204,7 +262,9 @@
     for offset in range(ring):
         z = lax.rem(at_ref[0] + offset, ring)
         part = grad_ref[:, pl.ds(pl.multiple_of(z * both, both), both), :].reshape(count, width)
-        sums = mm(ones_where(rows_ref[z] == iota((half, count), 0) + at_ref[1]), part)
+        ids = rows_ref[z] - at_ref[1]
+        hot = [hits(ids, (PLACES, count), 0, low) for low in range(0, half, PLACES)]
+        sums = mm(jnp.concatenate(hot, axis=0), part)
         if len(refs) > 2:
             sums += refs[0][offset]
         out_ref[offset] = sums.astype(out_ref.dtype)
@@ -290,11 +350,11 @@
         ahead = lax.ppermute(ahead, "z", ring_of(ring, 1))
         back = lax.ppermute(back, "z", ring_of(ring, -1))
         rounds.append((ahead, back))
-    swapped = [lax.ppermute(jnp.stack(blocks), "nn", swap) for blocks in rounds]
-    far = jnp.stack([ahead, swapped[-1][0] if swapped else other_half])
-    far = lax.ppermute(far, "z", ring_of(ring, 1))
+    far = lax.ppermute(my_half, "z", ring_of(ring, ring // 2))
+    swapped = [lax.ppermute(jnp.stack(blocks), "nn", swap) for blocks in [(far, *rounds[0]), *rounds[1:]]] if rounds else [lax.ppermute(far[None], "nn", swap)]
 
     anywhere = pl.BlockSpec(memory_space=pl.ANY)
+    main = pl.BlockSpec(memory_space=pltpu.HBM)
     high, low, bagpos, old_pos, bag_or_none = call(
         functools.partial(route_body, samples * FEATS),
         (
@@ -305,14 +365,12 @@
             shape_of((2, 1, length), I32),
         ),
         (pltpu.VMEM((6, 2, 1, length), I32), pltpu.SemaphoreType.DMA((6,))),
-        in_specs=[anywhere] * 6,
+        in_specs=[main] * 6,
     )(
-        id_owner.reshape(2, 1, length),
-        stale_owner.reshape(2, 1, length),
-        id_row,
-        stale_row,
-        id_mask,
-        bag_index,
+        *(
+            pltpu.with_memory_space_constraint(x.reshape(2, 1, length), pltpu.HBM)
+            for x in (id_owner, stale_owner, id_row, stale_row, id_mask, bag_index)
+        )
     )
     bag_rows = (
         bagpos[:, : 2 * CAP].reshape(peers, 2, CAP).transpose(1, 0, 2).reshape(2, 1, peers * CAP)
@@ -331,11 +389,11 @@
             square,
             square,
         ]
-        + [anywhere] * 2,
+        + [],
         out_specs=pl.BlockSpec((groups // cut, rows, width), lambda i: (i, 0, 0)),
-    )(old_pos, stale_grad.reshape(2, length, width), high, low, *(rounds[0] if rounds else (my_half, my_half)))
-    if len(rounds) > 1:
-        outgoing = tie(outgoing, *rounds[1])
+    )(old_pos, stale_grad.reshape(2, length, width), high, low)
+    if rounds:
+        outgoing = tie(outgoing, *rounds[0], far)
     incoming = lax.all_to_all(outgoing, "w", split_axis=0, concat_axis=0, tiled=True)
 
     others = [my_half, other_half, *(block for blocks in rounds for block in blocks), *swapped, far]
@@ -347,7 +405,7 @@
         ),
         (
             pltpu.VMEM((ring, LANES, LANES), I32),
-            pltpu.VMEM((groups * 2 * CAP, table_rows), BF),
+            pltpu.VMEM((2, groups * 2 * CAP, table_rows), BF),
             pltpu.VMEM((peers, LANES), I32),
         ),
         grid=(1,),
@@ -369,6 +427,7 @@
         .reshape(ring, 1, groups * 2 * CAP)
     )
 
+
     def scatter(first, dtype, *more):
         return call(
             scatter_body,
@@ -380,27 +439,34 @@
 
     theirs = lax.ppermute(scatter(half_rows, F32), "nn", swap)
     ours = scatter(0, BF, theirs)
-    pooled = call(
-        pool_body,
-        shape_of((2 * samples, FEATS * width), BF),
-    )(bag_rows, here_replies)
-
     dense_rows = dense_input.reshape(2 * samples, dense_input.shape[2])
-    label_rows = labels.reshape(2 * samples)
     hidden = jax.nn.relu(mm(dense_rows, bottom_first) + bottom_bias).astype(BF)
     bottom = jax.nn.relu(mm(hidden, bottom_second)).astype(BF)
-    joined = jnp.concatenate([bottom, pooled], axis=1)
-    before = mm(joined, top_weight) + top_bias
-    gate = jax.nn.sigmoid(before)
-    active = (before * gate).astype(BF)
-    logits = mm(active, out_weight)
-    logit_grad = LOSS_SCALE * (jax.nn.sigmoid(logits) - label_rows.astype(F32))
-    top_delta = (
-        logit_grad[:, None]
-        * out_weight.astype(F32)[None, :]
-        * gate
-        * (1.0 + before * (1.0 - gate))
-    ).astype(BF)
+    steps = 8
+    hidden_units = top_weight.shape[1]
+    wide = hidden_units // steps
+    joined, top_delta = call(
+        dense_body,
+        (
+            shape_of((2 * samples, top_weight.shape[0]), BF),
+            shape_of((2 * samples, hidden_units), BF),
+        ),
+        (
+            pltpu.VMEM((steps, top_weight.shape[0], wide), BF),
+            pltpu.VMEM((steps, 2 * samples, wide), F32),
+            pltpu.SemaphoreType.DMA((steps,)),
+        ),
+        vmem=32 * 1024 * 1024,
+        in_specs=[pl.BlockSpec()] * 6 + [main],
+    )(
+        bag_rows,
+        here_replies,
+        bottom,
+        top_bias.reshape(steps, 1, wide),
+        out_weight.astype(F32).reshape(steps, 1, wide),
+        labels,
+        pltpu.with_memory_space_constraint(top_weight, pltpu.HBM),
+    )
     split_at = bottom.shape[1]
     back_grad = nt(top_delta, top_weight[split_at:])
     row_grads = call(pick_body, shape_of((2, 1, length, width), BF))(bag_or_none, back_grad)

time: 181 us -> 171 us (0.945)
  Pallas kernels: 33.2 us -> 39.8 us
  waiting for transfers between devices: 53.3 us -> 46.8 us
  local copies, waits for them, and re-layouts: 13.4 us -> 7.43 us
  matrix products: 10.6 us -> 5.09 us
  starting transfers between devices: 47.8 us -> 50.1 us
    ppermute x4, waiting for transfers between devices: 10.2 us -> 1.8 us  [the longest x3 1.8 us: per_device(): lax.ppermute(jnp.stack(blocks), 'nn', swap)]
    all_to_all x1, waiting for transfers between devices: 0.01 us -> 6.5 us  [per_device(): lax.all_to_all(outgoing, 'w', split_axis=0, concat_axis=0, tiled=True)]
    unnamed x47 -> x30, local copies, waits for them, and re-layouts: 10 us -> 3.82 us
    pallas_call x1, Pallas kernels: 1.79 us -> 7.75 us  [per_device(): call(dense_body, (shape_of((2 * samples, top_weight.shape[0]), BF), shape...]
    dot_general x3 -> x1, matrix products: 6.75 us -> 1.29 us  [mm(): return jnp.dot(a, b, preferred_element_type=F32)]
    ppermute x3, waiting for transfers between devices: 5.27 us -> 0.01 us  [per_device(): back = lax.ppermute(back, 'z', ring_of(ring, -1))]
    ppermute x4, starting transfers between devices: 0.61 us -> 4.99 us  [the longest x1 4.48 us: per_device(): far = lax.ppermute(my_half, 'z', ring_of(ring, ring // 2))]
    ppermute x3, starting transfers between devices: 12.9 us -> 10.5 us  [per_device(): back = lax.ppermute(back, 'z', ring_of(ring, -1))]
  transfers between devices with their start and end apart: 23 -> 23, of which waited for: 13 -> 10; matrix products, arithmetic and copies ran while one was open for 7% -> 7% of each run, Pallas kernels for 12% -> 14%
where the time goes in v3:
time: 171 us; the launch traced here: 170 us
  starting transfers between devices  50.1 us (29%)
  waiting for transfers between devices  46.8 us (27%)
  Pallas kernels  39.8 us (23%)
  blocking collectives  13.1 us (8%)
  local copies, waits for them, and re-layouts  7.43 us (4%)
  other arithmetic  6.93 us (4%)
  matrix products  5.09 us (3%)
    all_to_all x1, waiting for transfers between devices, per_device(): lax.all_to_all(replies, 'w', split_axis=0, concat_axis=0, tiled=True)  17.7 us
    all_to_all x1, blocking collectives, per_device(): lax.all_to_all(unit_part, 'z', split_axis=0, concat_axis=0, tiled=True)  13.1 us
    ppermute x7, starting transfers between devices, per_device(): lax.ppermute(ours[shift], 'z', ring_of(ring, shift))  12.1 us
    ppermute x3, starting transfers between devices, per_device(): back = lax.ppermute(back, 'z', ring_of(ring, -1))  10.5 us
    ppermute x7, waiting for transfers between devices, per_device(): lax.ppermute(ours[shift], 'z', ring_of(ring, shift))  9.52 us
    pallas_call x1, Pallas kernels, per_device(): call(dense_body, (shape_of((2 * samples, top_weight.shape[0]), BF), shape...  7.75 us
    all_to_all x1, starting transfers between devices, per_device(): lax.all_to_all(outgoing, 'w', split_axis=0, concat_axis=0, tiled=True)  7.4 us
    pallas_call x2, Pallas kernels, scatter(): call(scatter_body, shape_of((ring, half_rows, width), dtype), in_specs=[p...  7.22 us
  transfers between devices with their start and end apart: 23, of which 10 were waited for; matrix products, arithmetic and copies ran while one was open for 7% of the time, Pallas kernels for 14%

profile of v3, /device:TPU:8, one launch (start us, length us, event | category | flops | bytes accessed | tf_op | source)
XLA Modules:
  0.0 170.2 jit_solution(14986655712441364)
XLA Ops:
  1.8 2.0 %collective-permute-start = (bf16[512,128]{1,0:T(8,128)(2,1)S(1)}, bf16[512,128]{1,0:T(8,128)(2,1)S(1)}, u32[]{:S(2)}, u32[]{:S(2)}) collective-permute-start(bf16[512,128]{1,0:T(8,128)(2,1)S(1)} %get-tuple-element.32.refs_0_), channel_id=1, source_target_pairs={{0,2},{2,4},{4,6},{6,8},{8,10},{10,12},{12,14},{14,0},{1,3},{3,5},... | collective-permute-start | bytes 393224 | tf_op jit(solution)/shard_map/ppermute | solution.py:350
  3.8 4.0 %collective-permute-start.1 = (bf16[512,128]{1,0:T(8,128)(2,1)S(1)}, bf16[512,128]{1,0:T(8,128)(2,1)S(1)}, u32[]{:S(2)}, u32[]{:S(2)}) collective-permute-start(bf16[512,128]{1,0:T(8,128)(2,1)S(1)} %get-tuple-element.32.refs_0_), channel_id=1, source_target_pairs={{0,14},{2,0},{4,2},{6,4},{8,6},{10,8},{12,10},{14,12},{1,15},{3,1}... | collective-permute-start | bytes 393224 | tf_op jit(solution)/shard_map/ppermute | solution.py:351
  7.8 4.5 %collective-permute-start.2 = (bf16[512,128]{1,0:T(8,128)(2,1)S(1)}, bf16[512,128]{1,0:T(8,128)(2,1)S(1)}, u32[]{:S(2)}, u32[]{:S(2)}) collective-permute-start(bf16[512,128]{1,0:T(8,128)(2,1)S(1)} %get-tuple-element.32.refs_0_), channel_id=1, source_target_pairs={{0,8},{2,10},{4,12},{6,14},{8,0},{10,2},{12,4},{14,6},{1,9},{3,11}... | collective-permute-start | bytes 393224 | tf_op jit(solution)/shard_map/ppermute | solution.py:353
  12.3 4.2 %shard_map.201 = (f32[128,128]{1,0:T(8,128)S(1)}, f32[128,128]{1,0:T(8,128)S(1)}, s32[128,128]{1,0:T(8,128)S(1)}, s32[2,1,1536]{2,1,0:T(1,128)S(1)}, s32[2,1,1536]{2,1,0:T(1,128)S(1)}) custom-call(s32[2,1,1536]{2,1,0:T(1,128)} %bitcast.73, s32[2,1,1536]{2,1,0:T(1,128)} %bitcast.74, s32[2,1,1536]{2,1,0:T(1,128)} %refs_2_.1, s32[2,1,1536]{2,1,0:T(1,128)} %refs_3_.1, ...), custom_call_target="tpu_custom_call" | custom-call | tf_op jit(solution)/shard_map/pallas_call | solution.py:358
  17.6 6.3 %shard_map.202.refs_0_ = bf16[16,400,128]{2,1,0:T(8,128)(2,1)} custom-call(s32[2,1,1536]{2,1,0:T(1,128)S(1)} %get-tuple-element.15.pos_ref, bf16[2,1536,128]{2,1,0:T(8,128)(2,1)S(1)} %bitcast.62, f32[128,128]{1,0:T(8,128)S(1)} %get-tuple-element.16.high_ref, f32[128,128]{1,0:T(8,128)S(1)} %get-tuple-element.17.low_ref), custom_call_target="tpu_custom_call" | custom-call | tf_op jit(solution)/shard_map/pallas_call | solution.py:382
  23.9 7.4 %all-to-all-start = ((bf16[16,400,128]{2,1,0:T(8,128)(2,1)}), bf16[16,400,128]{2,1,0:T(8,128)(2,1)S(1)}, u32[]{:S(2)}, u32[]{:S(2)}) async-start(bf16[16,400,128]{2,1,0:T(8,128)(2,1)} %shard_map.203), calls=%async_computation | async-start | bytes 3276800 | tf_op jit(solution)/shard_map/all_to_all | solution.py:397
  31.3 3.2 %collective-permute-start.4 = (bf16[512,128]{1,0:T(8,128)(2,1)S(1)}, bf16[512,128]{1,0:T(8,128)(2,1)S(1)}, u32[]{:S(2)}, u32[]{:S(2)}) collective-permute-start(bf16[512,128]{1,0:T(8,128)(2,1)S(1)} %collective-permute-done.1.refs_2_.refs_3_), channel_id=1, source_target_pairs={{0,14},{2,0},{4,2},{6,4},{8,6},{10,8},{12,10},{14,12},{1,15},{3,1}... | collective-permute-start | bytes 393224 | tf_op jit(solution)/shard_map/ppermute | solution.py:351
  34.5 2.9 %collective-permute-done.3.refs_4_ = bf16[512,128]{1,0:T(8,128)(2,1)S(1)} collective-permute-done((bf16[512,128]{1,0:T(8,128)(2,1)S(1)}, bf16[512,128]{1,0:T(8,128)(2,1)S(1)}, u32[]{:S(2)}, u32[]{:S(2)}) %collective-permute-start.3) | collective-permute-done | bytes 131104 | tf_op jit(solution)/shard_map/ppermute | solution.py:350
  37.5 3.2 %collective-permute-start.6 = (bf16[512,128]{1,0:T(8,128)(2,1)S(1)}, bf16[512,128]{1,0:T(8,128)(2,1)S(1)}, u32[]{:S(2)}, u32[]{:S(2)}) collective-permute-start(bf16[512,128]{1,0:T(8,128)(2,1)S(1)} %collective-permute-done.4.refs_5_), channel_id=1, source_target_pairs={{0,14},{2,0},{4,2},{6,4},{8,6},{10,8},{12,10},{14,12},{1,15},{3,1}... | collective-permute-start | bytes 393224 | tf_op jit(solution)/shard_map/ppermute | solution.py:351
  44.5 1.8 %collective-permute-done.9.refs_10_ = bf16[2,512,128]{2,1,0:T(8,128)(2,1)} collective-permute-done((bf16[2,512,128]{2,1,0:T(8,128)(2,1)}, bf16[2,512,128]{2,1,0:T(8,128)(2,1)}, u32[]{:S(2)}, u32[]{:S(2)}) %collective-permute-start.9) | collective-permute-done | bytes 262176 | tf_op jit(solution)/shard_map/ppermute | solution.py:354
  46.3 6.5 %all-to-all-done.asked_ref.grad_ref = bf16[16,400,128]{2,1,0:T(8,128)(2,1)S(1)} async-done(((bf16[16,400,128]{2,1,0:T(8,128)(2,1)}), bf16[16,400,128]{2,1,0:T(8,128)(2,1)S(1)}, u32[]{:S(2)}, u32[]{:S(2)}) %all-to-all-start) | async-done | bytes 1638432 | tf_op jit(solution)/shard_map/all_to_all | solution.py:397
  52.8 6.1 %shard_map.204 = (bf16[16,8,48,128]{3,2,1,0:T(8,128)(2,1)}, s32[128,128]{1,0:T(8,128)S(1)}) custom-call(s32[2]{0:T(128)S(1)} %get-tuple-element.35.z_ref, bf16[16,400,128]{2,1,0:T(8,128)(2,1)S(1)} %all-to-all-done.asked_ref.grad_ref, bf16[512,128]{1,0:T(8,128)(2,1)S(1)} %get-tuple-element.32.refs_0_, bf16[512,128]{1,0:T(8,128)(2,1)S(1)} %get-tuple-element.31.refs_1_, ...), custom_call_target="tpu_custom_call" | custom-call | tf_op jit(solution)/shard_map/pallas_call | solution.py:400
  58.9 6.0 %all-to-all-start.1 = ((bf16[16,8,48,128]{3,2,1,0:T(8,128)(2,1)}), bf16[16,8,48,128]{3,2,1,0:T(8,128)(2,1)S(1)}, u32[]{:S(2)}, u32[]{:S(2)}) async-start(bf16[16,8,48,128]{3,2,1,0:T(8,128)(2,1)} %get-tuple-element.18.refs_0_.refs_1_), calls=%async_computation.1 | async-start | bytes 3145728 | tf_op jit(solution)/shard_map/all_to_all | solution.py:422
  68.8 17.7 %all-to-all-done.1.refs_1_ = bf16[16,8,48,128]{3,2,1,0:T(8,128)(2,1)S(1)} async-done(((bf16[16,8,48,128]{3,2,1,0:T(8,128)(2,1)}), bf16[16,8,48,128]{3,2,1,0:T(8,128)(2,1)S(1)}, u32[]{:S(2)}, u32[]{:S(2)}) %all-to-all-start.1) | async-done | bytes 1572896 | tf_op jit(solution)/shard_map/all_to_all | solution.py:422
  86.4 7.8 %shard_map.205 = (bf16[256,640]{1,0:T(8,128)(2,1)S(1)}, bf16[256,4096]{1,0:T(8,128)(2,1)S(1)}) custom-call(s32[2,1,3072]{2,1,0:T(1,128)S(1)} %reshape.61.refs_0_, bf16[16,8,48,128]{3,2,1,0:T(8,128)(2,1)S(1)} %all-to-all-done.1.refs_1_, bf16[256,128]{1,0:T(8,128)(2,1)S(1)} %fusion.6.refs_2_, f32[8,1,512]{2,1,0:T(1,128)S(1)} %bitcast.69, ...), custom_call_target="tpu_custom_call" | custom-call | tf_op jit(solution)/shard_map/pallas_call | solution.py:448
  94.4 2.9 %shard_map.209 = bf16[16,320,256]{2,1,0:T(8,128)(2,1)} custom-call(bf16[256,320]{1,0:T(8,128)(2,1)S(1)} %get-tuple-element.33.part_ref, bf16[256,4096]{1,0:T(8,128)(2,1)S(1)} %get-tuple-element.19.delta_ref), custom_call_target="tpu_custom_call" | custom-call | tf_op jit(solution)/shard_map/pallas_call | solution.py:481
  97.6 3.7 %shard_map.207 = f32[8,512,128]{2,1,0:T(8,128)} custom-call(s32[2]{0:T(128)S(1)} %get-tuple-element.36.at_ref, s32[8,1,768]{2,1,0:T(1,128)S(1)} %reshape.56.rows_ref, bf16[16,400,128]{2,1,0:T(8,128)(2,1)S(1)} %all-to-all-done.asked_ref.grad_ref, bf16[16,8,48,128]{3,2,1,0:T(8,128)(2,1)} %get-tuple-element.18.refs_0_.refs_1_), custom_call_target="tpu_custom_call" | custom-call | tf_op jit(solution)/shard_map/pallas_call | solution.py:432
  102.6 3.4 %shard_map.210.refs_1_ = bf16[16,320,256]{2,1,0:T(8,128)(2,1)S(1)} custom-call(bf16[256,320]{1,0:T(8,128)(2,1)S(1)} %get-tuple-element.34.part_ref, bf16[256,4096]{1,0:T(8,128)(2,1)S(1)} %copy-done.4, bf16[16,320,256]{2,1,0:T(8,128)(2,1)} %collective-permute-done.11.refs_0_), custom_call_target="tpu_custom_call" | custom-call | tf_op jit(solution)/shard_map/pallas_call | solution.py:481
  106.0 1.5 copy-done.1
  107.5 6.5 %all-to-all-start.2 = ((bf16[16,320,256]{2,1,0:T(8,128)(2,1)}), bf16[16,320,256]{2,1,0:T(8,128)(2,1)}, u32[]{:S(2)}, u32[]{:S(2)}) async-start(bf16[16,320,256]{2,1,0:T(8,128)(2,1)} %copy-done.1), calls=%async_computation.2 | async-start | bytes 5242880 | tf_op jit(solution)/shard_map/all_to_all | solution.py:495
  114.1 3.6 %shard_map.208.refs_0_ = bf16[8,512,128]{2,1,0:T(8,128)(2,1)S(1)} custom-call(s32[2]{0:T(128)S(1)} %pad_add_fusion.1.at_ref, s32[8,1,768]{2,1,0:T(1,128)S(1)} %reshape.56.rows_ref, bf16[16,400,128]{2,1,0:T(8,128)(2,1)S(1)} %all-to-all-done.asked_ref.grad_ref, f32[8,512,128]{2,1,0:T(8,128)} %collective-permute-done.10.refs_0_, ...), custom_call_target="tpu_custom_call" | custom-call | tf_op jit(solution)/shard_map/pallas_call | solution.py:432
  118.5 1.4 collective-permute-start.12
  120.0 4.5 %collective-permute-start.16 = (bf16[512,128]{1,0:T(8,128)(2,1)S(1)}, bf16[512,128]{1,0:T(8,128)(2,1)S(1)}, u32[]{:S(2)}, u32[]{:S(2)}) collective-permute-start(bf16[512,128]{1,0:T(8,128)(2,1)S(1)} %get-tuple-element.27), channel_id=1, source_target_pairs={{0,10},{2,12},{4,14},{6,0},{8,2},{10,4},{12,6},{14,8},{1,11},{3,13... | collective-permute-start | bytes 393224 | tf_op jit(solution)/shard_map/ppermute | solution.py:497
  124.5 3.1 %collective-permute-start.15 = (bf16[512,128]{1,0:T(8,128)(2,1)S(1)}, bf16[512,128]{1,0:T(8,128)(2,1)S(1)}, u32[]{:S(2)}, u32[]{:S(2)}) collective-permute-start(bf16[512,128]{1,0:T(8,128)(2,1)S(1)} %get-tuple-element.28), channel_id=1, source_target_pairs={{0,8},{2,10},{4,12},{6,14},{8,0},{10,2},{12,4},{14,6},{1,9},{3,11}... | collective-permute-start | bytes 393224 | tf_op jit(solution)/shard_map/ppermute | solution.py:497
  127.6 2.3 %collective-permute-start.13 = (bf16[512,128]{1,0:T(8,128)(2,1)S(1)}, bf16[512,128]{1,0:T(8,128)(2,1)S(1)}, u32[]{:S(2)}, u32[]{:S(2)}) collective-permute-start(bf16[512,128]{1,0:T(8,128)(2,1)S(1)} %get-tuple-element.30), channel_id=1, source_target_pairs={{0,4},{2,6},{4,8},{6,10},{8,12},{10,14},{12,0},{14,2},{1,5},{3,7},... | collective-permute-start | bytes 393224 | tf_op jit(solution)/shard_map/ppermute | solution.py:497
  129.9 3.8 %fusion.back_ref = f32[256,512]{1,0:T(8,128)S(1)} fusion(bf16[256,4096]{1,0:T(8,128)(2,1)S(1)} %copy-done.5, bf16[640,4096]{1,0:T(8,128)(2,1)} %refs_6_.1), kind=kOutput, calls=%fused_computation | convolution fusion | flops 1073741824 | bytes 6815744 | tf_op jit(solution)/shard_map/dot_general | solution.py:60
  133.7 1.9 %shard_map.206.refs_1_ = bf16[2,1,1536,128]{3,2,1,0:T(8,128)(2,1)} custom-call(s32[2,1,1536]{2,1,0:T(1,128)S(1)} %get-tuple-element.13.bag_ref, f32[256,512]{1,0:T(8,128)S(1)} %fusion.back_ref), custom_call_target="tpu_custom_call" | custom-call | tf_op jit(solution)/shard_map/pallas_call | solution.py:472
  137.8 8.5 %collective-permute-done.14 = bf16[512,128]{1,0:T(8,128)(2,1)S(1)} collective-permute-done((bf16[512,128]{1,0:T(8,128)(2,1)S(1)}, bf16[512,128]{1,0:T(8,128)(2,1)S(1)}, u32[]{:S(2)}, u32[]{:S(2)}) %collective-permute-start.14) | collective-permute-done | bytes 131104 | tf_op jit(solution)/shard_map/ppermute | solution.py:497
  146.5 1.5 collective-permute-done.19
  149.0 5.1 %all-to-all-done.2 = bf16[16,320,256]{2,1,0:T(8,128)(2,1)} async-done(((bf16[16,320,256]{2,1,0:T(8,128)(2,1)}), bf16[16,320,256]{2,1,0:T(8,128)(2,1)}, u32[]{:S(2)}, u32[]{:S(2)}) %all-to-all-start.2) | async-done | bytes 2621472 | tf_op jit(solution)/shard_map/all_to_all | solution.py:495
  154.1 2.1 %reduce_sum.21 = bf16[320,256]{1,0:T(8,128)(2,1)S(1)} reduce(bf16[16,320,256]{2,1,0:T(8,128)(2,1)} %all-to-all-done.2, bf16[]{:T(256)} %constant.33.clone.1), dimensions={0}, to_apply=%region_0.1 | reduce | flops 1228800 | bytes 2785282 | tf_op jit(solution)/shard_map/reduce_sum | solution.py:511
  156.4 13.1 %all_to_all.20 = bf16[8,32,320]{2,1,0:T(8,128)(2,1)S(1)} all-to-all(bf16[8,32,320]{2,1,0:T(8,128)(2,1)S(1)} %shard_map.213), channel_id=1, replica_groups=mesh['w'=16,'z'=8,'nn'=2] {'z'}, dimensions={0} | all-to-all | bytes 327680 | tf_op jit(solution)/shard_map/all_to_all | solution.py:513
  (81 shorter events, 16.7 us)
Async XLA Ops:
  0.6 66.8 %copy-start = (bf16[512,128]{1,0:T(8,128)(2,1)S(1)}, bf16[512,128]{1,0:T(8,128)(2,1)}, u32[]{:S(2)}) copy-start(bf16[512,128]{1,0:T(8,128)(2,1)} %param.31) | copy-start | bytes 393220
  1.8 22.1 %collective-permute-start = (bf16[512,128]{1,0:T(8,128)(2,1)S(1)}, bf16[512,128]{1,0:T(8,128)(2,1)S(1)}, u32[]{:S(2)}, u32[]{:S(2)}) collective-permute-start(bf16[512,128]{1,0:T(8,128)(2,1)S(1)} %get-tuple-element.32.refs_0_), channel_id=1, source_target_pairs={{0,2},{2,4},{4,6},{6,8},{8,10},{10,12},{12,14},{14,0},{1,3},{3,5},... | collective-permute-start | bytes 393224 | tf_op jit(solution)/shard_map/ppermute | solution.py:350
  3.8 20.1 %collective-permute-start.1 = (bf16[512,128]{1,0:T(8,128)(2,1)S(1)}, bf16[512,128]{1,0:T(8,128)(2,1)S(1)}, u32[]{:S(2)}, u32[]{:S(2)}) collective-permute-start(bf16[512,128]{1,0:T(8,128)(2,1)S(1)} %get-tuple-element.32.refs_0_), channel_id=1, source_target_pairs={{0,14},{2,0},{4,2},{6,4},{8,6},{10,8},{12,10},{14,12},{1,15},{3,1}... | collective-permute-start | bytes 393224 | tf_op jit(solution)/shard_map/ppermute | solution.py:351
  7.8 16.1 %collective-permute-start.2 = (bf16[512,128]{1,0:T(8,128)(2,1)S(1)}, bf16[512,128]{1,0:T(8,128)(2,1)S(1)}, u32[]{:S(2)}, u32[]{:S(2)}) collective-permute-start(bf16[512,128]{1,0:T(8,128)(2,1)S(1)} %get-tuple-element.32.refs_0_), channel_id=1, source_target_pairs={{0,8},{2,10},{4,12},{6,14},{8,0},{10,2},{12,4},{14,6},{1,9},{3,11}... | collective-permute-start | bytes 393224 | tf_op jit(solution)/shard_map/ppermute | solution.py:353
  23.9 28.9 %all-to-all-start = ((bf16[16,400,128]{2,1,0:T(8,128)(2,1)}), bf16[16,400,128]{2,1,0:T(8,128)(2,1)S(1)}, u32[]{:S(2)}, u32[]{:S(2)}) async-start(bf16[16,400,128]{2,1,0:T(8,128)(2,1)} %shard_map.203), calls=%async_computation | async-start | bytes 3276800 | tf_op jit(solution)/shard_map/all_to_all | solution.py:397
  31.3 6.2 %collective-permute-start.3 = (bf16[512,128]{1,0:T(8,128)(2,1)S(1)}, bf16[512,128]{1,0:T(8,128)(2,1)S(1)}, u32[]{:S(2)}, u32[]{:S(2)}) collective-permute-start(bf16[512,128]{1,0:T(8,128)(2,1)S(1)} %collective-permute-done.refs_1_.refs_2_), channel_id=1, source_target_pairs={{0,2},{2,4},{4,6},{6,8},{8,10},{10,12},{12,14},{14,0},{1,3},{3,5},... | collective-permute-start | bytes 393224 | tf_op jit(solution)/shard_map/ppermute | solution.py:350
  31.3 6.2 %collective-permute-start.4 = (bf16[512,128]{1,0:T(8,128)(2,1)S(1)}, bf16[512,128]{1,0:T(8,128)(2,1)S(1)}, u32[]{:S(2)}, u32[]{:S(2)}) collective-permute-start(bf16[512,128]{1,0:T(8,128)(2,1)S(1)} %collective-permute-done.1.refs_2_.refs_3_), channel_id=1, source_target_pairs={{0,14},{2,0},{4,2},{6,4},{8,6},{10,8},{12,10},{14,12},{1,15},{3,1}... | collective-permute-start | bytes 393224 | tf_op jit(solution)/shard_map/ppermute | solution.py:351
  37.5 6.2 %collective-permute-start.5 = (bf16[512,128]{1,0:T(8,128)(2,1)S(1)}, bf16[512,128]{1,0:T(8,128)(2,1)S(1)}, u32[]{:S(2)}, u32[]{:S(2)}) collective-permute-start(bf16[512,128]{1,0:T(8,128)(2,1)S(1)} %collective-permute-done.3.refs_4_), channel_id=1, source_target_pairs={{0,2},{2,4},{4,6},{6,8},{8,10},{10,12},{12,14},{14,0},{1,3},{3,5},... | collective-permute-start | bytes 393224 | tf_op jit(solution)/shard_map/ppermute | solution.py:350
  37.5 6.2 %collective-permute-start.6 = (bf16[512,128]{1,0:T(8,128)(2,1)S(1)}, bf16[512,128]{1,0:T(8,128)(2,1)S(1)}, u32[]{:S(2)}, u32[]{:S(2)}) collective-permute-start(bf16[512,128]{1,0:T(8,128)(2,1)S(1)} %collective-permute-done.4.refs_5_), channel_id=1, source_target_pairs={{0,14},{2,0},{4,2},{6,4},{8,6},{10,8},{12,10},{14,12},{1,15},{3,1}... | collective-permute-start | bytes 393224 | tf_op jit(solution)/shard_map/ppermute | solution.py:351
  41.5 3.0 %collective-permute-start.7 = (bf16[3,512,128]{2,1,0:T(8,128)(2,1)}, bf16[3,512,128]{2,1,0:T(8,128)(2,1)S(1)}, u32[]{:S(2)}, u32[]{:S(2)}) collective-permute-start(bf16[3,512,128]{2,1,0:T(8,128)(2,1)} %pad_maximum_fusion), channel_id=1, source_target_pairs={{0,1},{1,0},{2,3},{3,2},{4,5},{5,4},{6,7},{7,6},{8,9},{9,8},{10,11... | collective-permute-start | bytes 1179656 | tf_op jit(solution)/shard_map/ppermute | solution.py:354
  42.2 2.2 %collective-permute-start.8 = (bf16[2,512,128]{2,1,0:T(8,128)(2,1)}, bf16[2,512,128]{2,1,0:T(8,128)(2,1)}, u32[]{:S(2)}, u32[]{:S(2)}) collective-permute-start(bf16[2,512,128]{2,1,0:T(8,128)(2,1)} %pad_maximum_fusion.1), channel_id=1, source_target_pairs={{0,1},{1,0},{2,3},{3,2},{4,5},{5,4},{6,7},{7,6},{8,9},{9,8},{10,11... | collective-permute-start | bytes 786440 | tf_op jit(solution)/shard_map/ppermute | solution.py:354
  44.4 1.9 %collective-permute-start.9 = (bf16[2,512,128]{2,1,0:T(8,128)(2,1)}, bf16[2,512,128]{2,1,0:T(8,128)(2,1)}, u32[]{:S(2)}, u32[]{:S(2)}) collective-permute-start(bf16[2,512,128]{2,1,0:T(8,128)(2,1)} %pad_maximum_fusion.2), channel_id=1, source_target_pairs={{0,1},{1,0},{2,3},{3,2},{4,5},{5,4},{6,7},{7,6},{8,9},{9,8},{10,11... | collective-permute-start | bytes 786440 | tf_op jit(solution)/shard_map/ppermute | solution.py:354
  58.8 8.6 %copy-start.14 = (f32[512]{0:T(512)S(1)}, f32[512]{0:T(512)}, u32[]{:S(2)}) copy-start(f32[512]{0:T(512)} %param.30) | copy-start | bytes 6148
  58.8 27.6 %copy-start.9 = (f32[4096]{0:T(1024)S(1)}, f32[4096]{0:T(1024)}, u32[]{:S(2)}) copy-start(f32[4096]{0:T(1024)} %param.33) | copy-start | bytes 49156
  58.9 27.6 %copy-start.10 = (s32[2,128]{1,0:T(2,128)S(1)}, s32[2,128]{1,0:T(2,128)}, u32[]{:S(2)}) copy-start(s32[2,128]{1,0:T(2,128)} %refs_5_.3) | copy-start | bytes 3076
  58.9 27.6 %all-to-all-start.1 = ((bf16[16,8,48,128]{3,2,1,0:T(8,128)(2,1)}), bf16[16,8,48,128]{3,2,1,0:T(8,128)(2,1)S(1)}, u32[]{:S(2)}, u32[]{:S(2)}) async-start(bf16[16,8,48,128]{3,2,1,0:T(8,128)(2,1)} %get-tuple-element.18.refs_0_.refs_1_), calls=%async_computation.1 | async-start | bytes 3145728 | tf_op jit(solution)/shard_map/all_to_all | solution.py:422
  97.3 5.3 %collective-permute-start.11 = (bf16[16,320,256]{2,1,0:T(8,128)(2,1)}, bf16[16,320,256]{2,1,0:T(8,128)(2,1)}, u32[]{:S(2)}, u32[]{:S(2)}) collective-permute-start(bf16[16,320,256]{2,1,0:T(8,128)(2,1)} %shard_map.209), channel_id=1, source_target_pairs={{0,1},{1,0},{2,3},{3,2},{4,5},{5,4},{6,7},{7,6},{8,9},{9,8},{10,11... | collective-permute-start | bytes 7864328 | tf_op jit(solution)/shard_map/ppermute | solution.py:493
  101.2 12.9 %collective-permute-start.10 = (f32[8,512,128]{2,1,0:T(8,128)}, f32[8,512,128]{2,1,0:T(8,128)}, u32[]{:S(2)}, u32[]{:S(2)}) collective-permute-start(f32[8,512,128]{2,1,0:T(8,128)} %shard_map.207), channel_id=1, source_target_pairs={{0,1},{1,0},{2,3},{3,2},{4,5},{5,4},{6,7},{7,6},{8,9},{9,8},{10,11... | collective-permute-start | bytes 6291464 | tf_op jit(solution)/shard_map/ppermute | solution.py:440
  107.5 46.6 %all-to-all-start.2 = ((bf16[16,320,256]{2,1,0:T(8,128)(2,1)}), bf16[16,320,256]{2,1,0:T(8,128)(2,1)}, u32[]{:S(2)}, u32[]{:S(2)}) async-start(bf16[16,320,256]{2,1,0:T(8,128)(2,1)} %copy-done.1), calls=%async_computation.2 | async-start | bytes 5242880 | tf_op jit(solution)/shard_map/all_to_all | solution.py:495
  117.7 12.2 %copy-start.5 = (bf16[256,4096]{1,0:T(8,128)(2,1)S(1)}, bf16[256,4096]{1,0:T(8,128)(2,1)}, u32[]{:S(2)}) copy-start(bf16[256,4096]{1,0:T(8,128)(2,1)} %copy-done.3) | copy-start | bytes 6291460
  117.8 9.8 %collective-permute-start.18 = (bf16[512,128]{1,0:T(8,128)(2,1)S(1)}, bf16[512,128]{1,0:T(8,128)(2,1)S(1)}, u32[]{:S(2)}, u32[]{:S(2)}) collective-permute-start(bf16[512,128]{1,0:T(8,128)(2,1)S(1)} %get-tuple-element.25), channel_id=1, source_target_pairs={{0,14},{2,0},{4,2},{6,4},{8,6},{10,8},{12,10},{14,12},{1,15},{3,1}... | collective-permute-start | bytes 393224 | tf_op jit(solution)/shard_map/ppermute | solution.py:497
  118.5 9.2 %collective-permute-start.12 = (bf16[512,128]{1,0:T(8,128)(2,1)S(1)}, bf16[512,128]{1,0:T(8,128)(2,1)S(1)}, u32[]{:S(2)}, u32[]{:S(2)}) collective-permute-start(bf16[512,128]{1,0:T(8,128)(2,1)S(1)} %get-tuple-element.24), channel_id=1, source_target_pairs={{0,2},{2,4},{4,6},{6,8},{8,10},{10,12},{12,14},{14,0},{1,3},{3,5},... | collective-permute-start | bytes 393224 | tf_op jit(solution)/shard_map/ppermute | solution.py:497
  119.9 16.9 %collective-permute-start.17 = (bf16[512,128]{1,0:T(8,128)(2,1)S(1)}, bf16[512,128]{1,0:T(8,128)(2,1)S(1)}, u32[]{:S(2)}, u32[]{:S(2)}) collective-permute-start(bf16[512,128]{1,0:T(8,128)(2,1)S(1)} %get-tuple-element.26), channel_id=1, source_target_pairs={{0,12},{2,14},{4,0},{6,2},{8,4},{10,6},{12,8},{14,10},{1,13},{3,15... | collective-permute-start | bytes 393224 | tf_op jit(solution)/shard_map/ppermute | solution.py:497
  120.0 16.8 %collective-permute-start.16 = (bf16[512,128]{1,0:T(8,128)(2,1)S(1)}, bf16[512,128]{1,0:T(8,128)(2,1)S(1)}, u32[]{:S(2)}, u32[]{:S(2)}) collective-permute-start(bf16[512,128]{1,0:T(8,128)(2,1)S(1)} %get-tuple-element.27), channel_id=1, source_target_pairs={{0,10},{2,12},{4,14},{6,0},{8,2},{10,4},{12,6},{14,8},{1,11},{3,13... | collective-permute-start | bytes 393224 | tf_op jit(solution)/shard_map/ppermute | solution.py:497
  124.5 13.3 %collective-permute-start.15 = (bf16[512,128]{1,0:T(8,128)(2,1)S(1)}, bf16[512,128]{1,0:T(8,128)(2,1)S(1)}, u32[]{:S(2)}, u32[]{:S(2)}) collective-permute-start(bf16[512,128]{1,0:T(8,128)(2,1)S(1)} %get-tuple-element.28), channel_id=1, source_target_pairs={{0,8},{2,10},{4,12},{6,14},{8,0},{10,2},{12,4},{14,6},{1,9},{3,11}... | collective-permute-start | bytes 393224 | tf_op jit(solution)/shard_map/ppermute | solution.py:497
  127.6 18.7 %collective-permute-start.14 = (bf16[512,128]{1,0:T(8,128)(2,1)S(1)}, bf16[512,128]{1,0:T(8,128)(2,1)S(1)}, u32[]{:S(2)}, u32[]{:S(2)}) collective-permute-start(bf16[512,128]{1,0:T(8,128)(2,1)S(1)} %get-tuple-element.29), channel_id=1, source_target_pairs={{0,6},{2,8},{4,10},{6,12},{8,14},{10,0},{12,2},{14,4},{1,7},{3,9},... | collective-permute-start | bytes 393224 | tf_op jit(solution)/shard_map/ppermute | solution.py:497
  127.6 18.7 %collective-permute-start.13 = (bf16[512,128]{1,0:T(8,128)(2,1)S(1)}, bf16[512,128]{1,0:T(8,128)(2,1)S(1)}, u32[]{:S(2)}, u32[]{:S(2)}) collective-permute-start(bf16[512,128]{1,0:T(8,128)(2,1)S(1)} %get-tuple-element.30), channel_id=1, source_target_pairs={{0,4},{2,6},{4,8},{6,10},{8,12},{10,14},{12,0},{14,2},{1,5},{3,7},... | collective-permute-start | bytes 393224 | tf_op jit(solution)/shard_map/ppermute | solution.py:497
  133.7 14.3 %copy-start.11 = (f32[1024,128]{1,0:T(8,128)S(1)}, f32[1024,128]{1,0:T(8,128)}, u32[]{:S(2)}) copy-start(f32[1024,128]{1,0:T(8,128)} %param.27) | copy-start | bytes 1572868
  133.7 14.3 %copy-start.12 = (f32[1024,128]{1,0:T(8,128)S(1)}, f32[1024,128]{1,0:T(8,128)}, u32[]{:S(2)}) copy-start(f32[1024,128]{1,0:T(8,128)} %param.28) | copy-start | bytes 1572868
  146.4 1.6 collective-permute-start.19
  149.0 7.4 %copy-start.7 = (f32[1024,128]{1,0:T(8,128)}, f32[1024,128]{1,0:T(8,128)S(1)}, u32[]{:S(2)}) copy-start(f32[1024,128]{1,0:T(8,128)S(1)} %get-tuple-element.22.refs_2_) | copy-start | bytes 1572868
  149.0 20.5 %copy-start.13 = (f32[320,32]{0,1:T(8,128)S(1)}, f32[320,32]{0,1:T(8,128)}, u32[]{:S(2)}) copy-start(f32[320,32]{0,1:T(8,128)} %param.35) | copy-start | bytes 122884
  (6 other events, 15.5 us)

commit v4 on v3

--- a/solution.py
+++ b/solution.py
@@ -432,12 +432,14 @@
         return call(
             scatter_body,
             shape_of((ring, half_rows, width), dtype),
+            vmem=10 * 1024 * 1024,
             in_specs=[pl.BlockSpec(memory_space=pltpu.SMEM)]
             + [pl.BlockSpec()] * (2 + len(more))
             + [anywhere],
         )(jnp.stack([my_z, jnp.full((), first, I32)]), old_rows, incoming, *more, replies)
 
-    theirs = lax.ppermute(scatter(half_rows, F32), "nn", swap)
+    leaving = scatter(half_rows, F32)
+    theirs = lax.ppermute(leaving, "nn", swap)
     ours = scatter(0, BF, theirs)
     dense_rows = dense_input.reshape(2 * samples, dense_input.shape[2])
     hidden = jax.nn.relu(mm(dense_rows, bottom_first) + bottom_bias).astype(BF)
@@ -456,8 +458,8 @@
             pltpu.VMEM((steps, 2 * samples, wide), F32),
             pltpu.SemaphoreType.DMA((steps,)),
         ),
-        vmem=32 * 1024 * 1024,
-        in_specs=[pl.BlockSpec()] * 6 + [main],
+        vmem=24 * 1024 * 1024,
+        in_specs=[pl.BlockSpec()] * 6 + [main, anywhere],
     )(
         bag_rows,
         here_replies,
@@ -466,10 +468,11 @@
         out_weight.astype(F32).reshape(steps, 1, wide),
         labels,
         pltpu.with_memory_space_constraint(top_weight, pltpu.HBM),
+        leaving,
     )
     split_at = bottom.shape[1]
     back_grad = nt(top_delta, top_weight[split_at:])
-    row_grads = call(pick_body, shape_of((2, 1, length, width), BF))(bag_or_none, back_grad)
+    row_grads = call(pick_body, shape_of((2, 1, length, width), BF), vmem=8 * 1024 * 1024)(bag_or_none, back_grad)
 
     inputs = joined.shape[1] // 2
     units = top_delta.shape[1] // peers
@@ -481,12 +484,13 @@
         return call(
             outer_body,
             shape_of((groups, inputs, wide), BF),
+            vmem=8 * 1024 * 1024,
             grid=(4,),
             in_specs=[
                 pl.BlockSpec((2 * samples, inputs), lambda i: (0, 0)),
                 pl.BlockSpec((2 * samples, here * wide), lambda i: (0, i)),
             ]
-            + [block] * len(more),
+            + [block, anywhere][: len(more)],
             out_specs=block,
         )(lax.dynamic_slice_in_dim(joined, at * inputs, inputs, 1), top_delta, *more)
 
@@ -509,7 +513,7 @@
     new_table = emb_table - LEARN_RATE * row_sum * lax.rsqrt(new_squares)
 
     unit_part = jnp.sum(unit_part.astype(F32), axis=0).T.astype(BF).reshape(ring, units, inputs)
-    unit_part = tie(unit_part, row_grads, new_table)
+    unit_part = tie(unit_part, row_grads)
     unit_part = lax.all_to_all(unit_part, "z", split_axis=0, concat_axis=0, tiled=True)
     top_grad = jnp.sum(unit_part.astype(F32), axis=0).T
     top_step = top_grad * lax.rsqrt(top_squares + top_grad * top_grad)

time: 171 us -> 169 us (0.988)
  blocking collectives: 13.1 us -> 0 us
  waiting for transfers between devices: 46.8 us -> 59.7 us
  starting transfers between devices: 50.1 us -> 53.8 us
  Pallas kernels: 39.8 us -> 36.7 us
  matrix products: 5.09 us -> 2.87 us
    all_to_all x1 -> x0, blocking collectives: 13.1 us -> none  [per_device(): lax.all_to_all(unit_part, 'z', split_axis=0, concat_axis=0, tiled=True)]
    all_to_all x0 -> x1, waiting for transfers between devices: none -> 9.02 us  [per_device(): lax.all_to_all(unit_part, 'z', split_axis=0, concat_axis=0, tiled=True)]
    ppermute x1, waiting for transfers between devices: 0.84 us -> 4.94 us  [per_device(): unit_part = outer(core, lax.ppermute(outer(1 - core), 'nn', swap))]
    all_to_all x0 -> x1, starting transfers between devices: none -> 3.52 us  [per_device(): lax.all_to_all(unit_part, 'z', split_axis=0, concat_axis=0, tiled=True)]
    all_to_all x1, waiting for transfers between devices: 17.7 us -> 14.3 us  [per_device(): lax.all_to_all(replies, 'w', split_axis=0, concat_axis=0, tiled=True)]
    ppermute x7, waiting for transfers between devices: 9.52 us -> 12.7 us  [per_device(): lax.ppermute(ours[shift], 'z', ring_of(ring, shift))]
    pallas_call x5, Pallas kernels: 15.5 us -> 12.4 us  [the longest x2 7.29 us: scatter(): call(scatter_body, shape_of((ring, half_rows, width), dtype), vmem=10 * 1...]
    dot_general x1, matrix products: 3.8 us -> 1.62 us  [nt(): lax.dot_general(a, b, (((1,), (1,)), ((), ())), preferred_element_type=F32)]
  transfers between devices with their start and end apart: 23 -> 24, of which waited for: 10 -> 11; matrix products, arithmetic and copies ran while one was open for 7% -> 7% of each run, Pallas kernels for 14% -> 13%
where the time goes in v4:
time: 169 us
  waiting for transfers between devices  59.7 us (35%)
  starting transfers between devices  53.8 us (32%)
  Pallas kernels  36.7 us (22%)
  local copies, waits for them, and re-layouts  8.1 us (5%)
  other arithmetic  6.48 us (4%)
  matrix products  2.87 us (2%)
    all_to_all x1, waiting for transfers between devices, per_device(): lax.all_to_all(replies, 'w', split_axis=0, concat_axis=0, tiled=True)  14.3 us
    ppermute x7, waiting for transfers between devices, per_device(): lax.ppermute(ours[shift], 'z', ring_of(ring, shift))  12.7 us
    ppermute x7, starting transfers between devices, per_device(): lax.ppermute(ours[shift], 'z', ring_of(ring, shift))  12.1 us
    ppermute x3, starting transfers between devices, per_device(): back = lax.ppermute(back, 'z', ring_of(ring, -1))  10.5 us
    all_to_all x1, waiting for transfers between devices, per_device(): lax.all_to_all(unit_part, 'z', split_axis=0, concat_axis=0, tiled=True)  9.02 us
    pallas_call x1, Pallas kernels, per_device(): call(dense_body, (shape_of((2 * samples, top_weight.shape[0]), BF), shape...  7.72 us
    all_to_all x1, starting transfers between devices, per_device(): lax.all_to_all(outgoing, 'w', split_axis=0, concat_axis=0, tiled=True)  7.4 us
    pallas_call x2, Pallas kernels, scatter(): call(scatter_body, shape_of((ring, half_rows, width), dtype), vmem=10 * 1...  7.29 us
  transfers between devices with their start and end apart: 24, of which 11 were waited for; matrix products, arithmetic and copies ran while one was open for 7% of the time, Pallas kernels for 13%

profile of v4, /device:TPU:8, one launch (start us, length us, event | category | flops | bytes accessed | tf_op | source)
XLA Modules:
  0.0 168.7 jit_solution(16865248823387682537)
XLA Ops:
  1.8 2.0 %collective-permute-start = (bf16[512,128]{1,0:T(8,128)(2,1)S(1)}, bf16[512,128]{1,0:T(8,128)(2,1)S(1)}, u32[]{:S(2)}, u32[]{:S(2)}) collective-permute-start(bf16[512,128]{1,0:T(8,128)(2,1)S(1)} %get-tuple-element.32.refs_0_), channel_id=1, source_target_pairs={{0,2},{2,4},{4,6},{6,8},{8,10},{10,12},{12,14},{14,0},{1,3},{3,5},... | collective-permute-start | bytes 393224 | tf_op jit(solution)/shard_map/ppermute | solution.py:350
  3.8 4.0 %collective-permute-start.1 = (bf16[512,128]{1,0:T(8,128)(2,1)S(1)}, bf16[512,128]{1,0:T(8,128)(2,1)S(1)}, u32[]{:S(2)}, u32[]{:S(2)}) collective-permute-start(bf16[512,128]{1,0:T(8,128)(2,1)S(1)} %get-tuple-element.32.refs_0_), channel_id=1, source_target_pairs={{0,14},{2,0},{4,2},{6,4},{8,6},{10,8},{12,10},{14,12},{1,15},{3,1}... | collective-permute-start | bytes 393224 | tf_op jit(solution)/shard_map/ppermute | solution.py:351
  7.8 4.5 %collective-permute-start.2 = (bf16[512,128]{1,0:T(8,128)(2,1)S(1)}, bf16[512,128]{1,0:T(8,128)(2,1)S(1)}, u32[]{:S(2)}, u32[]{:S(2)}) collective-permute-start(bf16[512,128]{1,0:T(8,128)(2,1)S(1)} %get-tuple-element.32.refs_0_), channel_id=1, source_target_pairs={{0,8},{2,10},{4,12},{6,14},{8,0},{10,2},{12,4},{14,6},{1,9},{3,11}... | collective-permute-start | bytes 393224 | tf_op jit(solution)/shard_map/ppermute | solution.py:353
  12.3 4.2 %shard_map.201 = (f32[128,128]{1,0:T(8,128)S(1)}, f32[128,128]{1,0:T(8,128)S(1)}, s32[128,128]{1,0:T(8,128)S(1)}, s32[2,1,1536]{2,1,0:T(1,128)S(1)}, s32[2,1,1536]{2,1,0:T(1,128)S(1)}) custom-call(s32[2,1,1536]{2,1,0:T(1,128)} %bitcast.74, s32[2,1,1536]{2,1,0:T(1,128)} %bitcast.75, s32[2,1,1536]{2,1,0:T(1,128)} %refs_2_.1, s32[2,1,1536]{2,1,0:T(1,128)} %refs_3_.1, ...), custom_call_target="tpu_custom_call" | custom-call | tf_op jit(solution)/shard_map/pallas_call | solution.py:358
  17.6 6.3 %shard_map.202.refs_0_ = bf16[16,400,128]{2,1,0:T(8,128)(2,1)} custom-call(s32[2,1,1536]{2,1,0:T(1,128)S(1)} %get-tuple-element.15.pos_ref, bf16[2,1536,128]{2,1,0:T(8,128)(2,1)S(1)} %bitcast.61, f32[128,128]{1,0:T(8,128)S(1)} %get-tuple-element.16.high_ref, f32[128,128]{1,0:T(8,128)S(1)} %get-tuple-element.17.low_ref), custom_call_target="tpu_custom_call" | custom-call | tf_op jit(solution)/shard_map/pallas_call | solution.py:382
  23.9 7.4 %all-to-all-start = ((bf16[16,400,128]{2,1,0:T(8,128)(2,1)}), bf16[16,400,128]{2,1,0:T(8,128)(2,1)S(1)}, u32[]{:S(2)}, u32[]{:S(2)}) async-start(bf16[16,400,128]{2,1,0:T(8,128)(2,1)} %shard_map.203), calls=%async_computation | async-start | bytes 3276800 | tf_op jit(solution)/shard_map/all_to_all | solution.py:397
  31.3 3.2 %collective-permute-start.4 = (bf16[512,128]{1,0:T(8,128)(2,1)S(1)}, bf16[512,128]{1,0:T(8,128)(2,1)S(1)}, u32[]{:S(2)}, u32[]{:S(2)}) collective-permute-start(bf16[512,128]{1,0:T(8,128)(2,1)S(1)} %collective-permute-done.1.refs_2_.refs_3_), channel_id=1, source_target_pairs={{0,14},{2,0},{4,2},{6,4},{8,6},{10,8},{12,10},{14,12},{1,15},{3,1}... | collective-permute-start | bytes 393224 | tf_op jit(solution)/shard_map/ppermute | solution.py:351
  34.5 2.9 %collective-permute-done.3.refs_4_ = bf16[512,128]{1,0:T(8,128)(2,1)S(1)} collective-permute-done((bf16[512,128]{1,0:T(8,128)(2,1)S(1)}, bf16[512,128]{1,0:T(8,128)(2,1)S(1)}, u32[]{:S(2)}, u32[]{:S(2)}) %collective-permute-start.3) | collective-permute-done | bytes 131104 | tf_op jit(solution)/shard_map/ppermute | solution.py:350
  37.5 3.2 %collective-permute-start.6 = (bf16[512,128]{1,0:T(8,128)(2,1)S(1)}, bf16[512,128]{1,0:T(8,128)(2,1)S(1)}, u32[]{:S(2)}, u32[]{:S(2)}) collective-permute-start(bf16[512,128]{1,0:T(8,128)(2,1)S(1)} %collective-permute-done.4.refs_5_), channel_id=1, source_target_pairs={{0,14},{2,0},{4,2},{6,4},{8,6},{10,8},{12,10},{14,12},{1,15},{3,1}... | collective-permute-start | bytes 393224 | tf_op jit(solution)/shard_map/ppermute | solution.py:351
  44.5 1.8 %collective-permute-done.9.refs_10_ = bf16[2,512,128]{2,1,0:T(8,128)(2,1)} collective-permute-done((bf16[2,512,128]{2,1,0:T(8,128)(2,1)}, bf16[2,512,128]{2,1,0:T(8,128)(2,1)}, u32[]{:S(2)}, u32[]{:S(2)}) %collective-permute-start.9) | collective-permute-done | bytes 262176 | tf_op jit(solution)/shard_map/ppermute | solution.py:354
  46.3 6.5 %all-to-all-done.asked_ref.grad_ref = bf16[16,400,128]{2,1,0:T(8,128)(2,1)S(1)} async-done(((bf16[16,400,128]{2,1,0:T(8,128)(2,1)}), bf16[16,400,128]{2,1,0:T(8,128)(2,1)S(1)}, u32[]{:S(2)}, u32[]{:S(2)}) %all-to-all-start) | async-done | bytes 1638432 | tf_op jit(solution)/shard_map/all_to_all | solution.py:397
  52.8 6.1 %shard_map.204 = (bf16[16,8,48,128]{3,2,1,0:T(8,128)(2,1)}, s32[128,128]{1,0:T(8,128)S(1)}) custom-call(s32[2]{0:T(128)S(1)} %pad_add_fusion.z_ref, bf16[16,400,128]{2,1,0:T(8,128)(2,1)S(1)} %all-to-all-done.asked_ref.grad_ref, bf16[512,128]{1,0:T(8,128)(2,1)S(1)} %get-tuple-element.32.refs_0_, bf16[512,128]{1,0:T(8,128)(2,1)S(1)} %get-tuple-element.31.refs_1_, ...), custom_call_target="tpu_custom_call" | custom-call | tf_op jit(solution)/shard_map/pallas_call | solution.py:400
  58.9 6.0 %all-to-all-start.1 = ((bf16[16,8,48,128]{3,2,1,0:T(8,128)(2,1)}), bf16[16,8,48,128]{3,2,1,0:T(8,128)(2,1)S(1)}, u32[]{:S(2)}, u32[]{:S(2)}) async-start(bf16[16,8,48,128]{3,2,1,0:T(8,128)(2,1)} %get-tuple-element.18.refs_0_.refs_1_), calls=%async_computation.1 | async-start | bytes 3145728 | tf_op jit(solution)/shard_map/all_to_all | solution.py:422
  68.4 3.7 %shard_map.205.refs_7_ = f32[8,512,128]{2,1,0:T(8,128)} custom-call(s32[2]{0:T(128)S(1)} %pad_add_fusion.1.at_ref, s32[8,1,768]{2,1,0:T(1,128)S(1)} %reshape.56.rows_ref, bf16[16,400,128]{2,1,0:T(8,128)(2,1)S(1)} %all-to-all-done.asked_ref.grad_ref, bf16[16,8,48,128]{3,2,1,0:T(8,128)(2,1)} %get-tuple-element.18.refs_0_.refs_1_), custom_call_target="tpu_custom_call" | custom-call | tf_op jit(solution)/shard_map/pallas_call | solution.py:432
  72.1 14.3 %all-to-all-done.1.refs_1_ = bf16[16,8,48,128]{3,2,1,0:T(8,128)(2,1)S(1)} async-done(((bf16[16,8,48,128]{3,2,1,0:T(8,128)(2,1)}), bf16[16,8,48,128]{3,2,1,0:T(8,128)(2,1)S(1)}, u32[]{:S(2)}, u32[]{:S(2)}) %all-to-all-start.1) | async-done | bytes 1572896 | tf_op jit(solution)/shard_map/all_to_all | solution.py:422
  86.4 7.7 %shard_map.206 = (bf16[256,640]{1,0:T(8,128)(2,1)S(1)}, bf16[256,4096]{1,0:T(8,128)(2,1)S(1)}) custom-call(s32[2,1,3072]{2,1,0:T(1,128)S(1)} %reshape.61.refs_0_, bf16[16,8,48,128]{3,2,1,0:T(8,128)(2,1)S(1)} %all-to-all-done.1.refs_1_, bf16[256,128]{1,0:T(8,128)(2,1)S(1)} %fusion.6.refs_2_, f32[8,1,512]{2,1,0:T(1,128)S(1)} %bitcast.68, ...), custom_call_target="tpu_custom_call" | custom-call | tf_op jit(solution)/shard_map/pallas_call | solution.py:450
  94.4 1.6 shard_map.209
  96.6 4.9 %collective-permute-done.11.refs_0_ = bf16[16,320,256]{2,1,0:T(8,128)(2,1)S(1)} collective-permute-done((bf16[16,320,256]{2,1,0:T(8,128)(2,1)S(1)}, bf16[16,320,256]{2,1,0:T(8,128)(2,1)S(1)}, u32[]{:S(2)}, u32[]{:S(2)}) %collective-permute-start.11) | collective-permute-done | bytes 2621472 | tf_op jit(solution)/shard_map/ppermute | solution.py:497
  101.6 1.6 shard_map.210.refs_1_
  104.7 6.6 %all-to-all-start.2 = ((bf16[16,320,256]{2,1,0:T(8,128)(2,1)}), bf16[16,320,256]{2,1,0:T(8,128)(2,1)}, u32[]{:S(2)}, u32[]{:S(2)}) async-start(bf16[16,320,256]{2,1,0:T(8,128)(2,1)} %copy-done.1), calls=%async_computation.2 | async-start | bytes 5242880 | tf_op jit(solution)/shard_map/all_to_all | solution.py:499
  111.4 3.6 %shard_map.208.refs_0_ = bf16[8,512,128]{2,1,0:T(8,128)(2,1)S(1)} custom-call(s32[2]{0:T(128)S(1)} %pad_add_fusion.2.at_ref, s32[8,1,768]{2,1,0:T(1,128)S(1)} %reshape.56.rows_ref, bf16[16,400,128]{2,1,0:T(8,128)(2,1)S(1)} %all-to-all-done.asked_ref.grad_ref, f32[8,512,128]{2,1,0:T(8,128)} %collective-permute-done.10.refs_0_, ...), custom_call_target="tpu_custom_call" | custom-call | tf_op jit(solution)/shard_map/pallas_call | solution.py:432
  117.3 4.5 %collective-permute-start.16 = (bf16[512,128]{1,0:T(8,128)(2,1)S(1)}, bf16[512,128]{1,0:T(8,128)(2,1)S(1)}, u32[]{:S(2)}, u32[]{:S(2)}) collective-permute-start(bf16[512,128]{1,0:T(8,128)(2,1)S(1)} %get-tuple-element.27), channel_id=1, source_target_pairs={{0,10},{2,12},{4,14},{6,0},{8,2},{10,4},{12,6},{14,8},{1,11},{3,13... | collective-permute-start | bytes 393224 | tf_op jit(solution)/shard_map/ppermute | solution.py:501
  121.8 3.1 %collective-permute-start.15 = (bf16[512,128]{1,0:T(8,128)(2,1)S(1)}, bf16[512,128]{1,0:T(8,128)(2,1)S(1)}, u32[]{:S(2)}, u32[]{:S(2)}) collective-permute-start(bf16[512,128]{1,0:T(8,128)(2,1)S(1)} %get-tuple-element.28), channel_id=1, source_target_pairs={{0,8},{2,10},{4,12},{6,14},{8,0},{10,2},{12,4},{14,6},{1,9},{3,11}... | collective-permute-start | bytes 393224 | tf_op jit(solution)/shard_map/ppermute | solution.py:501
  124.9 2.3 %collective-permute-start.13 = (bf16[512,128]{1,0:T(8,128)(2,1)S(1)}, bf16[512,128]{1,0:T(8,128)(2,1)S(1)}, u32[]{:S(2)}, u32[]{:S(2)}) collective-permute-start(bf16[512,128]{1,0:T(8,128)(2,1)S(1)} %get-tuple-element.30), channel_id=1, source_target_pairs={{0,4},{2,6},{4,8},{6,10},{8,12},{10,14},{12,0},{14,2},{1,5},{3,7},... | collective-permute-start | bytes 393224 | tf_op jit(solution)/shard_map/ppermute | solution.py:501
  127.2 1.6 fusion.back_ref
  128.8 1.9 %shard_map.207.refs_1_ = bf16[2,1,1536,128]{3,2,1,0:T(8,128)(2,1)} custom-call(s32[2,1,1536]{2,1,0:T(1,128)S(1)} %get-tuple-element.13.bag_ref, f32[256,512]{1,0:T(8,128)S(1)} %fusion.back_ref), custom_call_target="tpu_custom_call" | custom-call | tf_op jit(solution)/shard_map/pallas_call | solution.py:475
  131.9 1.8 %collective-permute-done.16 = bf16[512,128]{1,0:T(8,128)(2,1)S(1)} collective-permute-done((bf16[512,128]{1,0:T(8,128)(2,1)S(1)}, bf16[512,128]{1,0:T(8,128)(2,1)S(1)}, u32[]{:S(2)}, u32[]{:S(2)}) %collective-permute-start.16) | collective-permute-done | bytes 131104 | tf_op jit(solution)/shard_map/ppermute | solution.py:501
  135.1 9.5 %collective-permute-done.14 = bf16[512,128]{1,0:T(8,128)(2,1)S(1)} collective-permute-done((bf16[512,128]{1,0:T(8,128)(2,1)S(1)}, bf16[512,128]{1,0:T(8,128)(2,1)S(1)}, u32[]{:S(2)}, u32[]{:S(2)}) %collective-permute-start.14) | collective-permute-done | bytes 131104 | tf_op jit(solution)/shard_map/ppermute | solution.py:501
  144.9 6.5 %all-to-all-done.2 = bf16[16,320,256]{2,1,0:T(8,128)(2,1)} async-done(((bf16[16,320,256]{2,1,0:T(8,128)(2,1)}), bf16[16,320,256]{2,1,0:T(8,128)(2,1)}, u32[]{:S(2)}, u32[]{:S(2)}) %all-to-all-start.2) | async-done | bytes 2621472 | tf_op jit(solution)/shard_map/all_to_all | solution.py:499
  151.4 2.1 %reduce_sum.21 = bf16[320,256]{1,0:T(8,128)(2,1)S(1)} reduce(bf16[16,320,256]{2,1,0:T(8,128)(2,1)} %all-to-all-done.2, bf16[]{:T(256)} %constant.33.clone.1), dimensions={0}, to_apply=%region_0.1 | reduce | flops 1228800 | bytes 2785282 | tf_op jit(solution)/shard_map/reduce_sum | solution.py:515
  154.3 3.5 %all-to-all-start.3 = ((bf16[8,32,320]{2,1,0:T(8,128)(2,1)}), bf16[8,32,320]{2,1,0:T(8,128)(2,1)S(1)}, u32[]{:S(2)}, u32[]{:S(2)}) async-start(bf16[8,32,320]{2,1,0:T(8,128)(2,1)} %shard_map.213), calls=%async_computation.3 | async-start | bytes 393216 | tf_op jit(solution)/shard_map/all_to_all | solution.py:517
  159.0 9.0 %all-to-all-done.3 = bf16[8,32,320]{2,1,0:T(8,128)(2,1)S(1)} async-done(((bf16[8,32,320]{2,1,0:T(8,128)(2,1)}), bf16[8,32,320]{2,1,0:T(8,128)(2,1)S(1)}, u32[]{:S(2)}, u32[]{:S(2)}) %all-to-all-start.3) | async-done | bytes 163872 | tf_op jit(solution)/shard_map/all_to_all | solution.py:517
  (84 shorter events, 19.5 us)
Async XLA Ops:
  0.6 66.2 %copy-start = (bf16[512,128]{1,0:T(8,128)(2,1)S(1)}, bf16[512,128]{1,0:T(8,128)(2,1)}, u32[]{:S(2)}) copy-start(bf16[512,128]{1,0:T(8,128)(2,1)} %param.31) | copy-start | bytes 393220
  1.8 22.1 %collective-permute-start = (bf16[512,128]{1,0:T(8,128)(2,1)S(1)}, bf16[512,128]{1,0:T(8,128)(2,1)S(1)}, u32[]{:S(2)}, u32[]{:S(2)}) collective-permute-start(bf16[512,128]{1,0:T(8,128)(2,1)S(1)} %get-tuple-element.32.refs_0_), channel_id=1, source_target_pairs={{0,2},{2,4},{4,6},{6,8},{8,10},{10,12},{12,14},{14,0},{1,3},{3,5},... | collective-permute-start | bytes 393224 | tf_op jit(solution)/shard_map/ppermute | solution.py:350
  3.8 20.1 %collective-permute-start.1 = (bf16[512,128]{1,0:T(8,128)(2,1)S(1)}, bf16[512,128]{1,0:T(8,128)(2,1)S(1)}, u32[]{:S(2)}, u32[]{:S(2)}) collective-permute-start(bf16[512,128]{1,0:T(8,128)(2,1)S(1)} %get-tuple-element.32.refs_0_), channel_id=1, source_target_pairs={{0,14},{2,0},{4,2},{6,4},{8,6},{10,8},{12,10},{14,12},{1,15},{3,1}... | collective-permute-start | bytes 393224 | tf_op jit(solution)/shard_map/ppermute | solution.py:351
  7.8 16.1 %collective-permute-start.2 = (bf16[512,128]{1,0:T(8,128)(2,1)S(1)}, bf16[512,128]{1,0:T(8,128)(2,1)S(1)}, u32[]{:S(2)}, u32[]{:S(2)}) collective-permute-start(bf16[512,128]{1,0:T(8,128)(2,1)S(1)} %get-tuple-element.32.refs_0_), channel_id=1, source_target_pairs={{0,8},{2,10},{4,12},{6,14},{8,0},{10,2},{12,4},{14,6},{1,9},{3,11}... | collective-permute-start | bytes 393224 | tf_op jit(solution)/shard_map/ppermute | solution.py:353
  23.9 28.9 %all-to-all-start = ((bf16[16,400,128]{2,1,0:T(8,128)(2,1)}), bf16[16,400,128]{2,1,0:T(8,128)(2,1)S(1)}, u32[]{:S(2)}, u32[]{:S(2)}) async-start(bf16[16,400,128]{2,1,0:T(8,128)(2,1)} %shard_map.203), calls=%async_computation | async-start | bytes 3276800 | tf_op jit(solution)/shard_map/all_to_all | solution.py:397
  31.3 6.2 %collective-permute-start.3 = (bf16[512,128]{1,0:T(8,128)(2,1)S(1)}, bf16[512,128]{1,0:T(8,128)(2,1)S(1)}, u32[]{:S(2)}, u32[]{:S(2)}) collective-permute-start(bf16[512,128]{1,0:T(8,128)(2,1)S(1)} %collective-permute-done.refs_1_.refs_2_), channel_id=1, source_target_pairs={{0,2},{2,4},{4,6},{6,8},{8,10},{10,12},{12,14},{14,0},{1,3},{3,5},... | collective-permute-start | bytes 393224 | tf_op jit(solution)/shard_map/ppermute | solution.py:350
  31.3 6.2 %collective-permute-start.4 = (bf16[512,128]{1,0:T(8,128)(2,1)S(1)}, bf16[512,128]{1,0:T(8,128)(2,1)S(1)}, u32[]{:S(2)}, u32[]{:S(2)}) collective-permute-start(bf16[512,128]{1,0:T(8,128)(2,1)S(1)} %collective-permute-done.1.refs_2_.refs_3_), channel_id=1, source_target_pairs={{0,14},{2,0},{4,2},{6,4},{8,6},{10,8},{12,10},{14,12},{1,15},{3,1}... | collective-permute-start | bytes 393224 | tf_op jit(solution)/shard_map/ppermute | solution.py:351
  37.5 6.2 %collective-permute-start.5 = (bf16[512,128]{1,0:T(8,128)(2,1)S(1)}, bf16[512,128]{1,0:T(8,128)(2,1)S(1)}, u32[]{:S(2)}, u32[]{:S(2)}) collective-permute-start(bf16[512,128]{1,0:T(8,128)(2,1)S(1)} %collective-permute-done.3.refs_4_), channel_id=1, source_target_pairs={{0,2},{2,4},{4,6},{6,8},{8,10},{10,12},{12,14},{14,0},{1,3},{3,5},... | collective-permute-start | bytes 393224 | tf_op jit(solution)/shard_map/ppermute | solution.py:350
  37.5 6.2 %collective-permute-start.6 = (bf16[512,128]{1,0:T(8,128)(2,1)S(1)}, bf16[512,128]{1,0:T(8,128)(2,1)S(1)}, u32[]{:S(2)}, u32[]{:S(2)}) collective-permute-start(bf16[512,128]{1,0:T(8,128)(2,1)S(1)} %collective-permute-done.4.refs_5_), channel_id=1, source_target_pairs={{0,14},{2,0},{4,2},{6,4},{8,6},{10,8},{12,10},{14,12},{1,15},{3,1}... | collective-permute-start | bytes 393224 | tf_op jit(solution)/shard_map/ppermute | solution.py:351
  41.5 3.0 %collective-permute-start.7 = (bf16[3,512,128]{2,1,0:T(8,128)(2,1)}, bf16[3,512,128]{2,1,0:T(8,128)(2,1)S(1)}, u32[]{:S(2)}, u32[]{:S(2)}) collective-permute-start(bf16[3,512,128]{2,1,0:T(8,128)(2,1)} %pad_maximum_fusion), channel_id=1, source_target_pairs={{0,1},{1,0},{2,3},{3,2},{4,5},{5,4},{6,7},{7,6},{8,9},{9,8},{10,11... | collective-permute-start | bytes 1179656 | tf_op jit(solution)/shard_map/ppermute | solution.py:354
  42.3 2.2 %collective-permute-start.8 = (bf16[2,512,128]{2,1,0:T(8,128)(2,1)}, bf16[2,512,128]{2,1,0:T(8,128)(2,1)}, u32[]{:S(2)}, u32[]{:S(2)}) collective-permute-start(bf16[2,512,128]{2,1,0:T(8,128)(2,1)} %pad_maximum_fusion.1), channel_id=1, source_target_pairs={{0,1},{1,0},{2,3},{3,2},{4,5},{5,4},{6,7},{7,6},{8,9},{9,8},{10,11... | collective-permute-start | bytes 786440 | tf_op jit(solution)/shard_map/ppermute | solution.py:354
  44.4 1.9 %collective-permute-start.9 = (bf16[2,512,128]{2,1,0:T(8,128)(2,1)}, bf16[2,512,128]{2,1,0:T(8,128)(2,1)}, u32[]{:S(2)}, u32[]{:S(2)}) collective-permute-start(bf16[2,512,128]{2,1,0:T(8,128)(2,1)} %pad_maximum_fusion.2), channel_id=1, source_target_pairs={{0,1},{1,0},{2,3},{3,2},{4,5},{5,4},{6,7},{7,6},{8,9},{9,8},{10,11... | collective-permute-start | bytes 786440 | tf_op jit(solution)/shard_map/ppermute | solution.py:354
  58.9 27.5 %all-to-all-start.1 = ((bf16[16,8,48,128]{3,2,1,0:T(8,128)(2,1)}), bf16[16,8,48,128]{3,2,1,0:T(8,128)(2,1)S(1)}, u32[]{:S(2)}, u32[]{:S(2)}) async-start(bf16[16,8,48,128]{3,2,1,0:T(8,128)(2,1)} %get-tuple-element.18.refs_0_.refs_1_), calls=%async_computation.1 | async-start | bytes 3145728 | tf_op jit(solution)/shard_map/all_to_all | solution.py:422
  68.3 18.1 %copy-start.7 = (f32[4096]{0:T(1024)S(1)}, f32[4096]{0:T(1024)}, u32[]{:S(2)}) copy-start(f32[4096]{0:T(1024)} %param.33) | copy-start | bytes 49156
  68.4 18.1 %copy-start.8 = (s32[2,128]{1,0:T(2,128)S(1)}, s32[2,128]{1,0:T(2,128)}, u32[]{:S(2)}) copy-start(s32[2,128]{1,0:T(2,128)} %refs_5_.3) | copy-start | bytes 3076
  96.0 5.5 %collective-permute-start.11 = (bf16[16,320,256]{2,1,0:T(8,128)(2,1)S(1)}, bf16[16,320,256]{2,1,0:T(8,128)(2,1)S(1)}, u32[]{:S(2)}, u32[]{:S(2)}) collective-permute-start(bf16[16,320,256]{2,1,0:T(8,128)(2,1)S(1)} %shard_map.209), channel_id=1, source_target_pairs={{0,1},{1,0},{2,3},{3,2},{4,5},{5,4},{6,7},{7,6},{8,9},{9,8},{10,11... | collective-permute-start | bytes 7864328 | tf_op jit(solution)/shard_map/ppermute | solution.py:497
  96.1 15.3 %collective-permute-start.10 = (f32[8,512,128]{2,1,0:T(8,128)}, f32[8,512,128]{2,1,0:T(8,128)}, u32[]{:S(2)}, u32[]{:S(2)}) collective-permute-start(f32[8,512,128]{2,1,0:T(8,128)} %shard_map.205.refs_7_), channel_id=1, source_target_pairs={{0,1},{1,0},{2,3},{3,2},{4,5},{5,4},{6,7},{7,6},{8,9},{9,8},{10,11... | collective-permute-start | bytes 6291464 | tf_op jit(solution)/shard_map/ppermute | solution.py:442
  104.7 22.5 %slice-start = ((s8[5242880]{0:T(1024)(128)(4,1)}), s8[1048576]{0:T(1024)(128)(4,1)S(1)}, s32[]{:S(2)}) async-start(s8[5242880]{0:T(1024)(128)(4,1)} %bitcast.69), calls=%async_computation.4 | async-start | bytes 2097152
  104.7 46.7 %all-to-all-start.2 = ((bf16[16,320,256]{2,1,0:T(8,128)(2,1)}), bf16[16,320,256]{2,1,0:T(8,128)(2,1)}, u32[]{:S(2)}, u32[]{:S(2)}) async-start(bf16[16,320,256]{2,1,0:T(8,128)(2,1)} %copy-done.1), calls=%async_computation.2 | async-start | bytes 5242880 | tf_op jit(solution)/shard_map/all_to_all | solution.py:499
  111.4 15.8 %slice-start.1 = ((s8[5242880]{0:T(1024)(128)(4,1)}), s8[4194304]{0:T(1024)(128)(4,1)S(1)}, s32[]{:S(2)}) async-start(s8[5242880]{0:T(1024)(128)(4,1)} %bitcast.69), calls=%async_computation.5 | async-start | bytes 8388608
  115.1 9.9 %collective-permute-start.18 = (bf16[512,128]{1,0:T(8,128)(2,1)S(1)}, bf16[512,128]{1,0:T(8,128)(2,1)S(1)}, u32[]{:S(2)}, u32[]{:S(2)}) collective-permute-start(bf16[512,128]{1,0:T(8,128)(2,1)S(1)} %get-tuple-element.25), channel_id=1, source_target_pairs={{0,14},{2,0},{4,2},{6,4},{8,6},{10,8},{12,10},{14,12},{1,15},{3,1}... | collective-permute-start | bytes 393224 | tf_op jit(solution)/shard_map/ppermute | solution.py:501
  115.8 9.2 %collective-permute-start.12 = (bf16[512,128]{1,0:T(8,128)(2,1)S(1)}, bf16[512,128]{1,0:T(8,128)(2,1)S(1)}, u32[]{:S(2)}, u32[]{:S(2)}) collective-permute-start(bf16[512,128]{1,0:T(8,128)(2,1)S(1)} %get-tuple-element.24), channel_id=1, source_target_pairs={{0,2},{2,4},{4,6},{6,8},{8,10},{10,12},{12,14},{14,0},{1,3},{3,5},... | collective-permute-start | bytes 393224 | tf_op jit(solution)/shard_map/ppermute | solution.py:501
  117.2 14.7 %collective-permute-start.17 = (bf16[512,128]{1,0:T(8,128)(2,1)S(1)}, bf16[512,128]{1,0:T(8,128)(2,1)S(1)}, u32[]{:S(2)}, u32[]{:S(2)}) collective-permute-start(bf16[512,128]{1,0:T(8,128)(2,1)S(1)} %get-tuple-element.26), channel_id=1, source_target_pairs={{0,12},{2,14},{4,0},{6,2},{8,4},{10,6},{12,8},{14,10},{1,13},{3,15... | collective-permute-start | bytes 393224 | tf_op jit(solution)/shard_map/ppermute | solution.py:501
  117.3 16.4 %collective-permute-start.16 = (bf16[512,128]{1,0:T(8,128)(2,1)S(1)}, bf16[512,128]{1,0:T(8,128)(2,1)S(1)}, u32[]{:S(2)}, u32[]{:S(2)}) collective-permute-start(bf16[512,128]{1,0:T(8,128)(2,1)S(1)} %get-tuple-element.27), channel_id=1, source_target_pairs={{0,10},{2,12},{4,14},{6,0},{8,2},{10,4},{12,6},{14,8},{1,11},{3,13... | collective-permute-start | bytes 393224 | tf_op jit(solution)/shard_map/ppermute | solution.py:501
  121.8 13.3 %collective-permute-start.15 = (bf16[512,128]{1,0:T(8,128)(2,1)S(1)}, bf16[512,128]{1,0:T(8,128)(2,1)S(1)}, u32[]{:S(2)}, u32[]{:S(2)}) collective-permute-start(bf16[512,128]{1,0:T(8,128)(2,1)S(1)} %get-tuple-element.28), channel_id=1, source_target_pairs={{0,8},{2,10},{4,12},{6,14},{8,0},{10,2},{12,4},{14,6},{1,9},{3,11}... | collective-permute-start | bytes 393224 | tf_op jit(solution)/shard_map/ppermute | solution.py:501
  124.9 19.7 %collective-permute-start.14 = (bf16[512,128]{1,0:T(8,128)(2,1)S(1)}, bf16[512,128]{1,0:T(8,128)(2,1)S(1)}, u32[]{:S(2)}, u32[]{:S(2)}) collective-permute-start(bf16[512,128]{1,0:T(8,128)(2,1)S(1)} %get-tuple-element.29), channel_id=1, source_target_pairs={{0,6},{2,8},{4,10},{6,12},{8,14},{10,0},{12,2},{14,4},{1,7},{3,9},... | collective-permute-start | bytes 393224 | tf_op jit(solution)/shard_map/ppermute | solution.py:501
  124.9 19.6 %collective-permute-start.13 = (bf16[512,128]{1,0:T(8,128)(2,1)S(1)}, bf16[512,128]{1,0:T(8,128)(2,1)S(1)}, u32[]{:S(2)}, u32[]{:S(2)}) collective-permute-start(bf16[512,128]{1,0:T(8,128)(2,1)S(1)} %get-tuple-element.30), channel_id=1, source_target_pairs={{0,4},{2,6},{4,8},{6,10},{8,12},{10,14},{12,0},{14,2},{1,5},{3,7},... | collective-permute-start | bytes 393224 | tf_op jit(solution)/shard_map/ppermute | solution.py:501
  144.7 13.1 %copy-start.9 = (f32[1024,128]{1,0:T(8,128)S(1)}, f32[1024,128]{1,0:T(8,128)}, u32[]{:S(2)}) copy-start(f32[1024,128]{1,0:T(8,128)} %param.27) | copy-start | bytes 1572868
  144.7 13.1 %copy-start.10 = (f32[1024,128]{1,0:T(8,128)S(1)}, f32[1024,128]{1,0:T(8,128)}, u32[]{:S(2)}) copy-start(f32[1024,128]{1,0:T(8,128)} %param.28) | copy-start | bytes 1572868
  144.8 13.1 %collective-permute-start.19 = (f32[512,128]{1,0:T(8,128)S(1)}, f32[512,128]{1,0:T(8,128)S(1)}, u32[]{:S(2)}, u32[]{:S(2)}) collective-permute-start(f32[512,128]{1,0:T(8,128)S(1)} %fusion.12), channel_id=1, source_target_pairs={{0,1},{1,0},{2,3},{3,2},{4,5},{5,4},{6,7},{7,6},{8,9},{9,8},{10,11... | collective-permute-start | bytes 786440 | tf_op jit(solution)/shard_map/ppermute | solution.py:506
  154.3 13.7 %copy-start.11 = (f32[320,32]{0,1:T(8,128)S(1)}, f32[320,32]{0,1:T(8,128)}, u32[]{:S(2)}) copy-start(f32[320,32]{0,1:T(8,128)} %param.35) | copy-start | bytes 122884
  154.3 13.7 %all-to-all-start.3 = ((bf16[8,32,320]{2,1,0:T(8,128)(2,1)}), bf16[8,32,320]{2,1,0:T(8,128)(2,1)S(1)}, u32[]{:S(2)}, u32[]{:S(2)}) async-start(bf16[8,32,320]{2,1,0:T(8,128)(2,1)} %shard_map.213), calls=%async_computation.3 | async-start | bytes 393216 | tf_op jit(solution)/shard_map/all_to_all | solution.py:517
  (7 other events, 34.9 us)

commit v5 on v4

--- a/solution.py
+++ b/solution.py
@@ -499,7 +499,9 @@
     unit_part = lax.all_to_all(unit_part, "w", split_axis=0, concat_axis=0, tiled=True)
 
     arrived = [lax.ppermute(ours[shift], "z", ring_of(ring, shift)) for shift in range(1, ring)]
-    arrived[0] = tie(arrived[0], row_grads)
+    unit_part = jnp.sum(unit_part.astype(F32), axis=0).T.astype(BF).reshape(ring, units, inputs)
+    unit_part = tie(unit_part, row_grads)
+    arrived[0] = tie(arrived[0], unit_part)
     half_sum = ours[0].astype(F32)
     for part in arrived:
         half_sum += part.astype(F32)
@@ -512,8 +514,6 @@
     new_squares = grad_squares + row_sum * row_sum
     new_table = emb_table - LEARN_RATE * row_sum * lax.rsqrt(new_squares)
 
-    unit_part = jnp.sum(unit_part.astype(F32), axis=0).T.astype(BF).reshape(ring, units, inputs)
-    unit_part = tie(unit_part, row_grads)
     unit_part = lax.all_to_all(unit_part, "z", split_axis=0, concat_axis=0, tiled=True)
     top_grad = jnp.sum(unit_part.astype(F32), axis=0).T
     top_step = top_grad * lax.rsqrt(top_squares + top_grad * top_grad)

time: 169 us -> 174 us (1.030); the launches traced: 169 us -> 171 us
  matrix products: 2.87 us -> 5.06 us
    ppermute x7, waiting for transfers between devices: 12.7 us -> 0.02 us  [per_device(): lax.ppermute(ours[shift], 'z', ring_of(ring, shift))]
    all_to_all x1, waiting for transfers between devices: 6.54 us -> 17.8 us  [per_device(): lax.all_to_all(unit_part, 'w', split_axis=0, concat_axis=0, tiled=True)]
    dot_general x1, matrix products: 1.62 us -> 3.81 us  [nt(): lax.dot_general(a, b, (((1,), (1,)), ((), ())), preferred_element_type=F32)]
    unnamed x30 -> x28, local copies, waits for them, and re-layouts: 3.84 us -> 2.7 us
  transfers between devices with their start and end apart: 24 -> 24, of which waited for: 11 -> 8; matrix products, arithmetic and copies ran while one was open for 7% -> 8% of each run, Pallas kernels for 13% -> 12%
where the time goes in v5:
time: 174 us; the launch traced here: 171 us
  waiting for transfers between devices  59.5 us (34%)
  starting transfers between devices  53.5 us (31%)
  Pallas kernels  36.7 us (21%)
  local copies, waits for them, and re-layouts  7.69 us (4%)
  other arithmetic  7.68 us (4%)
  matrix products  5.06 us (3%)
    all_to_all x1, waiting for transfers between devices, per_device(): lax.all_to_all(unit_part, 'w', split_axis=0, concat_axis=0, tiled=True)  17.8 us
    all_to_all x1, waiting for transfers between devices, per_device(): lax.all_to_all(replies, 'w', split_axis=0, concat_axis=0, tiled=True)  14.4 us
    ppermute x7, starting transfers between devices, per_device(): lax.ppermute(ours[shift], 'z', ring_of(ring, shift))  12 us
    ppermute x3, starting transfers between devices, per_device(): back = lax.ppermute(back, 'z', ring_of(ring, -1))  10.5 us
    all_to_all x1, waiting for transfers between devices, per_device(): lax.all_to_all(unit_part, 'z', split_axis=0, concat_axis=0, tiled=True)  10.2 us
    pallas_call x1, Pallas kernels, per_device(): call(dense_body, (shape_of((2 * samples, top_weight.shape[0]), BF), shape...  7.72 us
    all_to_all x1, starting transfers between devices, per_device(): lax.all_to_all(outgoing, 'w', split_axis=0, concat_axis=0, tiled=True)  7.4 us
    pallas_call x2, Pallas kernels, scatter(): call(scatter_body, shape_of((ring, half_rows, width), dtype), vmem=10 * 1...  7.27 us
  transfers between devices with their start and end apart: 24, of which 8 were waited for; matrix products, arithmetic and copies ran while one was open for 8% of the time, Pallas kernels for 12%

profile of v5, /device:TPU:8, one launch (start us, length us, event | category | flops | bytes accessed | tf_op | source)
XLA Modules:
  0.0 171.1 jit_solution(16324444568498561814)
XLA Ops:
  1.8 2.0 %collective-permute-start = (bf16[512,128]{1,0:T(8,128)(2,1)S(1)}, bf16[512,128]{1,0:T(8,128)(2,1)S(1)}, u32[]{:S(2)}, u32[]{:S(2)}) collective-permute-start(bf16[512,128]{1,0:T(8,128)(2,1)S(1)} %get-tuple-element.32.refs_0_), channel_id=1, source_target_pairs={{0,2},{2,4},{4,6},{6,8},{8,10},{10,12},{12,14},{14,0},{1,3},{3,5},... | collective-permute-start | bytes 393224 | tf_op jit(solution)/shard_map/ppermute | solution.py:350
  3.8 4.0 %collective-permute-start.1 = (bf16[512,128]{1,0:T(8,128)(2,1)S(1)}, bf16[512,128]{1,0:T(8,128)(2,1)S(1)}, u32[]{:S(2)}, u32[]{:S(2)}) collective-permute-start(bf16[512,128]{1,0:T(8,128)(2,1)S(1)} %get-tuple-element.32.refs_0_), channel_id=1, source_target_pairs={{0,14},{2,0},{4,2},{6,4},{8,6},{10,8},{12,10},{14,12},{1,15},{3,1}... | collective-permute-start | bytes 393224 | tf_op jit(solution)/shard_map/ppermute | solution.py:351
  7.8 4.5 %collective-permute-start.2 = (bf16[512,128]{1,0:T(8,128)(2,1)S(1)}, bf16[512,128]{1,0:T(8,128)(2,1)S(1)}, u32[]{:S(2)}, u32[]{:S(2)}) collective-permute-start(bf16[512,128]{1,0:T(8,128)(2,1)S(1)} %get-tuple-element.32.refs_0_), channel_id=1, source_target_pairs={{0,8},{2,10},{4,12},{6,14},{8,0},{10,2},{12,4},{14,6},{1,9},{3,11}... | collective-permute-start | bytes 393224 | tf_op jit(solution)/shard_map/ppermute | solution.py:353
  12.3 4.2 %shard_map.201 = (f32[128,128]{1,0:T(8,128)S(1)}, f32[128,128]{1,0:T(8,128)S(1)}, s32[128,128]{1,0:T(8,128)S(1)}, s32[2,1,1536]{2,1,0:T(1,128)S(1)}, s32[2,1,1536]{2,1,0:T(1,128)S(1)}) custom-call(s32[2,1,1536]{2,1,0:T(1,128)} %bitcast.72, s32[2,1,1536]{2,1,0:T(1,128)} %bitcast.73, s32[2,1,1536]{2,1,0:T(1,128)} %refs_2_.1, s32[2,1,1536]{2,1,0:T(1,128)} %refs_3_.1, ...), custom_call_target="tpu_custom_call" | custom-call | tf_op jit(solution)/shard_map/pallas_call | solution.py:358
  17.6 6.3 %shard_map.202.refs_0_ = bf16[16,400,128]{2,1,0:T(8,128)(2,1)} custom-call(s32[2,1,1536]{2,1,0:T(1,128)S(1)} %get-tuple-element.15.pos_ref, bf16[2,1536,128]{2,1,0:T(8,128)(2,1)S(1)} %bitcast.61, f32[128,128]{1,0:T(8,128)S(1)} %get-tuple-element.16.high_ref, f32[128,128]{1,0:T(8,128)S(1)} %get-tuple-element.17.low_ref), custom_call_target="tpu_custom_call" | custom-call | tf_op jit(solution)/shard_map/pallas_call | solution.py:382
  23.9 7.4 %all-to-all-start = ((bf16[16,400,128]{2,1,0:T(8,128)(2,1)}), bf16[16,400,128]{2,1,0:T(8,128)(2,1)S(1)}, u32[]{:S(2)}, u32[]{:S(2)}) async-start(bf16[16,400,128]{2,1,0:T(8,128)(2,1)} %shard_map.203), calls=%async_computation | async-start | bytes 3276800 | tf_op jit(solution)/shard_map/all_to_all | solution.py:397
  31.3 3.2 %collective-permute-start.4 = (bf16[512,128]{1,0:T(8,128)(2,1)S(1)}, bf16[512,128]{1,0:T(8,128)(2,1)S(1)}, u32[]{:S(2)}, u32[]{:S(2)}) collective-permute-start(bf16[512,128]{1,0:T(8,128)(2,1)S(1)} %collective-permute-done.1.refs_2_.refs_3_), channel_id=1, source_target_pairs={{0,14},{2,0},{4,2},{6,4},{8,6},{10,8},{12,10},{14,12},{1,15},{3,1}... | collective-permute-start | bytes 393224 | tf_op jit(solution)/shard_map/ppermute | solution.py:351
  34.5 2.9 %collective-permute-done.3.refs_4_ = bf16[512,128]{1,0:T(8,128)(2,1)S(1)} collective-permute-done((bf16[512,128]{1,0:T(8,128)(2,1)S(1)}, bf16[512,128]{1,0:T(8,128)(2,1)S(1)}, u32[]{:S(2)}, u32[]{:S(2)}) %collective-permute-start.3) | collective-permute-done | bytes 131104 | tf_op jit(solution)/shard_map/ppermute | solution.py:350
  37.5 3.2 %collective-permute-start.6 = (bf16[512,128]{1,0:T(8,128)(2,1)S(1)}, bf16[512,128]{1,0:T(8,128)(2,1)S(1)}, u32[]{:S(2)}, u32[]{:S(2)}) collective-permute-start(bf16[512,128]{1,0:T(8,128)(2,1)S(1)} %collective-permute-done.4.refs_5_), channel_id=1, source_target_pairs={{0,14},{2,0},{4,2},{6,4},{8,6},{10,8},{12,10},{14,12},{1,15},{3,1}... | collective-permute-start | bytes 393224 | tf_op jit(solution)/shard_map/ppermute | solution.py:351
  44.5 1.8 %collective-permute-done.9.refs_10_ = bf16[2,512,128]{2,1,0:T(8,128)(2,1)} collective-permute-done((bf16[2,512,128]{2,1,0:T(8,128)(2,1)}, bf16[2,512,128]{2,1,0:T(8,128)(2,1)}, u32[]{:S(2)}, u32[]{:S(2)}) %collective-permute-start.9) | collective-permute-done | bytes 262176 | tf_op jit(solution)/shard_map/ppermute | solution.py:354
  46.3 6.5 %all-to-all-done.asked_ref.grad_ref = bf16[16,400,128]{2,1,0:T(8,128)(2,1)S(1)} async-done(((bf16[16,400,128]{2,1,0:T(8,128)(2,1)}), bf16[16,400,128]{2,1,0:T(8,128)(2,1)S(1)}, u32[]{:S(2)}, u32[]{:S(2)}) %all-to-all-start) | async-done | bytes 1638432 | tf_op jit(solution)/shard_map/all_to_all | solution.py:397
  52.8 6.1 %shard_map.204 = (bf16[16,8,48,128]{3,2,1,0:T(8,128)(2,1)}, s32[128,128]{1,0:T(8,128)S(1)}) custom-call(s32[2]{0:T(128)S(1)} %pad_add_fusion.z_ref, bf16[16,400,128]{2,1,0:T(8,128)(2,1)S(1)} %all-to-all-done.asked_ref.grad_ref, bf16[512,128]{1,0:T(8,128)(2,1)S(1)} %get-tuple-element.32.refs_0_, bf16[512,128]{1,0:T(8,128)(2,1)S(1)} %get-tuple-element.31.refs_1_, ...), custom_call_target="tpu_custom_call" | custom-call | tf_op jit(solution)/shard_map/pallas_call | solution.py:400
  58.8 6.0 %all-to-all-start.1 = ((bf16[16,8,48,128]{3,2,1,0:T(8,128)(2,1)}), bf16[16,8,48,128]{3,2,1,0:T(8,128)(2,1)S(1)}, u32[]{:S(2)}, u32[]{:S(2)}) async-start(bf16[16,8,48,128]{3,2,1,0:T(8,128)(2,1)} %get-tuple-element.18.refs_0_.refs_1_), calls=%async_computation.1 | async-start | bytes 3145728 | tf_op jit(solution)/shard_map/all_to_all | solution.py:422
  68.3 3.7 %shard_map.205.refs_7_ = f32[8,512,128]{2,1,0:T(8,128)} custom-call(s32[2]{0:T(128)S(1)} %pad_add_fusion.1.at_ref, s32[8,1,768]{2,1,0:T(1,128)S(1)} %reshape.56.rows_ref, bf16[16,400,128]{2,1,0:T(8,128)(2,1)S(1)} %all-to-all-done.asked_ref.grad_ref, bf16[16,8,48,128]{3,2,1,0:T(8,128)(2,1)} %get-tuple-element.18.refs_0_.refs_1_), custom_call_target="tpu_custom_call" | custom-call | tf_op jit(solution)/shard_map/pallas_call | solution.py:432
  72.1 14.4 %all-to-all-done.1.refs_1_ = bf16[16,8,48,128]{3,2,1,0:T(8,128)(2,1)S(1)} async-done(((bf16[16,8,48,128]{3,2,1,0:T(8,128)(2,1)}), bf16[16,8,48,128]{3,2,1,0:T(8,128)(2,1)S(1)}, u32[]{:S(2)}, u32[]{:S(2)}) %all-to-all-start.1) | async-done | bytes 1572896 | tf_op jit(solution)/shard_map/all_to_all | solution.py:422
  86.4 7.7 %shard_map.206 = (bf16[256,640]{1,0:T(8,128)(2,1)S(1)}, bf16[256,4096]{1,0:T(8,128)(2,1)S(1)}) custom-call(s32[2,1,3072]{2,1,0:T(1,128)S(1)} %reshape.61.refs_0_, bf16[16,8,48,128]{3,2,1,0:T(8,128)(2,1)S(1)} %all-to-all-done.1.refs_1_, bf16[256,128]{1,0:T(8,128)(2,1)S(1)} %fusion.6.refs_2_, f32[8,1,512]{2,1,0:T(1,128)S(1)} %bitcast.68, ...), custom_call_target="tpu_custom_call" | custom-call | tf_op jit(solution)/shard_map/pallas_call | solution.py:450
  94.4 1.6 shard_map.209
  96.6 4.9 %collective-permute-done.11.refs_0_ = bf16[16,320,256]{2,1,0:T(8,128)(2,1)S(1)} collective-permute-done((bf16[16,320,256]{2,1,0:T(8,128)(2,1)S(1)}, bf16[16,320,256]{2,1,0:T(8,128)(2,1)S(1)}, u32[]{:S(2)}, u32[]{:S(2)}) %collective-permute-start.11) | collective-permute-done | bytes 2621472 | tf_op jit(solution)/shard_map/ppermute | solution.py:497
  101.5 1.6 shard_map.210.refs_1_
  103.2 1.5 copy-done.1
  104.7 6.5 %all-to-all-start.2 = ((bf16[16,320,256]{2,1,0:T(8,128)(2,1)}), bf16[16,320,256]{2,1,0:T(8,128)(2,1)}, u32[]{:S(2)}, u32[]{:S(2)}) async-start(bf16[16,320,256]{2,1,0:T(8,128)(2,1)} %copy-done.1), calls=%async_computation.2 | async-start | bytes 5242880 | tf_op jit(solution)/shard_map/all_to_all | solution.py:499
  111.2 3.6 %shard_map.208.refs_0_ = bf16[8,512,128]{2,1,0:T(8,128)(2,1)S(1)} custom-call(s32[2]{0:T(128)S(1)} %pad_add_fusion.2.at_ref, s32[8,1,768]{2,1,0:T(1,128)S(1)} %reshape.56.rows_ref, bf16[16,400,128]{2,1,0:T(8,128)(2,1)S(1)} %all-to-all-done.asked_ref.grad_ref, f32[8,512,128]{2,1,0:T(8,128)} %collective-permute-done.10.refs_0_, ...), custom_call_target="tpu_custom_call" | custom-call | tf_op jit(solution)/shard_map/pallas_call | solution.py:432
  116.2 1.4 collective-permute-start.12
  117.7 4.6 %collective-permute-start.16 = (bf16[512,128]{1,0:T(8,128)(2,1)}, bf16[512,128]{1,0:T(8,128)(2,1)}, u32[]{:S(2)}, u32[]{:S(2)}) collective-permute-start(bf16[512,128]{1,0:T(8,128)(2,1)} %get-tuple-element.27), channel_id=1, source_target_pairs={{0,10},{2,12},{4,14},{6,0},{8,2},{10,4},{12,6},{14,8},{1,11},{3,13... | collective-permute-start | bytes 393224 | tf_op jit(solution)/shard_map/ppermute | solution.py:501
  122.3 3.1 %collective-permute-start.15 = (bf16[512,128]{1,0:T(8,128)(2,1)}, bf16[512,128]{1,0:T(8,128)(2,1)}, u32[]{:S(2)}, u32[]{:S(2)}) collective-permute-start(bf16[512,128]{1,0:T(8,128)(2,1)} %get-tuple-element.28), channel_id=1, source_target_pairs={{0,8},{2,10},{4,12},{6,14},{8,0},{10,2},{12,4},{14,6},{1,9},{3,11}... | collective-permute-start | bytes 393224 | tf_op jit(solution)/shard_map/ppermute | solution.py:501
  125.4 2.2 %collective-permute-start.13 = (bf16[512,128]{1,0:T(8,128)(2,1)S(1)}, bf16[512,128]{1,0:T(8,128)(2,1)}, u32[]{:S(2)}, u32[]{:S(2)}) collective-permute-start(bf16[512,128]{1,0:T(8,128)(2,1)S(1)} %get-tuple-element.30), channel_id=1, source_target_pairs={{0,4},{2,6},{4,8},{6,10},{8,12},{10,14},{12,0},{14,2},{1,5},{3,7},... | collective-permute-start | bytes 393224 | tf_op jit(solution)/shard_map/ppermute | solution.py:501
  127.7 3.8 %fusion.back_ref = f32[256,512]{1,0:T(8,128)S(1)} fusion(bf16[256,4096]{1,0:T(8,128)(2,1)S(1)} %copy-done.4, bf16[640,4096]{1,0:T(8,128)(2,1)} %refs_6_.1), kind=kOutput, calls=%fused_computation | convolution fusion | flops 1073741824 | bytes 6815744 | tf_op jit(solution)/shard_map/dot_general | solution.py:60
  131.5 1.9 %shard_map.207.refs_1_ = bf16[2,1,1536,128]{3,2,1,0:T(8,128)(2,1)} custom-call(s32[2,1,1536]{2,1,0:T(1,128)S(1)} %get-tuple-element.13.bag_ref, f32[256,512]{1,0:T(8,128)S(1)} %fusion.back_ref), custom_call_target="tpu_custom_call" | custom-call | tf_op jit(solution)/shard_map/pallas_call | solution.py:475
  133.4 17.8 %all-to-all-done.2 = bf16[16,320,256]{2,1,0:T(8,128)(2,1)} async-done(((bf16[16,320,256]{2,1,0:T(8,128)(2,1)}), bf16[16,320,256]{2,1,0:T(8,128)(2,1)}, u32[]{:S(2)}, u32[]{:S(2)}) %all-to-all-start.2) | async-done | bytes 2621472 | tf_op jit(solution)/shard_map/all_to_all | solution.py:499
  151.2 2.1 %reduce_sum.21 = bf16[320,256]{1,0:T(8,128)(2,1)S(1)} reduce(bf16[16,320,256]{2,1,0:T(8,128)(2,1)} %all-to-all-done.2, bf16[]{:T(256)} %constant.32.clone.1), dimensions={0}, to_apply=%region_0.1 | reduce | flops 1228800 | bytes 2785282 | tf_op jit(solution)/shard_map/reduce_sum | solution.py:502
  155.7 3.4 %all-to-all-start.3 = ((bf16[8,32,320]{2,1,0:T(8,128)(2,1)}), bf16[8,32,320]{2,1,0:T(8,128)(2,1)S(1)}, u32[]{:S(2)}, u32[]{:S(2)}) async-start(bf16[8,32,320]{2,1,0:T(8,128)(2,1)} %shard_map.212.refs_1_), calls=%async_computation.3 | async-start | bytes 393216 | tf_op jit(solution)/shard_map/all_to_all | solution.py:517
  160.2 10.2 %all-to-all-done.3 = bf16[8,32,320]{2,1,0:T(8,128)(2,1)S(1)} async-done(((bf16[8,32,320]{2,1,0:T(8,128)(2,1)}), bf16[8,32,320]{2,1,0:T(8,128)(2,1)S(1)}, u32[]{:S(2)}, u32[]{:S(2)}) %all-to-all-start.3) | async-done | bytes 163872 | tf_op jit(solution)/shard_map/all_to_all | solution.py:517
  (81 shorter events, 15.8 us)
Async XLA Ops:
  0.6 66.2 %copy-start = (bf16[512,128]{1,0:T(8,128)(2,1)S(1)}, bf16[512,128]{1,0:T(8,128)(2,1)}, u32[]{:S(2)}) copy-start(bf16[512,128]{1,0:T(8,128)(2,1)} %param.31) | copy-start | bytes 393220
  1.8 22.1 %collective-permute-start = (bf16[512,128]{1,0:T(8,128)(2,1)S(1)}, bf16[512,128]{1,0:T(8,128)(2,1)S(1)}, u32[]{:S(2)}, u32[]{:S(2)}) collective-permute-start(bf16[512,128]{1,0:T(8,128)(2,1)S(1)} %get-tuple-element.32.refs_0_), channel_id=1, source_target_pairs={{0,2},{2,4},{4,6},{6,8},{8,10},{10,12},{12,14},{14,0},{1,3},{3,5},... | collective-permute-start | bytes 393224 | tf_op jit(solution)/shard_map/ppermute | solution.py:350
  3.8 20.1 %collective-permute-start.1 = (bf16[512,128]{1,0:T(8,128)(2,1)S(1)}, bf16[512,128]{1,0:T(8,128)(2,1)S(1)}, u32[]{:S(2)}, u32[]{:S(2)}) collective-permute-start(bf16[512,128]{1,0:T(8,128)(2,1)S(1)} %get-tuple-element.32.refs_0_), channel_id=1, source_target_pairs={{0,14},{2,0},{4,2},{6,4},{8,6},{10,8},{12,10},{14,12},{1,15},{3,1}... | collective-permute-start | bytes 393224 | tf_op jit(solution)/shard_map/ppermute | solution.py:351
  7.8 16.1 %collective-permute-start.2 = (bf16[512,128]{1,0:T(8,128)(2,1)S(1)}, bf16[512,128]{1,0:T(8,128)(2,1)S(1)}, u32[]{:S(2)}, u32[]{:S(2)}) collective-permute-start(bf16[512,128]{1,0:T(8,128)(2,1)S(1)} %get-tuple-element.32.refs_0_), channel_id=1, source_target_pairs={{0,8},{2,10},{4,12},{6,14},{8,0},{10,2},{12,4},{14,6},{1,9},{3,11}... | collective-permute-start | bytes 393224 | tf_op jit(solution)/shard_map/ppermute | solution.py:353
  23.9 28.9 %all-to-all-start = ((bf16[16,400,128]{2,1,0:T(8,128)(2,1)}), bf16[16,400,128]{2,1,0:T(8,128)(2,1)S(1)}, u32[]{:S(2)}, u32[]{:S(2)}) async-start(bf16[16,400,128]{2,1,0:T(8,128)(2,1)} %shard_map.203), calls=%async_computation | async-start | bytes 3276800 | tf_op jit(solution)/shard_map/all_to_all | solution.py:397
  31.3 6.2 %collective-permute-start.3 = (bf16[512,128]{1,0:T(8,128)(2,1)S(1)}, bf16[512,128]{1,0:T(8,128)(2,1)S(1)}, u32[]{:S(2)}, u32[]{:S(2)}) collective-permute-start(bf16[512,128]{1,0:T(8,128)(2,1)S(1)} %collective-permute-done.refs_1_.refs_2_), channel_id=1, source_target_pairs={{0,2},{2,4},{4,6},{6,8},{8,10},{10,12},{12,14},{14,0},{1,3},{3,5},... | collective-permute-start | bytes 393224 | tf_op jit(solution)/shard_map/ppermute | solution.py:350
  31.3 6.2 %collective-permute-start.4 = (bf16[512,128]{1,0:T(8,128)(2,1)S(1)}, bf16[512,128]{1,0:T(8,128)(2,1)S(1)}, u32[]{:S(2)}, u32[]{:S(2)}) collective-permute-start(bf16[512,128]{1,0:T(8,128)(2,1)S(1)} %collective-permute-done.1.refs_2_.refs_3_), channel_id=1, source_target_pairs={{0,14},{2,0},{4,2},{6,4},{8,6},{10,8},{12,10},{14,12},{1,15},{3,1}... | collective-permute-start | bytes 393224 | tf_op jit(solution)/shard_map/ppermute | solution.py:351
  37.5 6.2 %collective-permute-start.5 = (bf16[512,128]{1,0:T(8,128)(2,1)S(1)}, bf16[512,128]{1,0:T(8,128)(2,1)S(1)}, u32[]{:S(2)}, u32[]{:S(2)}) collective-permute-start(bf16[512,128]{1,0:T(8,128)(2,1)S(1)} %collective-permute-done.3.refs_4_), channel_id=1, source_target_pairs={{0,2},{2,4},{4,6},{6,8},{8,10},{10,12},{12,14},{14,0},{1,3},{3,5},... | collective-permute-start | bytes 393224 | tf_op jit(solution)/shard_map/ppermute | solution.py:350
  37.5 6.2 %collective-permute-start.6 = (bf16[512,128]{1,0:T(8,128)(2,1)S(1)}, bf16[512,128]{1,0:T(8,128)(2,1)S(1)}, u32[]{:S(2)}, u32[]{:S(2)}) collective-permute-start(bf16[512,128]{1,0:T(8,128)(2,1)S(1)} %collective-permute-done.4.refs_5_), channel_id=1, source_target_pairs={{0,14},{2,0},{4,2},{6,4},{8,6},{10,8},{12,10},{14,12},{1,15},{3,1}... | collective-permute-start | bytes 393224 | tf_op jit(solution)/shard_map/ppermute | solution.py:351
  41.5 3.0 %collective-permute-start.7 = (bf16[3,512,128]{2,1,0:T(8,128)(2,1)}, bf16[3,512,128]{2,1,0:T(8,128)(2,1)S(1)}, u32[]{:S(2)}, u32[]{:S(2)}) collective-permute-start(bf16[3,512,128]{2,1,0:T(8,128)(2,1)} %pad_maximum_fusion), channel_id=1, source_target_pairs={{0,1},{1,0},{2,3},{3,2},{4,5},{5,4},{6,7},{7,6},{8,9},{9,8},{10,11... | collective-permute-start | bytes 1179656 | tf_op jit(solution)/shard_map/ppermute | solution.py:354
  42.2 2.2 %collective-permute-start.8 = (bf16[2,512,128]{2,1,0:T(8,128)(2,1)}, bf16[2,512,128]{2,1,0:T(8,128)(2,1)}, u32[]{:S(2)}, u32[]{:S(2)}) collective-permute-start(bf16[2,512,128]{2,1,0:T(8,128)(2,1)} %pad_maximum_fusion.1), channel_id=1, source_target_pairs={{0,1},{1,0},{2,3},{3,2},{4,5},{5,4},{6,7},{7,6},{8,9},{9,8},{10,11... | collective-permute-start | bytes 786440 | tf_op jit(solution)/shard_map/ppermute | solution.py:354
  44.4 1.9 %collective-permute-start.9 = (bf16[2,512,128]{2,1,0:T(8,128)(2,1)}, bf16[2,512,128]{2,1,0:T(8,128)(2,1)}, u32[]{:S(2)}, u32[]{:S(2)}) collective-permute-start(bf16[2,512,128]{2,1,0:T(8,128)(2,1)} %pad_maximum_fusion.2), channel_id=1, source_target_pairs={{0,1},{1,0},{2,3},{3,2},{4,5},{5,4},{6,7},{7,6},{8,9},{9,8},{10,11... | collective-permute-start | bytes 786440 | tf_op jit(solution)/shard_map/ppermute | solution.py:354
  58.8 7.9 %copy-start.13 = (bf16[4096]{0:T(1024)(128)(2,1)S(1)}, bf16[4096]{0:T(1024)(128)(2,1)}, u32[]{:S(2)}) copy-start(bf16[4096]{0:T(1024)(128)(2,1)} %param.34) | copy-start | bytes 24580
  58.8 27.6 %all-to-all-start.1 = ((bf16[16,8,48,128]{3,2,1,0:T(8,128)(2,1)}), bf16[16,8,48,128]{3,2,1,0:T(8,128)(2,1)S(1)}, u32[]{:S(2)}, u32[]{:S(2)}) async-start(bf16[16,8,48,128]{3,2,1,0:T(8,128)(2,1)} %get-tuple-element.18.refs_0_.refs_1_), calls=%async_computation.1 | async-start | bytes 3145728 | tf_op jit(solution)/shard_map/all_to_all | solution.py:422
  68.3 18.1 %copy-start.7 = (f32[4096]{0:T(1024)S(1)}, f32[4096]{0:T(1024)}, u32[]{:S(2)}) copy-start(f32[4096]{0:T(1024)} %param.33) | copy-start | bytes 49156
  68.3 18.1 %copy-start.8 = (s32[2,128]{1,0:T(2,128)S(1)}, s32[2,128]{1,0:T(2,128)}, u32[]{:S(2)}) copy-start(s32[2,128]{1,0:T(2,128)} %refs_5_.3) | copy-start | bytes 3076
  96.0 5.5 %collective-permute-start.11 = (bf16[16,320,256]{2,1,0:T(8,128)(2,1)S(1)}, bf16[16,320,256]{2,1,0:T(8,128)(2,1)S(1)}, u32[]{:S(2)}, u32[]{:S(2)}) collective-permute-start(bf16[16,320,256]{2,1,0:T(8,128)(2,1)S(1)} %shard_map.209), channel_id=1, source_target_pairs={{0,1},{1,0},{2,3},{3,2},{4,5},{5,4},{6,7},{7,6},{8,9},{9,8},{10,11... | collective-permute-start | bytes 7864328 | tf_op jit(solution)/shard_map/ppermute | solution.py:497
  96.1 15.1 %collective-permute-start.10 = (f32[8,512,128]{2,1,0:T(8,128)}, f32[8,512,128]{2,1,0:T(8,128)}, u32[]{:S(2)}, u32[]{:S(2)}) collective-permute-start(f32[8,512,128]{2,1,0:T(8,128)} %shard_map.205.refs_7_), channel_id=1, source_target_pairs={{0,1},{1,0},{2,3},{3,2},{4,5},{5,4},{6,7},{7,6},{8,9},{9,8},{10,11... | collective-permute-start | bytes 6291464 | tf_op jit(solution)/shard_map/ppermute | solution.py:442
  104.7 46.6 %all-to-all-start.2 = ((bf16[16,320,256]{2,1,0:T(8,128)(2,1)}), bf16[16,320,256]{2,1,0:T(8,128)(2,1)}, u32[]{:S(2)}, u32[]{:S(2)}) async-start(bf16[16,320,256]{2,1,0:T(8,128)(2,1)} %copy-done.1), calls=%async_computation.2 | async-start | bytes 5242880 | tf_op jit(solution)/shard_map/all_to_all | solution.py:499
  114.8 12.9 %copy-start.4 = (bf16[256,4096]{1,0:T(8,128)(2,1)S(1)}, bf16[256,4096]{1,0:T(8,128)(2,1)}, u32[]{:S(2)}) copy-start(bf16[256,4096]{1,0:T(8,128)(2,1)} %copy-done.3) | copy-start | bytes 6291460
  115.6 9.8 %collective-permute-start.18 = (bf16[512,128]{1,0:T(8,128)(2,1)S(1)}, bf16[512,128]{1,0:T(8,128)(2,1)S(1)}, u32[]{:S(2)}, u32[]{:S(2)}) collective-permute-start(bf16[512,128]{1,0:T(8,128)(2,1)S(1)} %get-tuple-element.25), channel_id=1, source_target_pairs={{0,14},{2,0},{4,2},{6,4},{8,6},{10,8},{12,10},{14,12},{1,15},{3,1}... | collective-permute-start | bytes 393224 | tf_op jit(solution)/shard_map/ppermute | solution.py:501
  116.2 9.2 %collective-permute-start.12 = (bf16[512,128]{1,0:T(8,128)(2,1)S(1)}, bf16[512,128]{1,0:T(8,128)(2,1)S(1)}, u32[]{:S(2)}, u32[]{:S(2)}) collective-permute-start(bf16[512,128]{1,0:T(8,128)(2,1)S(1)} %get-tuple-element.24), channel_id=1, source_target_pairs={{0,2},{2,4},{4,6},{6,8},{8,10},{10,12},{12,14},{14,0},{1,3},{3,5},... | collective-permute-start | bytes 393224 | tf_op jit(solution)/shard_map/ppermute | solution.py:501
  117.7 36.5 %collective-permute-start.17 = (bf16[512,128]{1,0:T(8,128)(2,1)}, bf16[512,128]{1,0:T(8,128)(2,1)}, u32[]{:S(2)}, u32[]{:S(2)}) collective-permute-start(bf16[512,128]{1,0:T(8,128)(2,1)} %get-tuple-element.26), channel_id=1, source_target_pairs={{0,12},{2,14},{4,0},{6,2},{8,4},{10,6},{12,8},{14,10},{1,13},{3,15... | collective-permute-start | bytes 393224 | tf_op jit(solution)/shard_map/ppermute | solution.py:501
  117.7 36.5 %collective-permute-start.16 = (bf16[512,128]{1,0:T(8,128)(2,1)}, bf16[512,128]{1,0:T(8,128)(2,1)}, u32[]{:S(2)}, u32[]{:S(2)}) collective-permute-start(bf16[512,128]{1,0:T(8,128)(2,1)} %get-tuple-element.27), channel_id=1, source_target_pairs={{0,10},{2,12},{4,14},{6,0},{8,2},{10,4},{12,6},{14,8},{1,11},{3,13... | collective-permute-start | bytes 393224 | tf_op jit(solution)/shard_map/ppermute | solution.py:501
  122.3 31.9 %collective-permute-start.15 = (bf16[512,128]{1,0:T(8,128)(2,1)}, bf16[512,128]{1,0:T(8,128)(2,1)}, u32[]{:S(2)}, u32[]{:S(2)}) collective-permute-start(bf16[512,128]{1,0:T(8,128)(2,1)} %get-tuple-element.28), channel_id=1, source_target_pairs={{0,8},{2,10},{4,12},{6,14},{8,0},{10,2},{12,4},{14,6},{1,9},{3,11}... | collective-permute-start | bytes 393224 | tf_op jit(solution)/shard_map/ppermute | solution.py:501
  125.4 25.8 %copy-start.11 = (bf16[512,128]{1,0:T(8,128)(2,1)}, bf16[512,128]{1,0:T(8,128)(2,1)S(1)}, u32[]{:S(2)}) copy-start(bf16[512,128]{1,0:T(8,128)(2,1)S(1)} %collective-permute-done.18) | copy-start | bytes 393220
  125.4 28.8 %collective-permute-start.14 = (bf16[512,128]{1,0:T(8,128)(2,1)}, bf16[512,128]{1,0:T(8,128)(2,1)}, u32[]{:S(2)}, u32[]{:S(2)}) collective-permute-start(bf16[512,128]{1,0:T(8,128)(2,1)} %get-tuple-element.29), channel_id=1, source_target_pairs={{0,6},{2,8},{4,10},{6,12},{8,14},{10,0},{12,2},{14,4},{1,7},{3,9},... | collective-permute-start | bytes 393224 | tf_op jit(solution)/shard_map/ppermute | solution.py:501
  125.4 28.8 %collective-permute-start.13 = (bf16[512,128]{1,0:T(8,128)(2,1)S(1)}, bf16[512,128]{1,0:T(8,128)(2,1)}, u32[]{:S(2)}, u32[]{:S(2)}) collective-permute-start(bf16[512,128]{1,0:T(8,128)(2,1)S(1)} %get-tuple-element.30), channel_id=1, source_target_pairs={{0,4},{2,6},{4,8},{6,10},{8,12},{10,14},{12,0},{14,2},{1,5},{3,7},... | collective-permute-start | bytes 393224 | tf_op jit(solution)/shard_map/ppermute | solution.py:501
  133.4 20.8 %copy-start.5 = (bf16[2,1,1536,128]{3,2,1,0:T(8,128)(2,1)S(1)}, bf16[2,1,1536,128]{3,2,1,0:T(8,128)(2,1)}, u32[]{:S(2)}) copy-start(bf16[2,1,1536,128]{3,2,1,0:T(8,128)(2,1)} %shard_map.207.refs_1_) | copy-start | bytes 2359300
  154.2 16.3 %copy-start.12 = (f32[320,32]{0,1:T(8,128)S(1)}, f32[320,32]{0,1:T(8,128)}, u32[]{:S(2)}) copy-start(f32[320,32]{0,1:T(8,128)} %param.35) | copy-start | bytes 122884
  155.6 3.5 %collective-permute-start.19 = (f32[512,128]{1,0:T(8,128)S(1)}, f32[512,128]{1,0:T(8,128)S(1)}, u32[]{:S(2)}, u32[]{:S(2)}) collective-permute-start(f32[512,128]{1,0:T(8,128)S(1)} %fusion.12), channel_id=1, source_target_pairs={{0,1},{1,0},{2,3},{3,2},{4,5},{5,4},{6,7},{7,6},{8,9},{9,8},{10,11... | collective-permute-start | bytes 786440 | tf_op jit(solution)/shard_map/ppermute | solution.py:508
  155.7 14.7 %all-to-all-start.3 = ((bf16[8,32,320]{2,1,0:T(8,128)(2,1)}), bf16[8,32,320]{2,1,0:T(8,128)(2,1)S(1)}, u32[]{:S(2)}, u32[]{:S(2)}) async-start(bf16[8,32,320]{2,1,0:T(8,128)(2,1)} %shard_map.212.refs_1_), calls=%async_computation.3 | async-start | bytes 393216 | tf_op jit(solution)/shard_map/all_to_all | solution.py:517
  (6 other events, 25.1 us)
